TPU v7x, 256 devices: a whole 4x4x8 slice. The times are simulated.
256 devices in a mesh: row: 64 (over z, x, y_hi), col: 4 (over y_lo, core).
Axes of the slice: x: 4, y: 4 (y_hi: 2, y_lo: 2; y = y_hi * 2 + y_lo), z: 8, core: 2. Of those that a mesh axis runs over, the one named last changes fastest.
Arguments:
- panel: bfloat16 [524288, 256], P(('row', 'col')), may hold values from 0 to 2
- source: bfloat16 [524288, 256], P(('row', 'col')), may hold values from 0 to 2
- reflect: float32 [524288], P(('row', 'col')), may hold values from 0.1 to 0.9
- blocks: bfloat16 [4096, 512, 512], P(('row', 'col')), may hold values from 0 to 0.001953125
- blk_rows: int32 [256, 16], P(('row', 'col')), may hold values from 0 to 1023, as said below
- blk_cols: int32 [256, 16], P(('row', 'col')), may hold values from 0 to 1023, as said below
- live_count: int32 [256], P(('row', 'col')), may hold values from 1 to 16, as said below
Outputs:
- radiosity: float32 [524288, 256], P(('row', 'col'))
Inputs may be any that keep to these rules, and one draw needn't show every extreme that they name: `blk_rows`: every block row of device d lies in row group d // 4, the block rows d // 4 * 4 * 4 to that plus 4 * 4 - 1; pairs may repeat and then add. `blk_cols`: each block column is at least its slot's block row and lies in the same row group or the next one. `live_count`: some device has all 16 slots live in every draw.
All inputs are finite; a program needn't handle non-finite values.
Results may differ from a plain program's by a relative error of at most 0.0003.
Values may be sent and summed in bfloat16 or wider, within the bound.
No kernel may reach another device: no remote copies, remote signals or barrier semaphores. Data moves between devices by JAX's collectives and lax.ppermute only.
A program may use at most 128 MiB of HBM per device.

v0:
```python
import jax
import jax.numpy as jnp
from jax import lax
from jax.sharding import PartitionSpec as P


def passed_along(block, axis, distance):
    devices = range(lax.axis_size(axis))
    route = [(i - distance, i) for i in devices if i - distance in devices]
    return lax.ppermute(block, axis, route)


def per_device(panel, source, reflect, blocks, blk_rows, blk_cols, live_count):
    piece_rows = panel.shape[0]
    block_size = blocks.shape[1]
    group_rows = piece_rows * lax.axis_size("col")
    group_blocks = group_rows // block_size
    group = lax.all_gather(panel, "col", axis=0, tiled=True)
    upper = passed_along(group, "row", -1)
    window = jnp.concatenate([group, upper], 0)
    base_block = lax.axis_index("row") * group_blocks
    partial_value = jnp.zeros((2 * group_rows, panel.shape[1]), jnp.float32)

    def add_slot(slot, partial_value):
        row_start = (blk_rows[0, slot] - base_block) * block_size
        col_start = (blk_cols[0, slot] - base_block) * block_size
        block = blocks[slot]
        from_col = lax.dynamic_slice_in_dim(window, col_start, block_size, 0)
        from_row = lax.dynamic_slice_in_dim(window, row_start, block_size, 0)
        direct = jnp.dot(block, from_col, preferred_element_type=jnp.float32)
        mirror = lax.dot_general(
            block, from_row, (((0,), (0,)), ((), ())), preferred_element_type=jnp.float32
        )
        current = lax.dynamic_slice_in_dim(partial_value, row_start, block_size, 0)
        partial_value = lax.dynamic_update_slice_in_dim(
            partial_value, current + direct, row_start, 0
        )
        current = lax.dynamic_slice_in_dim(partial_value, col_start, block_size, 0)
        return lax.dynamic_update_slice_in_dim(partial_value, current + mirror, col_start, 0)

    partial_value = lax.fori_loop(0, live_count[0], add_slot, partial_value)
    own_part = partial_value[:group_rows]
    next_part = partial_value[group_rows:]
    arrived = passed_along(next_part, "row", 1)
    mine = lax.psum_scatter(own_part + arrived, "col", scatter_dimension=0, tiled=True)
    return source.astype(jnp.float32) + reflect[:, None] * mine


def solution(mesh):
    return jax.shard_map(
        per_device,
        mesh=mesh,
        in_specs=(
            P(("row", "col"), None),
            P(("row", "col"), None),
            P(("row", "col")),
            P(("row", "col"), None, None),
            P(("row", "col"), None),
            P(("row", "col"), None),
            P(("row", "col")),
        ),
        out_specs=P(("row", "col"), None),
        check_vma=False,
    )
```

profile of v0, /device:TPU:1, one launch (start us, length us, event | category | flops | bytes accessed | tf_op | source)
XLA Modules:
  0.0 574.4 jit_solution(18129163589326122926)
XLA Ops:
  6.5 0.0 all-gather.2.cloned.1.call-start
  6.5 0.7 all-gather.2.cloned.1.call-update
  7.3 0.0 reduce-scatter.2.cloned.1.call-start
  7.3 55.2 %all-gather.2.cloned.1.call-done = bf16[8192,256]{1,0:T(8,128)(2,1)} async-done(((bf16[2048,256]{1,0:T(8,128)(2,1)}), bf16[8192,256]{1,0:T(8,128)(2,1)}) %all-gather.2.cloned.1.call-update) | async-done | bytes 4194320 | tf_op jit(solution)/shard_map/all_gather | solution.py:18
  62.5 1.3 collective-permute-start
  63.8 94.8 %collective-permute-done = bf16[8192,256]{1,0:T(8,128)(2,1)} collective-permute-done((bf16[8192,256]{1,0:T(8,128)(2,1)}, bf16[8192,256]{1,0:T(8,128)(2,1)}, u32[]{:S(2)}, u32[]{:S(2)}) %collective-permute-start) | collective-permute-done | bytes 4194336 | tf_op jit(solution)/shard_map/ppermute | solution.py:10
  158.6 9.7 %pad_maximum_fusion = bf16[16384,256]{1,0:T(8,128)(2,1)} fusion(bf16[8192,256]{1,0:T(8,128)(2,1)} %collective-permute-done, bf16[8192,256]{1,0:T(8,128)(2,1)} %all-gather.2.cloned.1.call-done), kind=kLoop, calls=%fused_computation.14 | loop fusion | flops 16777216 | bytes 16777216 | tf_op jit(solution)/shard_map/concatenate | solution.py:20
  168.3 6.0 %broadcast_in_dim.4 = f32[16384,256]{1,0:T(8,128)} broadcast(f32[]{:T(128)} %constant.8.clone.1), dimensions={} | broadcast | bytes 16777220 | tf_op jit(solution)/shard_map/broadcast_in_dim | solution.py:22
  174.4 0.0 copy-done.1
  174.4 0.0 copy-done.2
  174.4 29.6 %while.10 = (s32[]{:T(128)}, f32[16384,256]{1,0:T(8,128)}, s32[]{:T(128)}, s32[1,16]{1,0:T(1,128)S(1)}, s32[]{:T(128)}, /*index=5*/bf16[16,512,512]{2,1,0:T(8,12...) while((s32[]{:T(128)}, f32[16384,256]{1,0:T(8,128)}, ...), condition=%wide.region_1.0_spmd, body=%wide.region_0.0_spmd.sunk | while | flops 268697600 | bytes 3670343 | solution.py:41
  175.0 0.6 constant_dynamic-slice_fusion.3
  176.8 2.4 fusion.20
  179.2 2.4 fusion.21
  182.3 0.6 constant_dynamic-slice_fusion.3
  184.0 2.4 fusion.20
  186.4 2.4 fusion.21
  189.5 0.6 constant_dynamic-slice_fusion.3
  191.2 2.4 fusion.20
  193.7 2.4 fusion.21
  196.8 0.6 constant_dynamic-slice_fusion.3
  198.5 2.4 fusion.20
  200.9 2.4 fusion.21
  204.0 3.9 slice.7
  207.9 30.1 %collective-permute-start.1 = (f32[8192,256]{1,0:T(8,128)S(1)}, f32[8192,256]{1,0:T(8,128)}, u32[]{:S(2)}, u32[]{:S(2)}) collective-permute-start(f32[8192,256]{1,0:T(8,128)S(1)} %slice.7), channel_id=1, source_target_pairs={{0,4},{4,8},{8,12},{12,16},{16,20},{20,24},{24,28},{28,32},{32,36}... | collective-permute-start | bytes 25165832 | tf_op jit(solution)/shard_map/ppermute | solution.py:10
  238.0 147.0 %collective-permute-done.1 = f32[8192,256]{1,0:T(8,128)} collective-permute-done((f32[8192,256]{1,0:T(8,128)S(1)}, f32[8192,256]{1,0:T(8,128)}, u32[]{:S(2)}, u32[]{:S(2)}) %collective-permute-start.1) | collective-permute-done | bytes 8388640 | tf_op jit(solution)/shard_map/ppermute | solution.py:10
  385.1 10.1 %slice_add_fusion = f32[8192,256]{1,0:T(8,128)} fusion(f32[8192,256]{1,0:T(8,128)} %collective-permute-done.1, f32[16384,256]{1,0:T(8,128)} %get-tuple-element.48), kind=kLoop, calls=%fused_computation.15 | loop fusion | flops 2097152 | bytes 25165824 | tf_op jit(solution)/shard_map/add | solution.py:45
  395.1 0.0 reduce-scatter.2.cloned.1.call-update
  395.1 169.1 %reduce-scatter.2.cloned.1.call-done = f32[2048,256]{1,0:T(8,128)} async-done(((f32[8192,256]{1,0:T(8,128)}), f32[2048,256]{1,0:T(8,128)}) %reduce-scatter.2.cloned.1.call-update) | async-done | bytes 2097168 | tf_op jit(solution)/shard_map/reduce_scatter | solution.py:45
  564.3 0.0 copy-done
  564.3 0.0 copy-done.3
  564.3 3.2 multiply_add_fusion
  (4 shorter events, 0.0 us)
Async XLA Ops:
  6.5 56.0 %all-gather.2.cloned.1.call-start = ((), (), s32[]{:S(2)}) async-start(), calls=%async_computation.1 | async-start | bytes 5242880 | tf_op jit(solution)/shard_map/all_gather | solution.py:18
  7.3 557.0 %reduce-scatter.2.cloned.1.call-start = ((), (), s32[]{:S(2)}) async-start(), calls=%async_computation.2 | async-start | bytes 10485760 | tf_op jit(solution)/shard_map/reduce_scatter | solution.py:45
  62.5 96.1 %collective-permute-start = (bf16[8192,256]{1,0:T(8,128)(2,1)}, bf16[8192,256]{1,0:T(8,128)(2,1)}, u32[]{:S(2)}, u32[]{:S(2)}) collective-permute-start(bf16[8192,256]{1,0:T(8,128)(2,1)} %all-gather.2.cloned.1.call-done), channel_id=1, source_target_pairs={{4,0},{8,4},{12,8},{16,12},{20,16},{24,20},{28,24},{32,28},{36,32}... | collective-permute-start | bytes 12582920 | tf_op jit(solution)/shard_map/ppermute | solution.py:10
  168.3 6.0 %copy-start.1 = (s32[1,16]{1,0:T(1,128)S(1)}, s32[1,16]{1,0:T(1,128)}, u32[]{:S(2)}) copy-start(s32[1,16]{1,0:T(1,128)} %param.13) | copy-start | bytes 196
  168.3 6.0 %copy-start.2 = (s32[1,16]{1,0:T(1,128)S(1)}, s32[1,16]{1,0:T(1,128)}, u32[]{:S(2)}) copy-start(s32[1,16]{1,0:T(1,128)} %param.14) | copy-start | bytes 196
  207.9 177.1 %collective-permute-start.1 = (f32[8192,256]{1,0:T(8,128)S(1)}, f32[8192,256]{1,0:T(8,128)}, u32[]{:S(2)}, u32[]{:S(2)}) collective-permute-start(f32[8192,256]{1,0:T(8,128)S(1)} %slice.7), channel_id=1, source_target_pairs={{0,4},{4,8},{8,12},{12,16},{16,20},{20,24},{24,28},{28,32},{32,36}... | collective-permute-start | bytes 25165832 | tf_op jit(solution)/shard_map/ppermute | solution.py:10
  395.1 169.2 %copy-start = (bf16[2048,256]{1,0:T(8,128)(2,1)S(1)}, bf16[2048,256]{1,0:T(8,128)(2,1)}, u32[]{:S(2)}) copy-start(bf16[2048,256]{1,0:T(8,128)(2,1)} %param.10) | copy-start | bytes 3145732
  395.1 169.2 %copy-start.3 = (f32[2048]{0:T(1024)S(1)}, f32[2048]{0:T(1024)}, u32[]{:S(2)}) copy-start(f32[2048]{0:T(1024)} %param.11) | copy-start | bytes 24580
Sparse Core Ops, SparseCore 0:
  9.2 53.3 all-gather.1
  395.3 168.9 reduce-scatter.1
where the time goes:
time: 576 us; the launch traced here: 574 us
  waiting for transfers between devices  467 us (81%)
  starting transfers between devices  31.4 us (5%)
  other arithmetic  23 us (4%)
  matrix products  19.4 us (3%)
  between operations  13.4 us (2%)
  local copies, waits for them, and re-layouts  12.3 us (2%)
  loops' own time  7.9 us (1%)
    ppermute x2, waiting for transfers between devices, passed_along(): return lax.ppermute(block, axis, route)  242 us
    reduce_scatter x1, waiting for transfers between devices, per_device(): lax.psum_scatter(own_part + arrived, 'col', scatter_dimension=0, tiled=True)  169 us
    all_gather x1, waiting for transfers between devices, per_device(): group = lax.all_gather(panel, 'col', axis=0, tiled=True)  55.2 us
    ppermute x2, starting transfers between devices, passed_along(): return lax.ppermute(block, axis, route)  31.4 us
  transfers between devices with their start and end apart: 4, of which 4 were waited for; matrix products, arithmetic and copies ran while one was open for 0% of the time, Pallas kernels for 0%

commit v1 on v0

v1 whole, which is shorter than its diff:
```python
import jax
import jax.numpy as jnp
from jax import lax
from jax.experimental import pallas as pl
from jax.experimental.pallas import tpu as pltpu
from jax.sharding import PartitionSpec as P


AXES = ("row", "col")
SCALE_ROWS = 16
STEPS = 32766.0
LOG_STEPS = 256.0
LN2 = 0.6931471805599453
PARAMS = pltpu.CompilerParams(vmem_limit_bytes=12 * 1024 * 1024)


def send(x, route):
    groups, cols = lax.axis_size("row"), lax.axis_size("col")
    pairs = []
    for r in range(groups):
        for c in range(cols):
            to_r, to_h, to_k = route(r, c // 2, c % 2)
            pairs.append((r * cols + c, to_r % groups * cols + to_h * 2 + to_k))
    return lax.ppermute(x, AXES, pairs)


def quantized(x):
    top = jnp.max(jnp.abs(x), axis=0, keepdims=True)
    log = jnp.ceil(jnp.log(jnp.maximum(top, 1e-30)) * (LOG_STEPS / LN2))
    inverse = STEPS * jnp.exp(log * (-LN2 / LOG_STEPS))
    steps = jnp.round(x * inverse).astype(jnp.int32).astype(jnp.int16)
    return steps, log.astype(jnp.int32)


def store_quantized(ref, at, x):
    steps, log = quantized(x)
    blk, half = x.shape
    ref[at, :blk, :] = steps
    ref[at, blk:, :] = jnp.broadcast_to(log, (SCALE_ROWS, half)).astype(jnp.int16)


def load_quantized(ref, at, blk):
    log = ref[at, blk:, :].astype(jnp.int32).astype(jnp.float32)[:1]
    scale = jnp.exp(log * (LN2 / LOG_STEPS)) * (1.0 / STEPS)
    return ref[at, :blk, :].astype(jnp.int32).astype(jnp.float32) * scale


def split_columns(panel, k):
    half = panel.shape[1] // 2
    left, right = panel[:, :half], panel[:, half:]
    first = k == 0
    return jnp.where(first, left, right), jnp.where(first, right, left)


def goes_on(earlier, sums):
    pass


def products(mirror, direct, index, sib_index, blocks, sib_blocks, pieces, sums, plan, ring, x, sems):
    n_slots, blk = blocks.shape[0], blocks.shape[1]
    group = sums.shape[0]
    pb, depth = group // 4, ring.shape[0]
    turn = index[2 * n_slots + 1] * pb
    none = len(pieces)

    def planned(n, pick):
        def scan(is_sib, table):
            def step(slot, n):
                hit, piece, b, at = pick(table[slot] ^ turn, table[n_slots + slot] ^ turn)
                plan[n] = (((at * pb + b) * 8 + piece) * 2 + is_sib) * n_slots + slot
                return n + jnp.where(hit, 1, 0)

            return step

        end = lax.fori_loop(0, index[2 * n_slots], scan(0, index), n)
        end = lax.fori_loop(0, sib_index[2 * n_slots], scan(1, sib_index), end)

        @pl.when((end - n) % 2 == 1)
        def _():
            last = plan[end - 1]
            plan[end] = last + (none - last // (2 * n_slots) % 8) * (2 * n_slots)

        return end + (end - n) % 2

    def pick_mirror(row, col):
        hit, first = mirror(row // (2 * pb), col // group)
        return hit, first + row // pb % 2, row % pb, col % group

    def pick_direct(row, col):
        hit, first = direct(col // (2 * pb))
        return hit, first + col // pb % 2, col % pb, row

    zero = jnp.int32(0)
    n_mirror = planned(zero, pick_mirror) if mirror else zero
    n = planned(n_mirror, pick_direct) if direct else n_mirror

    def copy(source, slot, i):
        at = i % depth
        return pltpu.make_async_copy(source.at[slot], ring.at[at], sems.at[at])

    def start(i):
        @pl.when(i < n)
        def _():
            entry = plan[i]
            slot, is_sib = entry % n_slots, entry // n_slots % 2

            @pl.when(is_sib == 0)
            def _():
                copy(blocks, slot, i).start()

            @pl.when(is_sib == 1)
            def _():
                copy(sib_blocks, slot, i).start()

    for i in range(depth):
        start(i)

    def staged(i, u):
        entry = plan[i] // (2 * n_slots)
        piece, b, at = entry % 8, entry // 8 % pb, entry // (8 * pb)
        for p, ref in enumerate(pieces):

            @pl.when(piece == p)
            def _():
                x[u] = ref[pl.ds(pl.multiple_of(b * blk, blk), blk), :]

        @pl.when(piece == none)
        def _():
            x[u] = jnp.zeros(x.shape[1:], x.dtype)

        return at

    def steps(first, end, product):
        def step(pair, carry):
            i = first + 2 * pair
            places = [staged(i + u, u) for u in range(2)]
            for u in range(2):
                copy(blocks, 0, i + u).wait()
            results = [product(ring[(i + u) % depth], x[u]) for u in range(2)]
            for at, result in zip(places, results):
                sums[at] += result
            for u in range(2):
                start(i + u + depth)
            return carry

        lax.fori_loop(0, (end - first) // 2, step, 0)

    if mirror:
        steps(
            zero,
            n_mirror,
            lambda block, x: lax.dot_general(
                block, x, (((0,), (0,)), ((), ())), preferred_element_type=jnp.float32
            ),
        )
    if direct:
        steps(
            n_mirror, n, lambda block, x: jnp.dot(block, x, preferred_element_type=jnp.float32)
        )


def for_blocks(pb, body):
    def step(b, carry):
        body(b)
        return carry

    lax.fori_loop(0, pb, step, 0)


def to_next(pair):
    return lambda rows, ahead: ((rows == pair) & (ahead == 1), 0)


def to_own(pair):
    return lambda rows, ahead: ((rows == pair) & (ahead == 0), 0)


def from_pair(pair):
    return lambda cols: (cols == pair, 0)


def chip_up_kernel(*refs):
    tables, pieces, sums, scratch = refs[:4], refs[4:6], refs[6], refs[7:]
    sums[...] = jnp.zeros_like(sums)
    products(to_next(0), None, *tables, pieces, sums, *scratch)


def chip_here_kernel(*refs):
    tables, pieces, sums, scratch = refs[:4], refs[4:6], refs[6], refs[7:]
    sums[...] = jnp.zeros_like(sums)
    products(to_own(0), from_pair(0), *tables, pieces, sums, *scratch)


def up_kernel(*refs):
    tables, pieces, earlier = refs[:4], refs[4:6], refs[6]
    far0, far1, near1, sums = refs[7:11]
    goes_on(earlier, sums)
    products(to_next(1), None, *tables, pieces, sums, *refs[11:])
    pb = far0.shape[0]

    def finish(b):
        store_quantized(far1, b, sums[pb + b])
        store_quantized(far0, b, sums[b])
        store_quantized(near1, b, sums[3 * pb + b])

    for_blocks(pb, finish)


def group_kernel(*refs):
    tables, pieces, earlier, sums = refs[:4], refs[4:8], refs[8], refs[9]
    goes_on(earlier, sums)
    direct = lambda cols: ((cols == 1) | (cols == 3), jnp.where(cols == 3, 2, 0))
    products(to_own(1), direct, *tables, pieces, sums, *refs[10:])


def far_kernel(*refs):
    tables, pieces, earlier = refs[:4], refs[4:6], refs[6]
    own1, other0, sums = refs[7:10]
    goes_on(earlier, sums)
    products(None, from_pair(2), *tables, pieces, sums, *refs[10:])
    pb = own1.shape[0]

    def finish(b):
        store_quantized(other0, b, sums[2 * pb + b])
        own1[b] = sums[pb + b]

    for_blocks(pb, finish)


def add_kernel(first, sums, arrived, out):
    blk = sums.shape[1]

    def step(b):
        store_quantized(out, b, sums[first + b] + load_quantized(arrived, b, blk))

    for_blocks(out.shape[0], step)


def final_kernel(index, sums, sib, pair0, pair1, below0, below1, source, reflect, out):
    blk, half = sums.shape[1:]
    b = pl.program_id(0)
    mine = sums[b] + load_quantized(pair0, b, blk) + load_quantized(below0, b, blk)
    other = sib[b] + load_quantized(pair1, b, blk) + load_quantized(below1, b, blk)
    first = index[index.shape[0] - 1] % 2 == 0
    rows = pl.ds(pl.multiple_of(b * blk, blk), blk)
    factor = reflect[rows, :]
    left = jnp.where(first, mine, other)
    right = jnp.where(first, other, mine)
    out[:, :half] = source[rows, :half].astype(jnp.float32) + factor * left
    out[:, half:] = source[rows, half:].astype(jnp.float32) + factor * right


def in_vmem(x):
    return pltpu.with_memory_space_constraint(x, pltpu.VMEM)


def in_hbm(x):
    return pltpu.with_memory_space_constraint(x, pltpu.HBM)


def vmem_shape(shape, dtype):
    return pltpu.VMEM(shape, dtype)


def call(kernel, name, inputs, outputs, aliases=None, scratch=()):
    def spec(shape, dtype):
        if dtype == jnp.int32:
            return pl.BlockSpec(memory_space=pltpu.SMEM)
        if shape[-1] > 128 and len(shape) == 3:
            return pl.BlockSpec(memory_space=pltpu.HBM)
        return pl.BlockSpec(memory_space=pltpu.VMEM)

    specs = [spec(x.shape, x.dtype) for x in inputs]
    put = {pltpu.VMEM: in_vmem, pltpu.HBM: in_hbm, pltpu.SMEM: lambda x: x}
    return pl.pallas_call(
        kernel,
        in_specs=specs,
        out_specs=[pl.BlockSpec(memory_space=pltpu.VMEM)] * len(outputs),
        out_shape=[vmem_shape(*output) for output in outputs],
        scratch_shapes=scratch,
        input_output_aliases=aliases or {},
        compiler_params=PARAMS,
        cost_estimate=pl.CostEstimate(flops=1000, bytes_accessed=1000, transcendentals=0),
        name=name,
    )(*[put[s.memory_space](x) for x, s in zip(inputs, specs)])


def per_device(panel, source, reflect, blocks, blk_rows, blk_cols, live_count):
    f32 = jnp.float32
    piece_rows, width = panel.shape
    n_slots, blk, _ = blocks.shape
    half = width // 2
    pb = piece_rows // blk
    r, c = lax.axis_index("row"), lax.axis_index("col")
    k = c % 2

    base = r * (pb * lax.axis_size("col"))
    place = c.astype(jnp.int32)[None]
    index = jnp.concatenate([blk_rows[0] - base, blk_cols[0] - base, live_count, place])

    to_sibling = lambda r, h, k: (r, h, 1 - k)
    across = lambda r, h, k: (r, 1 - h, k)
    down = lambda r, h, k: (r - 1, 1 - h, k)
    pair = send(panel, across)
    near = send(panel, down)
    sib_blocks = send(blocks, to_sibling)
    mine, other = split_columns(panel, k)
    sib = send(other, to_sibling)
    sib_index = send(index, to_sibling)
    sums = ((pb, blk, half), f32)
    sent = ((pb, blk + SCALE_ROWS, half), jnp.int16)
    group = ((4 * pb, blk, half), f32)
    tables = [index, sib_index, blocks, sib_blocks]
    scratch = [
        pltpu.SMEM((4 * n_slots + 4,), jnp.int32),
        pltpu.VMEM((6, blk, blk), blocks.dtype),
        pltpu.VMEM((2, blk, half), panel.dtype),
        pltpu.SemaphoreType.DMA((6,)),
    ]

    (up,) = call(chip_up_kernel, "chip_up", tables + [mine, sib], [group], scratch=scratch)
    pair, near, up = lax.optimization_barrier((pair, near, up))
    pair0, other = split_columns(pair, k)
    pair1 = send(other, to_sibling)
    near0, other = split_columns(near, k)
    near1 = send(other, to_sibling)
    far0 = send(near0, across)
    far1 = send(pair1, down)

    (here,) = call(chip_here_kernel, "chip_here", tables + [mine, sib], [group], scratch=scratch)
    up, here, near1 = lax.optimization_barrier((up, here, near1))
    far_q0, far_q1, near_q1, up = call(
        up_kernel, "up", tables + [pair0, pair1, up], [sent, sent, sent, group], {6: 3}, scratch
    )
    part1 = send(far_q1, lambda r, h, k: (r + 1, 1 - h, k))
    part0 = send(far_q0, across)
    below1 = send(near_q1, lambda r, h, k: (r + 1, 1 - h, 1 - k))

    (here,) = call(
        group_kernel, "group", tables + [pair0, pair1, near0, near1, here], [group], {8: 0}, scratch
    )
    far0, far1, here = lax.optimization_barrier((far0, far1, here))
    own_f1, other_q0, here = call(
        far_kernel, "far", tables + [far0, far1, here], [sums, sent, group], {6: 2}, scratch
    )
    here0 = send(other_q0, lambda r, h, k: (r, 1 - h, k))
    here_sib = send(own_f1, lambda r, h, k: (r, h, 1 - k))
    (below0,) = call(lambda *refs: add_kernel(2 * pb, *refs), "add_up", [up, part0], [sent])
    below0 = send(below0, lambda r, h, k: (r + 1, 1 - h, k))
    part1, below1 = lax.optimization_barrier((part1, below1))
    (here1,) = call(lambda *refs: add_kernel(3 * pb, *refs), "add_here", [here, part1], [sent])
    here1 = send(here1, lambda r, h, k: (r, 1 - h, 1 - k))

    factor = jnp.broadcast_to(reflect[:, None], (piece_rows, half))
    args = [here, here_sib, here0, here1, below0, below1, source, factor]
    return pl.pallas_call(
        final_kernel,
        grid=(pb,),
        in_specs=[pl.BlockSpec(memory_space=pltpu.SMEM)]
        + [pl.BlockSpec(memory_space=pltpu.VMEM)] * len(args),
        out_specs=pl.BlockSpec((blk, width), lambda i: (i, 0)),
        out_shape=jax.ShapeDtypeStruct((piece_rows, width), f32),
        compiler_params=PARAMS,
        name="final",
    )(index, *map(in_vmem, args))


def solution(mesh):
    return jax.shard_map(
        per_device,
        mesh=mesh,
        in_specs=(
            P(("row", "col"), None),
            P(("row", "col"), None),
            P(("row", "col")),
            P(("row", "col"), None, None),
            P(("row", "col"), None),
            P(("row", "col"), None),
            P(("row", "col")),
        ),
        out_specs=P(("row", "col"), None),
        check_vma=False,
    )
```

time: 576 us -> 106 us (0.18)
  the two profiles are of different devices: /device:TPU:1 before, /device:TPU:231 now
where the time goes in v1:
time: 106 us; the launch traced here: 105 us
  waiting for transfers between devices  59.3 us (56%)
  starting transfers between devices  23.6 us (22%)
  Pallas kernels  17.5 us (17%)
  other arithmetic  2.96 us (3%)
    ppermute x16, waiting for transfers between devices, send(): return lax.ppermute(x, AXES, pairs)  59.3 us
    ppermute x16, starting transfers between devices, send(): return lax.ppermute(x, AXES, pairs)  23.6 us
    pallas_call x7, Pallas kernels, call(): pl.pallas_call(kernel, in_specs=specs, out_specs=[pl.BlockSpec(memory_spa...  14.6 us
    pallas_call x1, Pallas kernels, per_device(): pl.pallas_call(final_kernel, grid=(pb,), in_specs=[pl.BlockSpec(memory_sp...  2.91 us
    select_n x3, other arithmetic, split_columns(): return (jnp.where(first, left, right), jnp.where(first, right, left))  2.21 us
  transfers between devices with their start and end apart: 16, of which 9 were waited for; matrix products, arithmetic and copies ran while one was open for 3% of the time, Pallas kernels for 14%

profile of v1, /device:TPU:231, one launch (start us, length us, event | category | flops | bytes accessed | tf_op | source)
XLA Modules:
  0.0 104.5 jit_solution(11553888063850237572)
XLA Ops:
  0.0 0.7 collective-permute-start.1
  0.7 1.3 %collective-permute-start.2 = (bf16[2048,256]{1,0:T(8,128)(2,1)}, bf16[2048,256]{1,0:T(8,128)(2,1)S(1)}, u32[]{:S(2)}, u32[]{:S(2)}) collective-permute-start(bf16[2048,256]{1,0:T(8,128)(2,1)} %param.7), channel_id=1, source_target_pairs={{0,2},{1,3},{2,0},{3,1},{4,6},{5,7},{6,4},{7,5},{8,10},{9,11},{10,... | collective-permute-start | bytes 3145736 | tf_op jit(solution)/shard_map/ppermute | solution.py:24
  2.0 2.2 %collective-permute-start.3 = (bf16[2048,256]{1,0:T(8,128)(2,1)}, bf16[2048,256]{1,0:T(8,128)(2,1)S(1)}, u32[]{:S(2)}, u32[]{:S(2)}) collective-permute-start(bf16[2048,256]{1,0:T(8,128)(2,1)} %param.7), channel_id=1, source_target_pairs={{0,254},{1,255},{2,252},{3,253},{4,2},{5,3},{6,0},{7,1},{8,6},{9,7... | collective-permute-start | bytes 3145736 | tf_op jit(solution)/shard_map/ppermute | solution.py:24
  4.1 2.1 %broadcast_select_fusion.4 = (bf16[2048,128]{1,0:T(8,128)(2,1)}, bf16[2048,128]{1,0:T(8,128)(2,1)S(1)}) fusion(pred[]{:T(512)S(6)} %eq.4, bf16[2048,256]{1,0:T(8,128)(2,1)} %param.7), kind=kLoop, calls=%fused_computation.4 | loop fusion | flops 524288 | bytes 2097153 | tf_op jit(solution)/shard_map/jit(_where)/select_n | solution.py:52
  6.2 0.6 collective-permute-start.4
  7.4 0.7 subtract_bitcast_fusion
  8.2 5.3 %collective-permute-done.refs_1_ = s32[34]{0:T(128)S(1)} collective-permute-done((s32[34]{0:T(128)S(1)}, s32[34]{0:T(128)S(1)}, u32[]{:S(2)}, u32[]{:S(2)}) %collective-permute-start) | collective-permute-done | bytes 168 | tf_op jit(solution)/shard_map/ppermute | solution.py:24
  13.5 1.0 collective-permute-done.4.refs_5_
  14.4 2.7 %chip_up.1.refs_6_ = f32[16,512,128]{2,1,0:T(8,128)S(1)} custom-call(s32[34]{0:T(128)S(1)} %pad_add_fusion.refs_0_.index, s32[34]{0:T(128)S(1)} %collective-permute-done.refs_1_, bf16[16,512,512]{2,1,0:T(8,128)(2,1)} %refs_2_.9, bf16[16,512,512]{2,1,0:T(8,128)(2,1)} %collective-permute-done.1.refs_3_, bf16[2048,128]{1,0:T(8,128)(2,1)S(1)} %get-tuple-element.46.refs_4_, ...), custom_call_target="tpu_custom_call" | custom-call | flops 1000 | bytes 1000 | tf_op jit(solution)/shard_map/chip_up/pallas_call | solution.py:275
  17.1 8.6 %collective-permute-done.2 = bf16[2048,256]{1,0:T(8,128)(2,1)S(1)} collective-permute-done((bf16[2048,256]{1,0:T(8,128)(2,1)}, bf16[2048,256]{1,0:T(8,128)(2,1)S(1)}, u32[]{:S(2)}, u32[]{:S(2)}) %collective-permute-start.2) | collective-permute-done | bytes 1048608 | tf_op jit(solution)/shard_map/ppermute | solution.py:24
  25.7 2.2 %collective-permute-done.3 = bf16[2048,256]{1,0:T(8,128)(2,1)S(1)} collective-permute-done((bf16[2048,256]{1,0:T(8,128)(2,1)}, bf16[2048,256]{1,0:T(8,128)(2,1)S(1)}, u32[]{:S(2)}, u32[]{:S(2)}) %collective-permute-start.3) | collective-permute-done | bytes 1048608 | tf_op jit(solution)/shard_map/ppermute | solution.py:24
  27.9 1.2 %collective-permute-start.6 = (bf16[2048,128]{1,0:T(8,128)(2,1)S(1)}, bf16[2048,128]{1,0:T(8,128)(2,1)S(1)}, u32[]{:S(2)}, u32[]{:S(2)}) collective-permute-start(bf16[2048,128]{1,0:T(8,128)(2,1)S(1)} %get-tuple-element.44), channel_id=1, source_target_pairs={{0,1},{1,0},{2,3},{3,2},{4,5},{5,4},{6,7},{7,6},{8,9},{9,8},{10,11... | collective-permute-start | bytes 1572872 | tf_op jit(solution)/shard_map/ppermute | solution.py:24
  29.2 0.1 collective-permute-start.8
  29.4 1.3 %collective-permute-done.6.refs_5_ = bf16[2048,128]{1,0:T(8,128)(2,1)S(1)} collective-permute-done((bf16[2048,128]{1,0:T(8,128)(2,1)S(1)}, bf16[2048,128]{1,0:T(8,128)(2,1)S(1)}, u32[]{:S(2)}, u32[]{:S(2)}) %collective-permute-start.6) | collective-permute-done | bytes 524320 | tf_op jit(solution)/shard_map/ppermute | solution.py:24
  30.7 3.1 %collective-permute-start.7 = (bf16[2048,128]{1,0:T(8,128)(2,1)S(1)}, bf16[2048,128]{1,0:T(8,128)(2,1)S(1)}, u32[]{:S(2)}, u32[]{:S(2)}) collective-permute-start(bf16[2048,128]{1,0:T(8,128)(2,1)S(1)} %collective-permute-done.6.refs_5_), channel_id=1, source_target_pairs={{0,254},{1,255},{2,252},{3,253},{4,2},{5,3},{6,0},{7,1},{8,6},{9,7... | collective-permute-start | bytes 1572872 | tf_op jit(solution)/shard_map/ppermute | solution.py:24
  33.7 2.8 %chip_here.1.refs_8_ = f32[16,512,128]{2,1,0:T(8,128)S(1)} custom-call(s32[34]{0:T(128)S(1)} %pad_add_fusion.refs_0_.index, s32[34]{0:T(128)S(1)} %collective-permute-done.refs_1_, bf16[16,512,512]{2,1,0:T(8,128)(2,1)} %refs_2_.9, bf16[16,512,512]{2,1,0:T(8,128)(2,1)} %collective-permute-done.1.refs_3_, bf16[2048,128]{1,0:T(8,128)(2,1)S(1)} %get-tuple-element.46.refs_4_, ...), custom_call_target="tpu_custom_call" | custom-call | flops 1000 | bytes 1000 | tf_op jit(solution)/shard_map/chip_here/pallas_call | solution.py:275
  36.6 3.1 %up.1 = (s16[4,528,128]{2,1,0:T(8,128)(2,1)S(1)}, s16[4,528,128]{2,1,0:T(8,128)(2,1)S(1)}, s16[4,528,128]{2,1,0:T(8,128)(2,1)S(1)}, f32[16,512,128]{2,1,0:T(8,128)S(1)}) custom-call(s32[34]{0:T(128)S(1)} %pad_add_fusion.refs_0_.index, s32[34]{0:T(128)S(1)} %collective-permute-done.refs_1_, ...), custom_call_target="tpu_custom_call", output_to_operand_aliasing={{3}: (6, {})} | custom-call | flops 1000 | bytes 1000 | tf_op jit(solution)/shard_map/up/pallas_call | solution.py:275
  39.7 3.8 %collective-permute-start.14 = (s16[4,528,128]{2,1,0:T(8,128)(2,1)S(1)}, s16[4,528,128]{2,1,0:T(8,128)(2,1)S(1)}, u32[]{:S(2)}, u32[]{:S(2)}) collective-permute-start(s16[4,528,128]{2,1,0:T(8,128)(2,1)S(1)} %get-tuple-element.39), channel_id=1, source_target_pairs={{0,2},{1,3},{2,0},{3,1},{4,6},{5,7},{6,4},{7,5},{8,10},{9,11},{10,... | collective-permute-start | bytes 1622024 | tf_op jit(solution)/shard_map/ppermute | solution.py:24
  43.5 0.8 collective-permute-start.11
  44.3 7.0 %collective-permute-start.12 = (s16[4,528,128]{2,1,0:T(8,128)(2,1)S(1)}, s16[4,528,128]{2,1,0:T(8,128)(2,1)S(1)}, u32[]{:S(2)}, u32[]{:S(2)}) collective-permute-start(s16[4,528,128]{2,1,0:T(8,128)(2,1)S(1)} %get-tuple-element.36), channel_id=1, source_target_pairs={{0,7},{1,6},{2,5},{3,4},{4,11},{5,10},{6,9},{7,8},{8,15},{9,14},{1... | collective-permute-start | bytes 1622024 | tf_op jit(solution)/shard_map/ppermute | solution.py:24
  51.3 2.5 %group.1.refs_6_ = f32[16,512,128]{2,1,0:T(8,128)S(1)} custom-call(s32[34]{0:T(128)S(1)} %pad_add_fusion.refs_0_.index, s32[34]{0:T(128)S(1)} %collective-permute-done.refs_1_, bf16[16,512,512]{2,1,0:T(8,128)(2,1)} %refs_2_.9, bf16[16,512,512]{2,1,0:T(8,128)(2,1)} %collective-permute-done.1.refs_3_, ...), custom_call_target="tpu_custom_call", output_to_operand_aliasing={{}: (8, {})} | custom-call | flops 1000 | bytes 1000 | tf_op jit(solution)/shard_map/group/pallas_call | solution.py:275
  53.8 18.2 %collective-permute-done.7.refs_5_ = bf16[2048,128]{1,0:T(8,128)(2,1)S(1)} collective-permute-done((bf16[2048,128]{1,0:T(8,128)(2,1)S(1)}, bf16[2048,128]{1,0:T(8,128)(2,1)S(1)}, u32[]{:S(2)}, u32[]{:S(2)}) %collective-permute-start.7) | collective-permute-done | bytes 524320 | tf_op jit(solution)/shard_map/ppermute | solution.py:24
  72.0 2.7 %far.1 = (f32[4,512,128]{2,1,0:T(8,128)S(1)}, s16[4,528,128]{2,1,0:T(8,128)(2,1)S(1)}, f32[16,512,128]{2,1,0:T(8,128)S(1)}) custom-call(s32[34]{0:T(128)S(1)} %pad_add_fusion.refs_0_.index, s32[34]{0:T(128)S(1)} %collective-permute-done.refs_1_, bf16[16,512,512]{2,1,0:T(8,128)(2,1)} %refs_2_.9, ...), custom_call_target="tpu_custom_call", output_to_operand_aliasing={{2}: (6, {})} | custom-call | flops 1000 | bytes 1000 | tf_op jit(solution)/shard_map/far/pallas_call | solution.py:275
  74.7 1.0 collective-permute-start.9
  75.7 0.4 add_up.1
  76.2 0.4 add_here.1
  76.6 1.8 %collective-permute-start.13 = (s16[4,528,128]{2,1,0:T(8,128)(2,1)S(1)}, s16[4,528,128]{2,1,0:T(8,128)(2,1)S(1)}, u32[]{:S(2)}, u32[]{:S(2)}) collective-permute-start(s16[4,528,128]{2,1,0:T(8,128)(2,1)S(1)} %add_here.1), channel_id=1, source_target_pairs={{0,3},{1,2},{2,1},{3,0},{4,7},{5,6},{6,5},{7,4},{8,11},{9,10},{10,... | collective-permute-start | bytes 1622024 | tf_op jit(solution)/shard_map/ppermute | solution.py:24
  78.4 11.1 %collective-permute-done.10.pair0 = s16[4,528,128]{2,1,0:T(8,128)(2,1)S(1)} collective-permute-done((s16[4,528,128]{2,1,0:T(8,128)(2,1)S(1)}, s16[4,528,128]{2,1,0:T(8,128)(2,1)S(1)}, u32[]{:S(2)}, u32[]{:S(2)}) %collective-permute-start.10) | collective-permute-done | bytes 540704 | tf_op jit(solution)/shard_map/ppermute | solution.py:24
  89.5 2.4 %collective-permute-done.15.below0 = s16[4,528,128]{2,1,0:T(8,128)(2,1)S(1)} collective-permute-done((s16[4,528,128]{2,1,0:T(8,128)(2,1)S(1)}, s16[4,528,128]{2,1,0:T(8,128)(2,1)S(1)}, u32[]{:S(2)}, u32[]{:S(2)}) %collective-permute-start.15) | collective-permute-done | bytes 540704 | tf_op jit(solution)/shard_map/ppermute | solution.py:24
  91.9 9.4 %collective-permute-done.13.pair1 = s16[4,528,128]{2,1,0:T(8,128)(2,1)S(1)} collective-permute-done((s16[4,528,128]{2,1,0:T(8,128)(2,1)S(1)}, s16[4,528,128]{2,1,0:T(8,128)(2,1)S(1)}, u32[]{:S(2)}, u32[]{:S(2)}) %collective-permute-start.13) | collective-permute-done | bytes 540704 | tf_op jit(solution)/shard_map/ppermute | solution.py:24
  101.3 0.3 broadcast_in_dim.10.reflect
  101.6 2.9 %final.1 = f32[2048,256]{1,0:T(8,128)} custom-call(s32[34]{0:T(128)S(1)} %pad_add_fusion.refs_0_.index, f32[16,512,128]{2,1,0:T(8,128)S(1)} %get-tuple-element.31.refs_0_.sums, f32[4,512,128]{2,1,0:T(8,128)S(1)} %collective-permute-done.9.sib, s16[4,528,128]{2,1,0:T(8,128)(2,1)S(1)} %collective-permute-done.10.pair0, ...), custom_call_target="tpu_custom_call" | custom-call | tf_op jit(solution)/shard_map/final/pallas_call | solution.py:356
  (18 shorter events, 0.4 us)
Async XLA Ops:
  0.0 14.4 %collective-permute-start.1 = (bf16[16,512,512]{2,1,0:T(8,128)(2,1)}, bf16[16,512,512]{2,1,0:T(8,128)(2,1)}, u32[]{:S(2)}, u32[]{:S(2)}) collective-permute-start(bf16[16,512,512]{2,1,0:T(8,128)(2,1)} %refs_2_.9), channel_id=1, source_target_pairs={{0,1},{1,0},{2,3},{3,2},{4,5},{5,4},{6,7},{7,6},{8,9},{9,8},{10,11... | collective-permute-start | bytes 25165832 | tf_op jit(solution)/shard_map/ppermute | solution.py:24
  0.7 25.0 %collective-permute-start.2 = (bf16[2048,256]{1,0:T(8,128)(2,1)}, bf16[2048,256]{1,0:T(8,128)(2,1)S(1)}, u32[]{:S(2)}, u32[]{:S(2)}) collective-permute-start(bf16[2048,256]{1,0:T(8,128)(2,1)} %param.7), channel_id=1, source_target_pairs={{0,2},{1,3},{2,0},{3,1},{4,6},{5,7},{6,4},{7,5},{8,10},{9,11},{10,... | collective-permute-start | bytes 3145736 | tf_op jit(solution)/shard_map/ppermute | solution.py:24
  2.0 25.9 %collective-permute-start.3 = (bf16[2048,256]{1,0:T(8,128)(2,1)}, bf16[2048,256]{1,0:T(8,128)(2,1)S(1)}, u32[]{:S(2)}, u32[]{:S(2)}) collective-permute-start(bf16[2048,256]{1,0:T(8,128)(2,1)} %param.7), channel_id=1, source_target_pairs={{0,254},{1,255},{2,252},{3,253},{4,2},{5,3},{6,0},{7,1},{8,6},{9,7... | collective-permute-start | bytes 3145736 | tf_op jit(solution)/shard_map/ppermute | solution.py:24
  6.2 8.2 %collective-permute-start.4 = (bf16[2048,128]{1,0:T(8,128)(2,1)}, bf16[2048,128]{1,0:T(8,128)(2,1)S(1)}, u32[]{:S(2)}, u32[]{:S(2)}) collective-permute-start(bf16[2048,128]{1,0:T(8,128)(2,1)} %get-tuple-element.45), channel_id=1, source_target_pairs={{0,1},{1,0},{2,3},{3,2},{4,5},{5,4},{6,7},{7,6},{8,9},{9,8},{10,11... | collective-permute-start | bytes 1572872 | tf_op jit(solution)/shard_map/ppermute | solution.py:24
  8.2 5.3 %collective-permute-start = (s32[34]{0:T(128)S(1)}, s32[34]{0:T(128)S(1)}, u32[]{:S(2)}, u32[]{:S(2)}) collective-permute-start(s32[34]{0:T(128)S(1)} %pad_add_fusion.refs_0_.index), channel_id=1, source_target_pairs={{0,1},{1,0},{2,3},{3,2},{4,5},{5,4},{6,7},{7,6},{8,9},{9,8},{10,11... | collective-permute-start | bytes 416 | tf_op jit(solution)/shard_map/ppermute | solution.py:24
  27.9 2.7 %collective-permute-start.6 = (bf16[2048,128]{1,0:T(8,128)(2,1)S(1)}, bf16[2048,128]{1,0:T(8,128)(2,1)S(1)}, u32[]{:S(2)}, u32[]{:S(2)}) collective-permute-start(bf16[2048,128]{1,0:T(8,128)(2,1)S(1)} %get-tuple-element.44), channel_id=1, source_target_pairs={{0,1},{1,0},{2,3},{3,2},{4,5},{5,4},{6,7},{7,6},{8,9},{9,8},{10,11... | collective-permute-start | bytes 1572872 | tf_op jit(solution)/shard_map/ppermute | solution.py:24
  29.2 7.4 %collective-permute-start.8 = (bf16[2048,128]{1,0:T(8,128)(2,1)S(1)}, bf16[2048,128]{1,0:T(8,128)(2,1)S(1)}, u32[]{:S(2)}, u32[]{:S(2)}) collective-permute-start(bf16[2048,128]{1,0:T(8,128)(2,1)S(1)} %get-tuple-element.41), channel_id=1, source_target_pairs={{0,1},{1,0},{2,3},{3,2},{4,5},{5,4},{6,7},{7,6},{8,9},{9,8},{10,11... | collective-permute-start | bytes 1572872 | tf_op jit(solution)/shard_map/ppermute | solution.py:24
  29.3 24.5 %collective-permute-start.5 = (bf16[2048,128]{1,0:T(8,128)(2,1)S(1)}, bf16[2048,128]{1,0:T(8,128)(2,1)S(1)}, u32[]{:S(2)}, u32[]{:S(2)}) collective-permute-start(bf16[2048,128]{1,0:T(8,128)(2,1)S(1)} %get-tuple-element.42.refs_6_), channel_id=1, source_target_pairs={{0,2},{1,3},{2,0},{3,1},{4,6},{5,7},{6,4},{7,5},{8,10},{9,11},{10,... | collective-permute-start | bytes 1572872 | tf_op jit(solution)/shard_map/ppermute | solution.py:24
  30.7 41.3 %collective-permute-start.7 = (bf16[2048,128]{1,0:T(8,128)(2,1)S(1)}, bf16[2048,128]{1,0:T(8,128)(2,1)S(1)}, u32[]{:S(2)}, u32[]{:S(2)}) collective-permute-start(bf16[2048,128]{1,0:T(8,128)(2,1)S(1)} %collective-permute-done.6.refs_5_), channel_id=1, source_target_pairs={{0,254},{1,255},{2,252},{3,253},{4,2},{5,3},{6,0},{7,1},{8,6},{9,7... | collective-permute-start | bytes 1572872 | tf_op jit(solution)/shard_map/ppermute | solution.py:24
  39.7 36.0 %collective-permute-start.14 = (s16[4,528,128]{2,1,0:T(8,128)(2,1)S(1)}, s16[4,528,128]{2,1,0:T(8,128)(2,1)S(1)}, u32[]{:S(2)}, u32[]{:S(2)}) collective-permute-start(s16[4,528,128]{2,1,0:T(8,128)(2,1)S(1)} %get-tuple-element.39), channel_id=1, source_target_pairs={{0,2},{1,3},{2,0},{3,1},{4,6},{5,7},{6,4},{7,5},{8,10},{9,11},{10,... | collective-permute-start | bytes 1622024 | tf_op jit(solution)/shard_map/ppermute | solution.py:24
  43.5 32.7 %collective-permute-start.11 = (s16[4,528,128]{2,1,0:T(8,128)(2,1)S(1)}, s16[4,528,128]{2,1,0:T(8,128)(2,1)S(1)}, u32[]{:S(2)}, u32[]{:S(2)}) collective-permute-start(s16[4,528,128]{2,1,0:T(8,128)(2,1)S(1)} %get-tuple-element.35), channel_id=1, source_target_pairs={{0,6},{1,7},{2,4},{3,5},{4,10},{5,11},{6,8},{7,9},{8,14},{9,15},{1... | collective-permute-start | bytes 1622024 | tf_op jit(solution)/shard_map/ppermute | solution.py:24
  44.3 31.9 %collective-permute-start.12 = (s16[4,528,128]{2,1,0:T(8,128)(2,1)S(1)}, s16[4,528,128]{2,1,0:T(8,128)(2,1)S(1)}, u32[]{:S(2)}, u32[]{:S(2)}) collective-permute-start(s16[4,528,128]{2,1,0:T(8,128)(2,1)S(1)} %get-tuple-element.36), channel_id=1, source_target_pairs={{0,7},{1,6},{2,5},{3,4},{4,11},{5,10},{6,9},{7,8},{8,15},{9,14},{1... | collective-permute-start | bytes 1622024 | tf_op jit(solution)/shard_map/ppermute | solution.py:24
  74.7 26.6 %collective-permute-start.9 = (f32[4,512,128]{2,1,0:T(8,128)S(1)}, f32[4,512,128]{2,1,0:T(8,128)S(1)}, u32[]{:S(2)}, u32[]{:S(2)}) collective-permute-start(f32[4,512,128]{2,1,0:T(8,128)S(1)} %get-tuple-element.32), channel_id=1, source_target_pairs={{0,1},{1,0},{2,3},{3,2},{4,5},{5,4},{6,7},{7,6},{8,9},{9,8},{10,11... | collective-permute-start | bytes 3145736 | tf_op jit(solution)/shard_map/ppermute | solution.py:24
  75.6 13.8 %collective-permute-start.10 = (s16[4,528,128]{2,1,0:T(8,128)(2,1)S(1)}, s16[4,528,128]{2,1,0:T(8,128)(2,1)S(1)}, u32[]{:S(2)}, u32[]{:S(2)}) collective-permute-start(s16[4,528,128]{2,1,0:T(8,128)(2,1)S(1)} %get-tuple-element.33), channel_id=1, source_target_pairs={{0,2},{1,3},{2,0},{3,1},{4,6},{5,7},{6,4},{7,5},{8,10},{9,11},{10,... | collective-permute-start | bytes 1622024 | tf_op jit(solution)/shard_map/ppermute | solution.py:24
  75.7 25.6 %copy-start.1 = (f32[2048]{0:T(1024)S(1)}, f32[2048]{0:T(1024)}, u32[]{:S(2)}) copy-start(f32[2048]{0:T(1024)} %param.9) | copy-start | bytes 24580
  76.1 25.5 %copy-start = (bf16[2048,256]{1,0:T(8,128)(2,1)S(1)}, bf16[2048,256]{1,0:T(8,128)(2,1)}, u32[]{:S(2)}) copy-start(bf16[2048,256]{1,0:T(8,128)(2,1)} %source.1) | copy-start | bytes 3145732
  76.1 15.8 %collective-permute-start.15 = (s16[4,528,128]{2,1,0:T(8,128)(2,1)S(1)}, s16[4,528,128]{2,1,0:T(8,128)(2,1)S(1)}, u32[]{:S(2)}, u32[]{:S(2)}) collective-permute-start(s16[4,528,128]{2,1,0:T(8,128)(2,1)S(1)} %add_up.1), channel_id=1, source_target_pairs={{0,6},{1,7},{2,4},{3,5},{4,10},{5,11},{6,8},{7,9},{8,14},{9,15},{1... | collective-permute-start | bytes 1622024 | tf_op jit(solution)/shard_map/ppermute | solution.py:24
  76.6 24.7 %collective-permute-start.13 = (s16[4,528,128]{2,1,0:T(8,128)(2,1)S(1)}, s16[4,528,128]{2,1,0:T(8,128)(2,1)S(1)}, u32[]{:S(2)}, u32[]{:S(2)}) collective-permute-start(s16[4,528,128]{2,1,0:T(8,128)(2,1)S(1)} %add_here.1), channel_id=1, source_target_pairs={{0,3},{1,2},{2,1},{3,0},{4,7},{5,6},{6,5},{7,4},{8,11},{9,10},{10,... | collective-permute-start | bytes 1622024 | tf_op jit(solution)/shard_map/ppermute | solution.py:24

commit v2 on v1

--- a/solution.py
+++ b/solution.py
@@ -319,16 +319,17 @@
     ]
 
     (up,) = call(chip_up_kernel, "chip_up", tables + [mine, sib], [group], scratch=scratch)
-    pair, near, up = lax.optimization_barrier((pair, near, up))
+    (here,) = call(chip_here_kernel, "chip_here", tables + [mine, sib], [group], scratch=scratch)
+    pair, up, here = lax.optimization_barrier((pair, up, here))
     pair0, other = split_columns(pair, k)
+    near, _ = lax.optimization_barrier((near, other))
+    far1 = send(other, lambda r, h, k: (r - 1, 1 - h, 1 - k))
     pair1 = send(other, to_sibling)
     near0, other = split_columns(near, k)
     near1 = send(other, to_sibling)
     far0 = send(near0, across)
-    far1 = send(pair1, down)
-
-    (here,) = call(chip_here_kernel, "chip_here", tables + [mine, sib], [group], scratch=scratch)
-    up, here, near1 = lax.optimization_barrier((up, here, near1))
+
+    up, near1 = lax.optimization_barrier((up, near1))
     far_q0, far_q1, near_q1, up = call(
         up_kernel, "up", tables + [pair0, pair1, up], [sent, sent, sent, group], {6: 3}, scratch
     )
@@ -345,11 +346,11 @@
     )
     here0 = send(other_q0, lambda r, h, k: (r, 1 - h, k))
     here_sib = send(own_f1, lambda r, h, k: (r, h, 1 - k))
+    (here1,) = call(lambda *refs: add_kernel(3 * pb, *refs), "add_here", [here, part1], [sent])
+    part0, below1, _ = lax.optimization_barrier((part0, below1, here1))
+    here1 = send(here1, lambda r, h, k: (r, 1 - h, 1 - k))
     (below0,) = call(lambda *refs: add_kernel(2 * pb, *refs), "add_up", [up, part0], [sent])
     below0 = send(below0, lambda r, h, k: (r + 1, 1 - h, k))
-    part1, below1 = lax.optimization_barrier((part1, below1))
-    (here1,) = call(lambda *refs: add_kernel(3 * pb, *refs), "add_here", [here, part1], [sent])
-    here1 = send(here1, lambda r, h, k: (r, 1 - h, 1 - k))
 
     factor = jnp.broadcast_to(reflect[:, None], (piece_rows, half))
     args = [here, here_sib, here0, here1, below0, below1, source, factor]

time: 106 us -> 104 us (0.981)
  the two profiles are of different devices: /device:TPU:231 before, /device:TPU:1 now
where the time goes in v2:
time: 104 us; the launch traced here: 102 us
  waiting for transfers between devices  51.3 us (49%)
  Pallas kernels  23.9 us (23%)
  starting transfers between devices  23.1 us (22%)
  other arithmetic  2.96 us (3%)
    ppermute x16, waiting for transfers between devices, send(): return lax.ppermute(x, AXES, pairs)  51.3 us
    ppermute x16, starting transfers between devices, send(): return lax.ppermute(x, AXES, pairs)  23.1 us
    pallas_call x7, Pallas kernels, call(): pl.pallas_call(kernel, in_specs=specs, out_specs=[pl.BlockSpec(memory_spa...  21 us
    pallas_call x1, Pallas kernels, per_device(): pl.pallas_call(final_kernel, grid=(pb,), in_specs=[pl.BlockSpec(memory_sp...  2.91 us
    select_n x3, other arithmetic, split_columns(): return (jnp.where(first, left, right), jnp.where(first, right, left))  2.21 us
  transfers between devices with their start and end apart: 16, of which 8 were waited for; matrix products, arithmetic and copies ran while one was open for 3% of the time, Pallas kernels for 20%

profile of v2, /device:TPU:1, one launch (start us, length us, event | category | flops | bytes accessed | tf_op | source)
XLA Modules:
  0.0 102.4 jit_solution(5582657909638109001)
XLA Ops:
  0.0 3.2 %collective-permute-start.1 = (bf16[16,512,512]{2,1,0:T(8,128)(2,1)}, bf16[16,512,512]{2,1,0:T(8,128)(2,1)}, u32[]{:S(2)}, u32[]{:S(2)}) collective-permute-start(bf16[16,512,512]{2,1,0:T(8,128)(2,1)} %refs_2_.9), channel_id=1, source_target_pairs={{0,1},{1,0},{2,3},{3,2},{4,5},{5,4},{6,7},{7,6},{8,9},{9,8},{10,11... | collective-permute-start | bytes 25165832 | tf_op jit(solution)/shard_map/ppermute | solution.py:24
  3.2 8.9 %collective-permute-start.2 = (bf16[2048,256]{1,0:T(8,128)(2,1)}, bf16[2048,256]{1,0:T(8,128)(2,1)S(1)}, u32[]{:S(2)}, u32[]{:S(2)}) collective-permute-start(bf16[2048,256]{1,0:T(8,128)(2,1)} %param.7), channel_id=1, source_target_pairs={{0,254},{1,255},{2,252},{3,253},{4,2},{5,3},{6,0},{7,1},{8,6},{9,7... | collective-permute-start | bytes 3145736 | tf_op jit(solution)/shard_map/ppermute | solution.py:24
  12.2 2.1 %broadcast_select_fusion.4 = (bf16[2048,128]{1,0:T(8,128)(2,1)}, bf16[2048,128]{1,0:T(8,128)(2,1)S(1)}) fusion(pred[]{:T(512)S(6)} %eq.4, bf16[2048,256]{1,0:T(8,128)(2,1)} %param.7), kind=kLoop, calls=%fused_computation.4 | loop fusion | flops 524288 | bytes 2097153 | tf_op jit(solution)/shard_map/jit(_where)/select_n | solution.py:52
  14.3 0.6 collective-permute-start.4
  15.5 0.7 subtract_bitcast_fusion
  16.3 1.1 %collective-permute-done.refs_1_ = s32[34]{0:T(128)S(1)} collective-permute-done((s32[34]{0:T(128)S(1)}, s32[34]{0:T(128)S(1)}, u32[]{:S(2)}, u32[]{:S(2)}) %collective-permute-start) | collective-permute-done | bytes 168 | tf_op jit(solution)/shard_map/ppermute | solution.py:24
  17.4 3.5 %chip_up.1.refs_6_ = f32[16,512,128]{2,1,0:T(8,128)S(1)} custom-call(s32[34]{0:T(128)S(1)} %pad_add_fusion.refs_0_.index, s32[34]{0:T(128)S(1)} %collective-permute-done.refs_1_, bf16[16,512,512]{2,1,0:T(8,128)(2,1)} %refs_2_.9, bf16[16,512,512]{2,1,0:T(8,128)(2,1)} %collective-permute-done.1.refs_3_, bf16[2048,128]{1,0:T(8,128)(2,1)S(1)} %get-tuple-element.46.refs_4_, ...), custom_call_target="tpu_custom_call" | custom-call | flops 1000 | bytes 1000 | tf_op jit(solution)/shard_map/chip_up/pallas_call | solution.py:275
  20.9 3.7 %chip_here.1.refs_8_ = f32[16,512,128]{2,1,0:T(8,128)S(1)} custom-call(s32[34]{0:T(128)S(1)} %pad_add_fusion.refs_0_.index, s32[34]{0:T(128)S(1)} %collective-permute-done.refs_1_, bf16[16,512,512]{2,1,0:T(8,128)(2,1)} %refs_2_.9, bf16[16,512,512]{2,1,0:T(8,128)(2,1)} %collective-permute-done.1.refs_3_, bf16[2048,128]{1,0:T(8,128)(2,1)S(1)} %get-tuple-element.46.refs_4_, ...), custom_call_target="tpu_custom_call" | custom-call | flops 1000 | bytes 1000 | tf_op jit(solution)/shard_map/chip_here/pallas_call | solution.py:275
  24.6 3.6 %collective-permute-done.3 = bf16[2048,256]{1,0:T(8,128)(2,1)S(1)} collective-permute-done((bf16[2048,256]{1,0:T(8,128)(2,1)}, bf16[2048,256]{1,0:T(8,128)(2,1)S(1)}, u32[]{:S(2)}, u32[]{:S(2)}) %collective-permute-start.3) | collective-permute-done | bytes 1048608 | tf_op jit(solution)/shard_map/ppermute | solution.py:24
  28.3 6.5 %collective-permute-done.2 = bf16[2048,256]{1,0:T(8,128)(2,1)S(1)} collective-permute-done((bf16[2048,256]{1,0:T(8,128)(2,1)}, bf16[2048,256]{1,0:T(8,128)(2,1)S(1)}, u32[]{:S(2)}, u32[]{:S(2)}) %collective-permute-start.2) | collective-permute-done | bytes 1048608 | tf_op jit(solution)/shard_map/ppermute | solution.py:24
  34.9 1.2 %collective-permute-start.8 = (bf16[2048,128]{1,0:T(8,128)(2,1)S(1)}, bf16[2048,128]{1,0:T(8,128)(2,1)S(1)}, u32[]{:S(2)}, u32[]{:S(2)}) collective-permute-start(bf16[2048,128]{1,0:T(8,128)(2,1)S(1)} %get-tuple-element.41), channel_id=1, source_target_pairs={{0,1},{1,0},{2,3},{3,2},{4,5},{5,4},{6,7},{7,6},{8,9},{9,8},{10,11... | collective-permute-start | bytes 1572872 | tf_op jit(solution)/shard_map/ppermute | solution.py:24
  36.0 0.1 collective-permute-start.7
  36.1 0.4 collective-permute-start.5
  36.5 7.5 %collective-permute-start.6 = (bf16[2048,128]{1,0:T(8,128)(2,1)S(1)}, bf16[2048,128]{1,0:T(8,128)(2,1)S(1)}, u32[]{:S(2)}, u32[]{:S(2)}) collective-permute-start(bf16[2048,128]{1,0:T(8,128)(2,1)S(1)} %get-tuple-element.44), channel_id=1, source_target_pairs={{0,255},{1,254},{2,253},{3,252},{4,3},{5,2},{6,1},{7,0},{8,7},{9,6... | collective-permute-start | bytes 1572872 | tf_op jit(solution)/shard_map/ppermute | solution.py:24
  44.0 4.5 %up.1 = (s16[4,528,128]{2,1,0:T(8,128)(2,1)S(1)}, s16[4,528,128]{2,1,0:T(8,128)(2,1)S(1)}, s16[4,528,128]{2,1,0:T(8,128)(2,1)S(1)}, f32[16,512,128]{2,1,0:T(8,128)S(1)}) custom-call(s32[34]{0:T(128)S(1)} %pad_add_fusion.refs_0_.index, s32[34]{0:T(128)S(1)} %collective-permute-done.refs_1_, ...), custom_call_target="tpu_custom_call", output_to_operand_aliasing={{3}: (6, {})} | custom-call | flops 1000 | bytes 1000 | tf_op jit(solution)/shard_map/up/pallas_call | solution.py:275
  48.5 0.1 collective-permute-start.11
  48.6 0.1 collective-permute-start.13
  48.7 0.1 collective-permute-start.14
  48.8 4.5 %group.1.refs_6_ = f32[16,512,128]{2,1,0:T(8,128)S(1)} custom-call(s32[34]{0:T(128)S(1)} %pad_add_fusion.refs_0_.index, s32[34]{0:T(128)S(1)} %collective-permute-done.refs_1_, bf16[16,512,512]{2,1,0:T(8,128)(2,1)} %refs_2_.9, bf16[16,512,512]{2,1,0:T(8,128)(2,1)} %collective-permute-done.1.refs_3_, ...), custom_call_target="tpu_custom_call", output_to_operand_aliasing={{}: (8, {})} | custom-call | flops 1000 | bytes 1000 | tf_op jit(solution)/shard_map/group/pallas_call | solution.py:275
  53.3 2.2 %collective-permute-done.6.refs_5_ = bf16[2048,128]{1,0:T(8,128)(2,1)S(1)} collective-permute-done((bf16[2048,128]{1,0:T(8,128)(2,1)S(1)}, bf16[2048,128]{1,0:T(8,128)(2,1)S(1)}, u32[]{:S(2)}, u32[]{:S(2)}) %collective-permute-start.6) | collective-permute-done | bytes 524320 | tf_op jit(solution)/shard_map/ppermute | solution.py:24
  55.6 4.0 %far.1 = (f32[4,512,128]{2,1,0:T(8,128)S(1)}, s16[4,528,128]{2,1,0:T(8,128)(2,1)S(1)}, f32[16,512,128]{2,1,0:T(8,128)S(1)}) custom-call(s32[34]{0:T(128)S(1)} %pad_add_fusion.refs_0_.index, s32[34]{0:T(128)S(1)} %collective-permute-done.refs_1_, bf16[16,512,512]{2,1,0:T(8,128)(2,1)} %refs_2_.9, ...), custom_call_target="tpu_custom_call", output_to_operand_aliasing={{2}: (6, {})} | custom-call | flops 1000 | bytes 1000 | tf_op jit(solution)/shard_map/far/pallas_call | solution.py:275
  59.6 0.7 collective-permute-start.9
  60.3 7.7 %collective-permute-done.11.refs_1_ = s16[4,528,128]{2,1,0:T(8,128)(2,1)S(1)} collective-permute-done((s16[4,528,128]{2,1,0:T(8,128)(2,1)S(1)}, s16[4,528,128]{2,1,0:T(8,128)(2,1)S(1)}, u32[]{:S(2)}, u32[]{:S(2)}) %collective-permute-start.11) | collective-permute-done | bytes 540704 | tf_op jit(solution)/shard_map/ppermute | solution.py:24
  67.9 0.4 add_here.1
  68.3 0.1 collective-permute-start.12
  68.4 11.2 %collective-permute-done.14.below1 = s16[4,528,128]{2,1,0:T(8,128)(2,1)S(1)} collective-permute-done((s16[4,528,128]{2,1,0:T(8,128)(2,1)S(1)}, s16[4,528,128]{2,1,0:T(8,128)(2,1)S(1)}, u32[]{:S(2)}, u32[]{:S(2)}) %collective-permute-start.14) | collective-permute-done | bytes 540704 | tf_op jit(solution)/shard_map/ppermute | solution.py:24
  79.6 0.4 add_up.1
  80.0 0.1 collective-permute-start.15
  80.1 5.7 %collective-permute-done.12.pair1 = s16[4,528,128]{2,1,0:T(8,128)(2,1)S(1)} collective-permute-done((s16[4,528,128]{2,1,0:T(8,128)(2,1)S(1)}, s16[4,528,128]{2,1,0:T(8,128)(2,1)S(1)}, u32[]{:S(2)}, u32[]{:S(2)}) %collective-permute-start.12) | collective-permute-done | bytes 540704 | tf_op jit(solution)/shard_map/ppermute | solution.py:24
  85.9 13.3 %collective-permute-done.15.below0 = s16[4,528,128]{2,1,0:T(8,128)(2,1)S(1)} collective-permute-done((s16[4,528,128]{2,1,0:T(8,128)(2,1)S(1)}, s16[4,528,128]{2,1,0:T(8,128)(2,1)S(1)}, u32[]{:S(2)}, u32[]{:S(2)}) %collective-permute-start.15) | collective-permute-done | bytes 540704 | tf_op jit(solution)/shard_map/ppermute | solution.py:24
  99.1 0.3 broadcast_in_dim.10.reflect
  99.5 2.9 %final.1 = f32[2048,256]{1,0:T(8,128)} custom-call(s32[34]{0:T(128)S(1)} %pad_add_fusion.refs_0_.index, f32[16,512,128]{2,1,0:T(8,128)S(1)} %get-tuple-element.31.refs_0_.sums, f32[4,512,128]{2,1,0:T(8,128)S(1)} %collective-permute-done.9.sib, s16[4,528,128]{2,1,0:T(8,128)(2,1)S(1)} %collective-permute-done.10.pair0, ...), custom_call_target="tpu_custom_call" | custom-call | tf_op jit(solution)/shard_map/final/pallas_call | solution.py:357
  (18 shorter events, 0.3 us)
Async XLA Ops:
  0.0 17.4 %collective-permute-start.1 = (bf16[16,512,512]{2,1,0:T(8,128)(2,1)}, bf16[16,512,512]{2,1,0:T(8,128)(2,1)}, u32[]{:S(2)}, u32[]{:S(2)}) collective-permute-start(bf16[16,512,512]{2,1,0:T(8,128)(2,1)} %refs_2_.9), channel_id=1, source_target_pairs={{0,1},{1,0},{2,3},{3,2},{4,5},{5,4},{6,7},{7,6},{8,9},{9,8},{10,11... | collective-permute-start | bytes 25165832 | tf_op jit(solution)/shard_map/ppermute | solution.py:24
  3.2 25.0 %collective-permute-start.3 = (bf16[2048,256]{1,0:T(8,128)(2,1)}, bf16[2048,256]{1,0:T(8,128)(2,1)S(1)}, u32[]{:S(2)}, u32[]{:S(2)}) collective-permute-start(bf16[2048,256]{1,0:T(8,128)(2,1)} %param.7), channel_id=1, source_target_pairs={{0,2},{1,3},{2,0},{3,1},{4,6},{5,7},{6,4},{7,5},{8,10},{9,11},{10,... | collective-permute-start | bytes 3145736 | tf_op jit(solution)/shard_map/ppermute | solution.py:24
  3.2 31.5 %collective-permute-start.2 = (bf16[2048,256]{1,0:T(8,128)(2,1)}, bf16[2048,256]{1,0:T(8,128)(2,1)S(1)}, u32[]{:S(2)}, u32[]{:S(2)}) collective-permute-start(bf16[2048,256]{1,0:T(8,128)(2,1)} %param.7), channel_id=1, source_target_pairs={{0,254},{1,255},{2,252},{3,253},{4,2},{5,3},{6,0},{7,1},{8,6},{9,7... | collective-permute-start | bytes 3145736 | tf_op jit(solution)/shard_map/ppermute | solution.py:24
  14.3 3.1 %collective-permute-start.4 = (bf16[2048,128]{1,0:T(8,128)(2,1)}, bf16[2048,128]{1,0:T(8,128)(2,1)S(1)}, u32[]{:S(2)}, u32[]{:S(2)}) collective-permute-start(bf16[2048,128]{1,0:T(8,128)(2,1)} %get-tuple-element.45), channel_id=1, source_target_pairs={{0,1},{1,0},{2,3},{3,2},{4,5},{5,4},{6,7},{7,6},{8,9},{9,8},{10,11... | collective-permute-start | bytes 1572872 | tf_op jit(solution)/shard_map/ppermute | solution.py:24
  16.2 1.1 %collective-permute-start = (s32[34]{0:T(128)S(1)}, s32[34]{0:T(128)S(1)}, u32[]{:S(2)}, u32[]{:S(2)}) collective-permute-start(s32[34]{0:T(128)S(1)} %pad_add_fusion.refs_0_.index), channel_id=1, source_target_pairs={{0,1},{1,0},{2,3},{3,2},{4,5},{5,4},{6,7},{7,6},{8,9},{9,8},{10,11... | collective-permute-start | bytes 416 | tf_op jit(solution)/shard_map/ppermute | solution.py:24
  34.9 9.2 %collective-permute-start.8 = (bf16[2048,128]{1,0:T(8,128)(2,1)S(1)}, bf16[2048,128]{1,0:T(8,128)(2,1)S(1)}, u32[]{:S(2)}, u32[]{:S(2)}) collective-permute-start(bf16[2048,128]{1,0:T(8,128)(2,1)S(1)} %get-tuple-element.41), channel_id=1, source_target_pairs={{0,1},{1,0},{2,3},{3,2},{4,5},{5,4},{6,7},{7,6},{8,9},{9,8},{10,11... | collective-permute-start | bytes 1572872 | tf_op jit(solution)/shard_map/ppermute | solution.py:24
  36.0 8.0 %collective-permute-start.7 = (bf16[2048,128]{1,0:T(8,128)(2,1)S(1)}, bf16[2048,128]{1,0:T(8,128)(2,1)S(1)}, u32[]{:S(2)}, u32[]{:S(2)}) collective-permute-start(bf16[2048,128]{1,0:T(8,128)(2,1)S(1)} %get-tuple-element.44), channel_id=1, source_target_pairs={{0,1},{1,0},{2,3},{3,2},{4,5},{5,4},{6,7},{7,6},{8,9},{9,8},{10,11... | collective-permute-start | bytes 1572872 | tf_op jit(solution)/shard_map/ppermute | solution.py:24
  36.1 17.2 %collective-permute-start.5 = (bf16[2048,128]{1,0:T(8,128)(2,1)S(1)}, bf16[2048,128]{1,0:T(8,128)(2,1)S(1)}, u32[]{:S(2)}, u32[]{:S(2)}) collective-permute-start(bf16[2048,128]{1,0:T(8,128)(2,1)S(1)} %get-tuple-element.42.refs_6_), channel_id=1, source_target_pairs={{0,2},{1,3},{2,0},{3,1},{4,6},{5,7},{6,4},{7,5},{8,10},{9,11},{10,... | collective-permute-start | bytes 1572872 | tf_op jit(solution)/shard_map/ppermute | solution.py:24
  36.5 19.0 %collective-permute-start.6 = (bf16[2048,128]{1,0:T(8,128)(2,1)S(1)}, bf16[2048,128]{1,0:T(8,128)(2,1)S(1)}, u32[]{:S(2)}, u32[]{:S(2)}) collective-permute-start(bf16[2048,128]{1,0:T(8,128)(2,1)S(1)} %get-tuple-element.44), channel_id=1, source_target_pairs={{0,255},{1,254},{2,253},{3,252},{4,3},{5,2},{6,1},{7,0},{8,7},{9,6... | collective-permute-start | bytes 1572872 | tf_op jit(solution)/shard_map/ppermute | solution.py:24
  48.5 19.4 %collective-permute-start.11 = (s16[4,528,128]{2,1,0:T(8,128)(2,1)S(1)}, s16[4,528,128]{2,1,0:T(8,128)(2,1)S(1)}, u32[]{:S(2)}, u32[]{:S(2)}) collective-permute-start(s16[4,528,128]{2,1,0:T(8,128)(2,1)S(1)} %get-tuple-element.35), channel_id=1, source_target_pairs={{0,6},{1,7},{2,4},{3,5},{4,10},{5,11},{6,8},{7,9},{8,14},{9,15},{1... | collective-permute-start | bytes 1622024 | tf_op jit(solution)/shard_map/ppermute | solution.py:24
  48.6 19.8 %collective-permute-start.13 = (s16[4,528,128]{2,1,0:T(8,128)(2,1)S(1)}, s16[4,528,128]{2,1,0:T(8,128)(2,1)S(1)}, u32[]{:S(2)}, u32[]{:S(2)}) collective-permute-start(s16[4,528,128]{2,1,0:T(8,128)(2,1)S(1)} %get-tuple-element.37), channel_id=1, source_target_pairs={{0,2},{1,3},{2,0},{3,1},{4,6},{5,7},{6,4},{7,5},{8,10},{9,11},{10,... | collective-permute-start | bytes 1622024 | tf_op jit(solution)/shard_map/ppermute | solution.py:24
  48.7 30.9 %collective-permute-start.14 = (s16[4,528,128]{2,1,0:T(8,128)(2,1)S(1)}, s16[4,528,128]{2,1,0:T(8,128)(2,1)S(1)}, u32[]{:S(2)}, u32[]{:S(2)}) collective-permute-start(s16[4,528,128]{2,1,0:T(8,128)(2,1)S(1)} %get-tuple-element.38), channel_id=1, source_target_pairs={{0,7},{1,6},{2,5},{3,4},{4,11},{5,10},{6,9},{7,8},{8,15},{9,14},{1... | collective-permute-start | bytes 1622024 | tf_op jit(solution)/shard_map/ppermute | solution.py:24
  59.6 20.6 %collective-permute-start.9 = (f32[4,512,128]{2,1,0:T(8,128)S(1)}, f32[4,512,128]{2,1,0:T(8,128)S(1)}, u32[]{:S(2)}, u32[]{:S(2)}) collective-permute-start(f32[4,512,128]{2,1,0:T(8,128)S(1)} %get-tuple-element.32), channel_id=1, source_target_pairs={{0,1},{1,0},{2,3},{3,2},{4,5},{5,4},{6,7},{7,6},{8,9},{9,8},{10,11... | collective-permute-start | bytes 3145736 | tf_op jit(solution)/shard_map/ppermute | solution.py:24
  60.3 19.9 %collective-permute-start.10 = (s16[4,528,128]{2,1,0:T(8,128)(2,1)S(1)}, s16[4,528,128]{2,1,0:T(8,128)(2,1)S(1)}, u32[]{:S(2)}, u32[]{:S(2)}) collective-permute-start(s16[4,528,128]{2,1,0:T(8,128)(2,1)S(1)} %get-tuple-element.33), channel_id=1, source_target_pairs={{0,2},{1,3},{2,0},{3,1},{4,6},{5,7},{6,4},{7,5},{8,10},{9,11},{10,... | collective-permute-start | bytes 1622024 | tf_op jit(solution)/shard_map/ppermute | solution.py:24
  67.9 31.2 %copy-start.1 = (f32[2048]{0:T(1024)S(1)}, f32[2048]{0:T(1024)}, u32[]{:S(2)}) copy-start(f32[2048]{0:T(1024)} %param.9) | copy-start | bytes 24580
  68.3 31.2 %copy-start = (bf16[2048,256]{1,0:T(8,128)(2,1)S(1)}, bf16[2048,256]{1,0:T(8,128)(2,1)}, u32[]{:S(2)}) copy-start(bf16[2048,256]{1,0:T(8,128)(2,1)} %source.1) | copy-start | bytes 3145732
  68.3 17.6 %collective-permute-start.12 = (s16[4,528,128]{2,1,0:T(8,128)(2,1)S(1)}, s16[4,528,128]{2,1,0:T(8,128)(2,1)S(1)}, u32[]{:S(2)}, u32[]{:S(2)}) collective-permute-start(s16[4,528,128]{2,1,0:T(8,128)(2,1)S(1)} %add_here.1), channel_id=1, source_target_pairs={{0,3},{1,2},{2,1},{3,0},{4,7},{5,6},{6,5},{7,4},{8,11},{9,10},{10,... | collective-permute-start | bytes 1622024 | tf_op jit(solution)/shard_map/ppermute | solution.py:24
  80.0 19.1 %collective-permute-start.15 = (s16[4,528,128]{2,1,0:T(8,128)(2,1)S(1)}, s16[4,528,128]{2,1,0:T(8,128)(2,1)S(1)}, u32[]{:S(2)}, u32[]{:S(2)}) collective-permute-start(s16[4,528,128]{2,1,0:T(8,128)(2,1)S(1)} %add_up.1), channel_id=1, source_target_pairs={{0,6},{1,7},{2,4},{3,5},{4,10},{5,11},{6,8},{7,9},{8,14},{9,15},{1... | collective-permute-start | bytes 1622024 | tf_op jit(solution)/shard_map/ppermute | solution.py:24

commit v3 on v2

--- a/solution.py
+++ b/solution.py
@@ -333,24 +333,26 @@
     far_q0, far_q1, near_q1, up = call(
         up_kernel, "up", tables + [pair0, pair1, up], [sent, sent, sent, group], {6: 3}, scratch
     )
-    part1 = send(far_q1, lambda r, h, k: (r + 1, 1 - h, k))
     part0 = send(far_q0, across)
-    below1 = send(near_q1, lambda r, h, k: (r + 1, 1 - h, 1 - k))
 
     (here,) = call(
         group_kernel, "group", tables + [pair0, pair1, near0, near1, here], [group], {8: 0}, scratch
     )
-    far0, far1, here = lax.optimization_barrier((far0, far1, here))
+    far0, far1, here, far_q1, near_q1 = lax.optimization_barrier(
+        (far0, far1, here, far_q1, near_q1)
+    )
+    part1 = send(far_q1, lambda r, h, k: (r + 1, 1 - h, k))
+    below1 = send(near_q1, lambda r, h, k: (r + 1, 1 - h, 1 - k))
     own_f1, other_q0, here = call(
         far_kernel, "far", tables + [far0, far1, here], [sums, sent, group], {6: 2}, scratch
     )
     here0 = send(other_q0, lambda r, h, k: (r, 1 - h, k))
     here_sib = send(own_f1, lambda r, h, k: (r, h, 1 - k))
+    (below0,) = call(lambda *refs: add_kernel(2 * pb, *refs), "add_up", [up, part0], [sent])
+    part1, _ = lax.optimization_barrier((part1, below0))
     (here1,) = call(lambda *refs: add_kernel(3 * pb, *refs), "add_here", [here, part1], [sent])
-    part0, below1, _ = lax.optimization_barrier((part0, below1, here1))
+    below0 = send(below0, lambda r, h, k: (r + 1, 1 - h, k))
     here1 = send(here1, lambda r, h, k: (r, 1 - h, 1 - k))
-    (below0,) = call(lambda *refs: add_kernel(2 * pb, *refs), "add_up", [up, part0], [sent])
-    below0 = send(below0, lambda r, h, k: (r + 1, 1 - h, k))
 
     factor = jnp.broadcast_to(reflect[:, None], (piece_rows, half))
     args = [here, here_sib, here0, here1, below0, below1, source, factor]

time: 104 us -> 102 us (0.981); the launches traced: 102 us -> 102 us
  Pallas kernels: 23.9 us -> 16.4 us
  starting transfers between devices: 23.1 us -> 29.1 us
    pallas_call x7, Pallas kernels: 21 us -> 13.5 us  [call(): pl.pallas_call(kernel, in_specs=specs, out_specs=[pl.BlockSpec(memory_spa...]
    ppermute x16, starting transfers between devices: 23.1 us -> 29.1 us  [send(): return lax.ppermute(x, AXES, pairs)]
  transfers between devices with their start and end apart: 16 -> 16, of which waited for: 8 -> 9; matrix products, arithmetic and copies ran while one was open for 3% -> 3% of each run, Pallas kernels for 20% -> 13%
where the time goes in v3:
time: 102 us
  waiting for transfers between devices  52.3 us (51%)
  starting transfers between devices  29.1 us (29%)
  Pallas kernels  16.4 us (16%)
  other arithmetic  2.96 us (3%)
    ppermute x16, waiting for transfers between devices, send(): return lax.ppermute(x, AXES, pairs)  52.3 us
    ppermute x16, starting transfers between devices, send(): return lax.ppermute(x, AXES, pairs)  29.1 us
    pallas_call x7, Pallas kernels, call(): pl.pallas_call(kernel, in_specs=specs, out_specs=[pl.BlockSpec(memory_spa...  13.5 us
    pallas_call x1, Pallas kernels, per_device(): pl.pallas_call(final_kernel, grid=(pb,), in_specs=[pl.BlockSpec(memory_sp...  2.91 us
    select_n x3, other arithmetic, split_columns(): return (jnp.where(first, left, right), jnp.where(first, right, left))  2.21 us
  transfers between devices with their start and end apart: 16, of which 9 were waited for; matrix products, arithmetic and copies ran while one was open for 3% of the time, Pallas kernels for 13%

profile of v3, /device:TPU:1, one launch (start us, length us, event | category | flops | bytes accessed | tf_op | source)
XLA Modules:
  0.0 101.9 jit_solution(7425295348184339435)
XLA Ops:
  0.0 3.2 %collective-permute-start.1 = (bf16[16,512,512]{2,1,0:T(8,128)(2,1)}, bf16[16,512,512]{2,1,0:T(8,128)(2,1)}, u32[]{:S(2)}, u32[]{:S(2)}) collective-permute-start(bf16[16,512,512]{2,1,0:T(8,128)(2,1)} %refs_2_.9), channel_id=1, source_target_pairs={{0,1},{1,0},{2,3},{3,2},{4,5},{5,4},{6,7},{7,6},{8,9},{9,8},{10,11... | collective-permute-start | bytes 25165832 | tf_op jit(solution)/shard_map/ppermute | solution.py:24
  3.2 8.9 %collective-permute-start.2 = (bf16[2048,256]{1,0:T(8,128)(2,1)}, bf16[2048,256]{1,0:T(8,128)(2,1)S(1)}, u32[]{:S(2)}, u32[]{:S(2)}) collective-permute-start(bf16[2048,256]{1,0:T(8,128)(2,1)} %param.7), channel_id=1, source_target_pairs={{0,254},{1,255},{2,252},{3,253},{4,2},{5,3},{6,0},{7,1},{8,6},{9,7... | collective-permute-start | bytes 3145736 | tf_op jit(solution)/shard_map/ppermute | solution.py:24
  12.2 2.1 %broadcast_select_fusion.4 = (bf16[2048,128]{1,0:T(8,128)(2,1)}, bf16[2048,128]{1,0:T(8,128)(2,1)S(1)}) fusion(pred[]{:T(512)S(6)} %eq.4, bf16[2048,256]{1,0:T(8,128)(2,1)} %param.7), kind=kLoop, calls=%fused_computation.4 | loop fusion | flops 524288 | bytes 2097153 | tf_op jit(solution)/shard_map/jit(_where)/select_n | solution.py:52
  14.3 0.6 collective-permute-start.4
  15.5 0.7 subtract_bitcast_fusion
  16.1 0.1 pad_add_fusion.refs_0_.index
  16.3 1.1 %collective-permute-done.refs_1_ = s32[34]{0:T(128)S(1)} collective-permute-done((s32[34]{0:T(128)S(1)}, s32[34]{0:T(128)S(1)}, u32[]{:S(2)}, u32[]{:S(2)}) %collective-permute-start) | collective-permute-done | bytes 168 | tf_op jit(solution)/shard_map/ppermute | solution.py:24
  17.4 2.7 %chip_up.1.refs_6_ = f32[16,512,128]{2,1,0:T(8,128)S(1)} custom-call(s32[34]{0:T(128)S(1)} %pad_add_fusion.refs_0_.index, s32[34]{0:T(128)S(1)} %collective-permute-done.refs_1_, bf16[16,512,512]{2,1,0:T(8,128)(2,1)} %refs_2_.9, bf16[16,512,512]{2,1,0:T(8,128)(2,1)} %collective-permute-done.1.refs_3_, bf16[2048,128]{1,0:T(8,128)(2,1)S(1)} %get-tuple-element.48.refs_4_, ...), custom_call_target="tpu_custom_call" | custom-call | flops 1000 | bytes 1000 | tf_op jit(solution)/shard_map/chip_up/pallas_call | solution.py:275
  20.1 3.4 %chip_here.1.refs_8_ = f32[16,512,128]{2,1,0:T(8,128)S(1)} custom-call(s32[34]{0:T(128)S(1)} %pad_add_fusion.refs_0_.index, s32[34]{0:T(128)S(1)} %collective-permute-done.refs_1_, bf16[16,512,512]{2,1,0:T(8,128)(2,1)} %refs_2_.9, bf16[16,512,512]{2,1,0:T(8,128)(2,1)} %collective-permute-done.1.refs_3_, bf16[2048,128]{1,0:T(8,128)(2,1)S(1)} %get-tuple-element.48.refs_4_, ...), custom_call_target="tpu_custom_call" | custom-call | flops 1000 | bytes 1000 | tf_op jit(solution)/shard_map/chip_here/pallas_call | solution.py:275
  23.5 4.8 %collective-permute-done.3 = bf16[2048,256]{1,0:T(8,128)(2,1)S(1)} collective-permute-done((bf16[2048,256]{1,0:T(8,128)(2,1)}, bf16[2048,256]{1,0:T(8,128)(2,1)S(1)}, u32[]{:S(2)}, u32[]{:S(2)}) %collective-permute-start.3) | collective-permute-done | bytes 1048608 | tf_op jit(solution)/shard_map/ppermute | solution.py:24
  28.3 6.5 %collective-permute-done.2 = bf16[2048,256]{1,0:T(8,128)(2,1)S(1)} collective-permute-done((bf16[2048,256]{1,0:T(8,128)(2,1)}, bf16[2048,256]{1,0:T(8,128)(2,1)S(1)}, u32[]{:S(2)}, u32[]{:S(2)}) %collective-permute-start.2) | collective-permute-done | bytes 1048608 | tf_op jit(solution)/shard_map/ppermute | solution.py:24
  34.9 1.2 %collective-permute-start.8 = (bf16[2048,128]{1,0:T(8,128)(2,1)S(1)}, bf16[2048,128]{1,0:T(8,128)(2,1)S(1)}, u32[]{:S(2)}, u32[]{:S(2)}) collective-permute-start(bf16[2048,128]{1,0:T(8,128)(2,1)S(1)} %get-tuple-element.43), channel_id=1, source_target_pairs={{0,1},{1,0},{2,3},{3,2},{4,5},{5,4},{6,7},{7,6},{8,9},{9,8},{10,11... | collective-permute-start | bytes 1572872 | tf_op jit(solution)/shard_map/ppermute | solution.py:24
  36.0 0.1 collective-permute-start.7
  36.1 0.4 collective-permute-start.5
  36.5 7.5 %collective-permute-start.6 = (bf16[2048,128]{1,0:T(8,128)(2,1)S(1)}, bf16[2048,128]{1,0:T(8,128)(2,1)S(1)}, u32[]{:S(2)}, u32[]{:S(2)}) collective-permute-start(bf16[2048,128]{1,0:T(8,128)(2,1)S(1)} %get-tuple-element.46), channel_id=1, source_target_pairs={{0,255},{1,254},{2,253},{3,252},{4,3},{5,2},{6,1},{7,0},{8,7},{9,6... | collective-permute-start | bytes 1572872 | tf_op jit(solution)/shard_map/ppermute | solution.py:24
  44.0 1.4 %up.1 = (s16[4,528,128]{2,1,0:T(8,128)(2,1)S(1)}, s16[4,528,128]{2,1,0:T(8,128)(2,1)S(1)}, s16[4,528,128]{2,1,0:T(8,128)(2,1)S(1)}, f32[16,512,128]{2,1,0:T(8,128)S(1)}) custom-call(s32[34]{0:T(128)S(1)} %pad_add_fusion.refs_0_.index, s32[34]{0:T(128)S(1)} %collective-permute-done.refs_1_, ...), custom_call_target="tpu_custom_call", output_to_operand_aliasing={{3}: (6, {})} | custom-call | flops 1000 | bytes 1000 | tf_op jit(solution)/shard_map/up/pallas_call | solution.py:275
  45.5 3.1 %collective-permute-start.12 = (s16[4,528,128]{2,1,0:T(8,128)(2,1)S(1)}, s16[4,528,128]{2,1,0:T(8,128)(2,1)S(1)}, u32[]{:S(2)}, u32[]{:S(2)}) collective-permute-start(s16[4,528,128]{2,1,0:T(8,128)(2,1)S(1)} %get-tuple-element.40), channel_id=1, source_target_pairs={{0,2},{1,3},{2,0},{3,1},{4,6},{5,7},{6,4},{7,5},{8,10},{9,11},{10,... | collective-permute-start | bytes 1622024 | tf_op jit(solution)/shard_map/ppermute | solution.py:24
  48.6 2.5 %group.1.refs_6_ = f32[16,512,128]{2,1,0:T(8,128)S(1)} custom-call(s32[34]{0:T(128)S(1)} %pad_add_fusion.refs_0_.index, s32[34]{0:T(128)S(1)} %collective-permute-done.refs_1_, bf16[16,512,512]{2,1,0:T(8,128)(2,1)} %refs_2_.9, bf16[16,512,512]{2,1,0:T(8,128)(2,1)} %collective-permute-done.1.refs_3_, ...), custom_call_target="tpu_custom_call", output_to_operand_aliasing={{}: (8, {})} | custom-call | flops 1000 | bytes 1000 | tf_op jit(solution)/shard_map/group/pallas_call | solution.py:275
  51.1 4.5 %collective-permute-done.6.refs_5_ = bf16[2048,128]{1,0:T(8,128)(2,1)S(1)} collective-permute-done((bf16[2048,128]{1,0:T(8,128)(2,1)S(1)}, bf16[2048,128]{1,0:T(8,128)(2,1)S(1)}, u32[]{:S(2)}, u32[]{:S(2)}) %collective-permute-start.6) | collective-permute-done | bytes 524320 | tf_op jit(solution)/shard_map/ppermute | solution.py:24
  55.6 2.7 %far.1 = (f32[4,512,128]{2,1,0:T(8,128)S(1)}, s16[4,528,128]{2,1,0:T(8,128)(2,1)S(1)}, f32[16,512,128]{2,1,0:T(8,128)S(1)}) custom-call(s32[34]{0:T(128)S(1)} %pad_add_fusion.refs_0_.index, s32[34]{0:T(128)S(1)} %collective-permute-done.refs_1_, bf16[16,512,512]{2,1,0:T(8,128)(2,1)} %refs_2_.9, ...), custom_call_target="tpu_custom_call", output_to_operand_aliasing={{2}: (6, {})} | custom-call | flops 1000 | bytes 1000 | tf_op jit(solution)/shard_map/far/pallas_call | solution.py:275
  58.3 0.7 collective-permute-start.9
  59.0 1.9 %collective-permute-start.10 = (s16[4,528,128]{2,1,0:T(8,128)(2,1)S(1)}, s16[4,528,128]{2,1,0:T(8,128)(2,1)S(1)}, u32[]{:S(2)}, u32[]{:S(2)}) collective-permute-start(s16[4,528,128]{2,1,0:T(8,128)(2,1)S(1)} %get-tuple-element.37), channel_id=1, source_target_pairs={{0,2},{1,3},{2,0},{3,1},{4,6},{5,7},{6,4},{7,5},{8,10},{9,11},{10,... | collective-permute-start | bytes 1622024 | tf_op jit(solution)/shard_map/ppermute | solution.py:24
  60.9 0.6 collective-permute-done.12.refs_1_
  61.5 0.4 add_up.1
  61.9 13.6 %collective-permute-done.11.refs_1_ = s16[4,528,128]{2,1,0:T(8,128)(2,1)S(1)} collective-permute-done((s16[4,528,128]{2,1,0:T(8,128)(2,1)S(1)}, s16[4,528,128]{2,1,0:T(8,128)(2,1)S(1)}, u32[]{:S(2)}, u32[]{:S(2)}) %collective-permute-start.11) | collective-permute-done | bytes 540704 | tf_op jit(solution)/shard_map/ppermute | solution.py:24
  75.5 0.4 add_here.1
  75.9 1.5 %collective-permute-start.13 = (s16[4,528,128]{2,1,0:T(8,128)(2,1)S(1)}, s16[4,528,128]{2,1,0:T(8,128)(2,1)S(1)}, u32[]{:S(2)}, u32[]{:S(2)}) collective-permute-start(s16[4,528,128]{2,1,0:T(8,128)(2,1)S(1)} %add_here.1), channel_id=1, source_target_pairs={{0,3},{1,2},{2,1},{3,0},{4,7},{5,6},{6,5},{7,4},{8,11},{9,10},{10,... | collective-permute-start | bytes 1622024 | tf_op jit(solution)/shard_map/ppermute | solution.py:24
  77.4 10.4 %collective-permute-done.15.below1 = s16[4,528,128]{2,1,0:T(8,128)(2,1)S(1)} collective-permute-done((s16[4,528,128]{2,1,0:T(8,128)(2,1)S(1)}, s16[4,528,128]{2,1,0:T(8,128)(2,1)S(1)}, u32[]{:S(2)}, u32[]{:S(2)}) %collective-permute-start.15) | collective-permute-done | bytes 540704 | tf_op jit(solution)/shard_map/ppermute | solution.py:24
  87.8 2.3 %collective-permute-done.13.pair1 = s16[4,528,128]{2,1,0:T(8,128)(2,1)S(1)} collective-permute-done((s16[4,528,128]{2,1,0:T(8,128)(2,1)S(1)}, s16[4,528,128]{2,1,0:T(8,128)(2,1)S(1)}, u32[]{:S(2)}, u32[]{:S(2)}) %collective-permute-start.13) | collective-permute-done | bytes 540704 | tf_op jit(solution)/shard_map/ppermute | solution.py:24
  90.2 8.5 %collective-permute-done.14.below0 = s16[4,528,128]{2,1,0:T(8,128)(2,1)S(1)} collective-permute-done((s16[4,528,128]{2,1,0:T(8,128)(2,1)S(1)}, s16[4,528,128]{2,1,0:T(8,128)(2,1)S(1)}, u32[]{:S(2)}, u32[]{:S(2)}) %collective-permute-start.14) | collective-permute-done | bytes 540704 | tf_op jit(solution)/shard_map/ppermute | solution.py:24
  98.7 0.3 broadcast_in_dim.10.reflect
  99.0 2.9 %final.1 = f32[2048,256]{1,0:T(8,128)} custom-call(s32[34]{0:T(128)S(1)} %pad_add_fusion.refs_0_.index, f32[16,512,128]{2,1,0:T(8,128)S(1)} %get-tuple-element.35.refs_0_.sums, f32[4,512,128]{2,1,0:T(8,128)S(1)} %collective-permute-done.9.sib, s16[4,528,128]{2,1,0:T(8,128)(2,1)S(1)} %collective-permute-done.10.pair0, ...), custom_call_target="tpu_custom_call" | custom-call | tf_op jit(solution)/shard_map/final/pallas_call | solution.py:359
  (18 shorter events, 0.2 us)
Async XLA Ops:
  0.0 17.4 %collective-permute-start.1 = (bf16[16,512,512]{2,1,0:T(8,128)(2,1)}, bf16[16,512,512]{2,1,0:T(8,128)(2,1)}, u32[]{:S(2)}, u32[]{:S(2)}) collective-permute-start(bf16[16,512,512]{2,1,0:T(8,128)(2,1)} %refs_2_.9), channel_id=1, source_target_pairs={{0,1},{1,0},{2,3},{3,2},{4,5},{5,4},{6,7},{7,6},{8,9},{9,8},{10,11... | collective-permute-start | bytes 25165832 | tf_op jit(solution)/shard_map/ppermute | solution.py:24
  3.2 25.0 %collective-permute-start.3 = (bf16[2048,256]{1,0:T(8,128)(2,1)}, bf16[2048,256]{1,0:T(8,128)(2,1)S(1)}, u32[]{:S(2)}, u32[]{:S(2)}) collective-permute-start(bf16[2048,256]{1,0:T(8,128)(2,1)} %param.7), channel_id=1, source_target_pairs={{0,2},{1,3},{2,0},{3,1},{4,6},{5,7},{6,4},{7,5},{8,10},{9,11},{10,... | collective-permute-start | bytes 3145736 | tf_op jit(solution)/shard_map/ppermute | solution.py:24
  3.2 31.5 %collective-permute-start.2 = (bf16[2048,256]{1,0:T(8,128)(2,1)}, bf16[2048,256]{1,0:T(8,128)(2,1)S(1)}, u32[]{:S(2)}, u32[]{:S(2)}) collective-permute-start(bf16[2048,256]{1,0:T(8,128)(2,1)} %param.7), channel_id=1, source_target_pairs={{0,254},{1,255},{2,252},{3,253},{4,2},{5,3},{6,0},{7,1},{8,6},{9,7... | collective-permute-start | bytes 3145736 | tf_op jit(solution)/shard_map/ppermute | solution.py:24
  14.3 3.1 %collective-permute-start.4 = (bf16[2048,128]{1,0:T(8,128)(2,1)}, bf16[2048,128]{1,0:T(8,128)(2,1)S(1)}, u32[]{:S(2)}, u32[]{:S(2)}) collective-permute-start(bf16[2048,128]{1,0:T(8,128)(2,1)} %get-tuple-element.47), channel_id=1, source_target_pairs={{0,1},{1,0},{2,3},{3,2},{4,5},{5,4},{6,7},{7,6},{8,9},{9,8},{10,11... | collective-permute-start | bytes 1572872 | tf_op jit(solution)/shard_map/ppermute | solution.py:24
  16.2 1.1 %collective-permute-start = (s32[34]{0:T(128)S(1)}, s32[34]{0:T(128)S(1)}, u32[]{:S(2)}, u32[]{:S(2)}) collective-permute-start(s32[34]{0:T(128)S(1)} %pad_add_fusion.refs_0_.index), channel_id=1, source_target_pairs={{0,1},{1,0},{2,3},{3,2},{4,5},{5,4},{6,7},{7,6},{8,9},{9,8},{10,11... | collective-permute-start | bytes 416 | tf_op jit(solution)/shard_map/ppermute | solution.py:24
  34.9 9.2 %collective-permute-start.8 = (bf16[2048,128]{1,0:T(8,128)(2,1)S(1)}, bf16[2048,128]{1,0:T(8,128)(2,1)S(1)}, u32[]{:S(2)}, u32[]{:S(2)}) collective-permute-start(bf16[2048,128]{1,0:T(8,128)(2,1)S(1)} %get-tuple-element.43), channel_id=1, source_target_pairs={{0,1},{1,0},{2,3},{3,2},{4,5},{5,4},{6,7},{7,6},{8,9},{9,8},{10,11... | collective-permute-start | bytes 1572872 | tf_op jit(solution)/shard_map/ppermute | solution.py:24
  36.0 8.0 %collective-permute-start.7 = (bf16[2048,128]{1,0:T(8,128)(2,1)S(1)}, bf16[2048,128]{1,0:T(8,128)(2,1)S(1)}, u32[]{:S(2)}, u32[]{:S(2)}) collective-permute-start(bf16[2048,128]{1,0:T(8,128)(2,1)S(1)} %get-tuple-element.46), channel_id=1, source_target_pairs={{0,1},{1,0},{2,3},{3,2},{4,5},{5,4},{6,7},{7,6},{8,9},{9,8},{10,11... | collective-permute-start | bytes 1572872 | tf_op jit(solution)/shard_map/ppermute | solution.py:24
  36.1 15.0 %collective-permute-start.5 = (bf16[2048,128]{1,0:T(8,128)(2,1)S(1)}, bf16[2048,128]{1,0:T(8,128)(2,1)S(1)}, u32[]{:S(2)}, u32[]{:S(2)}) collective-permute-start(bf16[2048,128]{1,0:T(8,128)(2,1)S(1)} %get-tuple-element.44.refs_6_), channel_id=1, source_target_pairs={{0,2},{1,3},{2,0},{3,1},{4,6},{5,7},{6,4},{7,5},{8,10},{9,11},{10,... | collective-permute-start | bytes 1572872 | tf_op jit(solution)/shard_map/ppermute | solution.py:24
  36.5 19.0 %collective-permute-start.6 = (bf16[2048,128]{1,0:T(8,128)(2,1)S(1)}, bf16[2048,128]{1,0:T(8,128)(2,1)S(1)}, u32[]{:S(2)}, u32[]{:S(2)}) collective-permute-start(bf16[2048,128]{1,0:T(8,128)(2,1)S(1)} %get-tuple-element.46), channel_id=1, source_target_pairs={{0,255},{1,254},{2,253},{3,252},{4,3},{5,2},{6,1},{7,0},{8,7},{9,6... | collective-permute-start | bytes 1572872 | tf_op jit(solution)/shard_map/ppermute | solution.py:24
  45.5 16.0 %collective-permute-start.12 = (s16[4,528,128]{2,1,0:T(8,128)(2,1)S(1)}, s16[4,528,128]{2,1,0:T(8,128)(2,1)S(1)}, u32[]{:S(2)}, u32[]{:S(2)}) collective-permute-start(s16[4,528,128]{2,1,0:T(8,128)(2,1)S(1)} %get-tuple-element.40), channel_id=1, source_target_pairs={{0,2},{1,3},{2,0},{3,1},{4,6},{5,7},{6,4},{7,5},{8,10},{9,11},{10,... | collective-permute-start | bytes 1622024 | tf_op jit(solution)/shard_map/ppermute | solution.py:24
  55.6 19.9 %collective-permute-start.11 = (s16[4,528,128]{2,1,0:T(8,128)(2,1)S(1)}, s16[4,528,128]{2,1,0:T(8,128)(2,1)S(1)}, u32[]{:S(2)}, u32[]{:S(2)}) collective-permute-start(s16[4,528,128]{2,1,0:T(8,128)(2,1)S(1)} %get-tuple-element.38), channel_id=1, source_target_pairs={{0,6},{1,7},{2,4},{3,5},{4,10},{5,11},{6,8},{7,9},{8,14},{9,15},{1... | collective-permute-start | bytes 1622024 | tf_op jit(solution)/shard_map/ppermute | solution.py:24
  58.3 29.5 %collective-permute-start.9 = (f32[4,512,128]{2,1,0:T(8,128)S(1)}, f32[4,512,128]{2,1,0:T(8,128)S(1)}, u32[]{:S(2)}, u32[]{:S(2)}) collective-permute-start(f32[4,512,128]{2,1,0:T(8,128)S(1)} %get-tuple-element.36), channel_id=1, source_target_pairs={{0,1},{1,0},{2,3},{3,2},{4,5},{5,4},{6,7},{7,6},{8,9},{9,8},{10,11... | collective-permute-start | bytes 3145736 | tf_op jit(solution)/shard_map/ppermute | solution.py:24
  59.0 18.4 %collective-permute-start.10 = (s16[4,528,128]{2,1,0:T(8,128)(2,1)S(1)}, s16[4,528,128]{2,1,0:T(8,128)(2,1)S(1)}, u32[]{:S(2)}, u32[]{:S(2)}) collective-permute-start(s16[4,528,128]{2,1,0:T(8,128)(2,1)S(1)} %get-tuple-element.37), channel_id=1, source_target_pairs={{0,2},{1,3},{2,0},{3,1},{4,6},{5,7},{6,4},{7,5},{8,10},{9,11},{10,... | collective-permute-start | bytes 1622024 | tf_op jit(solution)/shard_map/ppermute | solution.py:24
  60.9 26.9 %collective-permute-start.15 = (s16[4,528,128]{2,1,0:T(8,128)(2,1)S(1)}, s16[4,528,128]{2,1,0:T(8,128)(2,1)S(1)}, u32[]{:S(2)}, u32[]{:S(2)}) collective-permute-start(s16[4,528,128]{2,1,0:T(8,128)(2,1)S(1)} %get-tuple-element.42), channel_id=1, source_target_pairs={{0,7},{1,6},{2,5},{3,4},{4,11},{5,10},{6,9},{7,8},{8,15},{9,14},{1... | collective-permute-start | bytes 1622024 | tf_op jit(solution)/shard_map/ppermute | solution.py:24
  61.5 37.2 %copy-start.1 = (f32[2048]{0:T(1024)S(1)}, f32[2048]{0:T(1024)}, u32[]{:S(2)}) copy-start(f32[2048]{0:T(1024)} %param.9) | copy-start | bytes 24580
  61.9 37.1 %copy-start = (bf16[2048,256]{1,0:T(8,128)(2,1)S(1)}, bf16[2048,256]{1,0:T(8,128)(2,1)}, u32[]{:S(2)}) copy-start(bf16[2048,256]{1,0:T(8,128)(2,1)} %source.1) | copy-start | bytes 3145732
  75.9 14.3 %collective-permute-start.13 = (s16[4,528,128]{2,1,0:T(8,128)(2,1)S(1)}, s16[4,528,128]{2,1,0:T(8,128)(2,1)S(1)}, u32[]{:S(2)}, u32[]{:S(2)}) collective-permute-start(s16[4,528,128]{2,1,0:T(8,128)(2,1)S(1)} %add_here.1), channel_id=1, source_target_pairs={{0,3},{1,2},{2,1},{3,0},{4,7},{5,6},{6,5},{7,4},{8,11},{9,10},{10,... | collective-permute-start | bytes 1622024 | tf_op jit(solution)/shard_map/ppermute | solution.py:24
  77.4 21.3 %collective-permute-start.14 = (s16[4,528,128]{2,1,0:T(8,128)(2,1)S(1)}, s16[4,528,128]{2,1,0:T(8,128)(2,1)S(1)}, u32[]{:S(2)}, u32[]{:S(2)}) collective-permute-start(s16[4,528,128]{2,1,0:T(8,128)(2,1)S(1)} %add_up.1), channel_id=1, source_target_pairs={{0,6},{1,7},{2,4},{3,5},{4,10},{5,11},{6,8},{7,9},{8,14},{9,15},{1... | collective-permute-start | bytes 1622024 | tf_op jit(solution)/shard_map/ppermute | solution.py:24

commit v4 on v3

--- a/solution.py
+++ b/solution.py
@@ -193,17 +193,12 @@
 
 def up_kernel(*refs):
     tables, pieces, earlier = refs[:4], refs[4:6], refs[6]
-    far0, far1, near1, sums = refs[7:11]
+    far0, far1, sums = refs[7:10]
     goes_on(earlier, sums)
-    products(to_next(1), None, *tables, pieces, sums, *refs[11:])
-    pb = far0.shape[0]
-
-    def finish(b):
-        store_quantized(far1, b, sums[pb + b])
-        store_quantized(far0, b, sums[b])
-        store_quantized(near1, b, sums[3 * pb + b])
-
-    for_blocks(pb, finish)
+    products(to_next(1), None, *tables, pieces, sums, *refs[10:])
+    n = far0.shape[0]
+    for_blocks(n, lambda b: store_quantized(far0, b, sums[b]))
+    for_blocks(far1.shape[0], lambda b: store_quantized(far1, b, sums[n + b]))
 
 
 def group_kernel(*refs):
@@ -222,32 +217,56 @@
 
     def finish(b):
         store_quantized(other0, b, sums[2 * pb + b])
-        own1[b] = sums[pb + b]
+        store_quantized(own1, b, sums[pb + b])
 
     for_blocks(pb, finish)
 
 
-def add_kernel(first, sums, arrived, out):
-    blk = sums.shape[1]
+def add_up_kernel(sums, arrived, out0, out1):
+    pb, blk = out0.shape[0], sums.shape[1]
+    for_blocks(
+        pb, lambda b: store_quantized(out0, b, sums[2 * pb + b] + load_quantized(arrived, b, blk))
+    )
+    for_blocks(pb - 1, lambda b: store_quantized(out1, 1 + b, sums[3 * pb + 1 + b]))
+    store_quantized(out1, 0, sums[3 * pb] + load_quantized(arrived, pb, blk))
+
+
+def add_here_kernel(sums, arrived, out):
+    pb, blk = out.shape[0], sums.shape[1]
 
     def step(b):
-        store_quantized(out, b, sums[first + b] + load_quantized(arrived, b, blk))
-
-    for_blocks(out.shape[0], step)
-
-
-def final_kernel(index, sums, sib, pair0, pair1, below0, below1, source, reflect, out):
-    blk, half = sums.shape[1:]
+        store_quantized(out, 1 + b, sums[3 * pb + 1 + b] + load_quantized(arrived, b, blk))
+
+    for_blocks(pb - 1, step)
+    store_quantized(out, 0, sums[3 * pb])
+
+
+def ready_kernel(index, sums, sib, here0, below1, source, reflect, mine, other):
+    pb, blk, half = mine.shape
+    first = index[index.shape[0] - 1] % 2 == 0
+
+    def step(b):
+        rows = pl.ds(pl.multiple_of(b * blk, blk), blk)
+        factor = reflect[rows, :]
+        left = source[rows, :half].astype(jnp.float32)
+        right = source[rows, half:].astype(jnp.float32)
+        add = factor * (sums[b] + load_quantized(here0, b, blk))
+        mine[b] = jnp.where(first, left, right) + add
+        add = factor * (load_quantized(sib, b, blk) + load_quantized(below1, b, blk))
+        other[b] = jnp.where(first, right, left) + add
+
+    for_blocks(pb, step)
+
+
+def final_kernel(index, mine, other, below0, here1, reflect, out):
+    blk, half = mine.shape[1:]
     b = pl.program_id(0)
-    mine = sums[b] + load_quantized(pair0, b, blk) + load_quantized(below0, b, blk)
-    other = sib[b] + load_quantized(pair1, b, blk) + load_quantized(below1, b, blk)
     first = index[index.shape[0] - 1] % 2 == 0
-    rows = pl.ds(pl.multiple_of(b * blk, blk), blk)
-    factor = reflect[rows, :]
-    left = jnp.where(first, mine, other)
-    right = jnp.where(first, other, mine)
-    out[:, :half] = source[rows, :half].astype(jnp.float32) + factor * left
-    out[:, half:] = source[rows, half:].astype(jnp.float32) + factor * right
+    factor = reflect[pl.ds(pl.multiple_of(b * blk, blk), blk), :]
+    a = mine[b] + factor * load_quantized(below0, b, blk)
+    c = other[b] + factor * load_quantized(here1, b, blk)
+    out[:, :half] = jnp.where(first, a, c)
+    out[:, half:] = jnp.where(first, c, a)
 
 
 def in_vmem(x):
@@ -330,32 +349,34 @@
     far0 = send(near0, across)
 
     up, near1 = lax.optimization_barrier((up, near1))
-    far_q0, far_q1, near_q1, up = call(
-        up_kernel, "up", tables + [pair0, pair1, up], [sent, sent, sent, group], {6: 3}, scratch
+    more, fewer = (((pb + n, *sent[0][1:]), sent[1]) for n in (1, -1))
+    far_q0, far_q1, up = call(
+        up_kernel, "up", tables + [pair0, pair1, up], [more, fewer, group], {6: 2}, scratch
     )
     part0 = send(far_q0, across)
 
     (here,) = call(
         group_kernel, "group", tables + [pair0, pair1, near0, near1, here], [group], {8: 0}, scratch
     )
-    far0, far1, here, far_q1, near_q1 = lax.optimization_barrier(
-        (far0, far1, here, far_q1, near_q1)
-    )
+    far0, far1, here, far_q1 = lax.optimization_barrier((far0, far1, here, far_q1))
     part1 = send(far_q1, lambda r, h, k: (r + 1, 1 - h, k))
-    below1 = send(near_q1, lambda r, h, k: (r + 1, 1 - h, 1 - k))
-    own_f1, other_q0, here = call(
-        far_kernel, "far", tables + [far0, far1, here], [sums, sent, group], {6: 2}, scratch
+    own_q1, other_q0, here = call(
+        far_kernel, "far", tables + [far0, far1, here], [sent, sent, group], {6: 2}, scratch
     )
     here0 = send(other_q0, lambda r, h, k: (r, 1 - h, k))
-    here_sib = send(own_f1, lambda r, h, k: (r, h, 1 - k))
-    (below0,) = call(lambda *refs: add_kernel(2 * pb, *refs), "add_up", [up, part0], [sent])
-    part1, _ = lax.optimization_barrier((part1, below0))
-    (here1,) = call(lambda *refs: add_kernel(3 * pb, *refs), "add_here", [here, part1], [sent])
+    here_sib = send(own_q1, lambda r, h, k: (r, h, 1 - k))
+    (here1,) = call(add_here_kernel, "add_here", [here, part1], [sent])
+    part0, _ = lax.optimization_barrier((part0, here1))
+    below0, below1 = call(add_up_kernel, "add_up", [up, part0], [sent, sent])
+    below1 = send(below1, lambda r, h, k: (r + 1, 1 - h, 1 - k))
     below0 = send(below0, lambda r, h, k: (r + 1, 1 - h, k))
     here1 = send(here1, lambda r, h, k: (r, 1 - h, 1 - k))
 
     factor = jnp.broadcast_to(reflect[:, None], (piece_rows, half))
-    args = [here, here_sib, here0, here1, below0, below1, source, factor]
+    ready = call(
+        ready_kernel, "ready", [index, here, here_sib, here0, below1, source, factor], [sums, sums]
+    )
+    args = [*ready, below0, here1, factor]
     return pl.pallas_call(
         final_kernel,
         grid=(pb,),

time: 102 us -> 109 us (1.069)
  Pallas kernels: 16.4 us -> 27.1 us
  waiting for transfers between devices: 52.3 us -> 43.7 us
  starting transfers between devices: 29.1 us -> 33.6 us
    pallas_call x7 -> x8, Pallas kernels: 13.5 us -> 24.6 us  [call(): pl.pallas_call(kernel, in_specs=specs, out_specs=[pl.BlockSpec(memory_spa...]
    ppermute x16, waiting for transfers between devices: 52.3 us -> 43.7 us  [send(): return lax.ppermute(x, AXES, pairs)]
    ppermute x16, starting transfers between devices: 29.1 us -> 33.6 us  [send(): return lax.ppermute(x, AXES, pairs)]
  transfers between devices with their start and end apart: 16 -> 16, of which waited for: 9 -> 7; matrix products, arithmetic and copies ran while one was open for 3% -> 3% of each run, Pallas kernels for 13% -> 23%
where the time goes in v4:
time: 109 us; the launch traced here: 108 us
  waiting for transfers between devices  43.7 us (40%)
  starting transfers between devices  33.6 us (31%)
  Pallas kernels  27.1 us (25%)
  other arithmetic  2.96 us (3%)
    ppermute x16, waiting for transfers between devices, send(): return lax.ppermute(x, AXES, pairs)  43.7 us
    ppermute x16, starting transfers between devices, send(): return lax.ppermute(x, AXES, pairs)  33.6 us
    pallas_call x8, Pallas kernels, call(): pl.pallas_call(kernel, in_specs=specs, out_specs=[pl.BlockSpec(memory_spa...  24.6 us
    pallas_call x1, Pallas kernels, per_device(): pl.pallas_call(final_kernel, grid=(pb,), in_specs=[pl.BlockSpec(memory_sp...  2.55 us
    select_n x3, other arithmetic, split_columns(): return (jnp.where(first, left, right), jnp.where(first, right, left))  2.21 us
  transfers between devices with their start and end apart: 16, of which 7 were waited for; matrix products, arithmetic and copies ran while one was open for 3% of the time, Pallas kernels for 23%

profile of v4, /device:TPU:1, one launch (start us, length us, event | category | flops | bytes accessed | tf_op | source)
XLA Modules:
  0.0 108.5 jit_solution(17333319881576334829)
XLA Ops:
  0.0 3.2 %collective-permute-start.1 = (bf16[16,512,512]{2,1,0:T(8,128)(2,1)}, bf16[16,512,512]{2,1,0:T(8,128)(2,1)}, u32[]{:S(2)}, u32[]{:S(2)}) collective-permute-start(bf16[16,512,512]{2,1,0:T(8,128)(2,1)} %refs_2_.9), channel_id=1, source_target_pairs={{0,1},{1,0},{2,3},{3,2},{4,5},{5,4},{6,7},{7,6},{8,9},{9,8},{10,11... | collective-permute-start | bytes 25165832 | tf_op jit(solution)/shard_map/ppermute | solution.py:24
  3.2 8.9 %collective-permute-start.2 = (bf16[2048,256]{1,0:T(8,128)(2,1)}, bf16[2048,256]{1,0:T(8,128)(2,1)S(1)}, u32[]{:S(2)}, u32[]{:S(2)}) collective-permute-start(bf16[2048,256]{1,0:T(8,128)(2,1)} %param.7), channel_id=1, source_target_pairs={{0,254},{1,255},{2,252},{3,253},{4,2},{5,3},{6,0},{7,1},{8,6},{9,7... | collective-permute-start | bytes 3145736 | tf_op jit(solution)/shard_map/ppermute | solution.py:24
  12.2 2.1 %broadcast_select_fusion.4 = (bf16[2048,128]{1,0:T(8,128)(2,1)}, bf16[2048,128]{1,0:T(8,128)(2,1)S(1)}) fusion(pred[]{:T(512)S(6)} %eq.4, bf16[2048,256]{1,0:T(8,128)(2,1)} %param.7), kind=kLoop, calls=%fused_computation.4 | loop fusion | flops 524288 | bytes 2097153 | tf_op jit(solution)/shard_map/jit(_where)/select_n | solution.py:52
  14.3 0.6 collective-permute-start.4
  15.5 0.7 subtract_bitcast_fusion
  16.3 1.1 %collective-permute-done.refs_1_ = s32[34]{0:T(128)S(1)} collective-permute-done((s32[34]{0:T(128)S(1)}, s32[34]{0:T(128)S(1)}, u32[]{:S(2)}, u32[]{:S(2)}) %collective-permute-start) | collective-permute-done | bytes 168 | tf_op jit(solution)/shard_map/ppermute | solution.py:24
  17.4 3.6 %chip_up.1.refs_6_ = f32[16,512,128]{2,1,0:T(8,128)S(1)} custom-call(s32[34]{0:T(128)S(1)} %pad_add_fusion.refs_0_.index, s32[34]{0:T(128)S(1)} %collective-permute-done.refs_1_, bf16[16,512,512]{2,1,0:T(8,128)(2,1)} %refs_2_.9, bf16[16,512,512]{2,1,0:T(8,128)(2,1)} %collective-permute-done.1.refs_3_, bf16[2048,128]{1,0:T(8,128)(2,1)S(1)} %get-tuple-element.52.refs_4_, ...), custom_call_target="tpu_custom_call" | custom-call | flops 1000 | bytes 1000 | tf_op jit(solution)/shard_map/chip_up/pallas_call | solution.py:294
  20.9 4.5 %chip_here.1.refs_8_ = f32[16,512,128]{2,1,0:T(8,128)S(1)} custom-call(s32[34]{0:T(128)S(1)} %pad_add_fusion.refs_0_.index, s32[34]{0:T(128)S(1)} %collective-permute-done.refs_1_, bf16[16,512,512]{2,1,0:T(8,128)(2,1)} %refs_2_.9, bf16[16,512,512]{2,1,0:T(8,128)(2,1)} %collective-permute-done.1.refs_3_, bf16[2048,128]{1,0:T(8,128)(2,1)S(1)} %get-tuple-element.52.refs_4_, ...), custom_call_target="tpu_custom_call" | custom-call | flops 1000 | bytes 1000 | tf_op jit(solution)/shard_map/chip_here/pallas_call | solution.py:294
  25.4 2.8 %collective-permute-done.3 = bf16[2048,256]{1,0:T(8,128)(2,1)S(1)} collective-permute-done((bf16[2048,256]{1,0:T(8,128)(2,1)}, bf16[2048,256]{1,0:T(8,128)(2,1)S(1)}, u32[]{:S(2)}, u32[]{:S(2)}) %collective-permute-start.3) | collective-permute-done | bytes 1048608 | tf_op jit(solution)/shard_map/ppermute | solution.py:24
  28.3 6.5 %collective-permute-done.2 = bf16[2048,256]{1,0:T(8,128)(2,1)S(1)} collective-permute-done((bf16[2048,256]{1,0:T(8,128)(2,1)}, bf16[2048,256]{1,0:T(8,128)(2,1)S(1)}, u32[]{:S(2)}, u32[]{:S(2)}) %collective-permute-start.2) | collective-permute-done | bytes 1048608 | tf_op jit(solution)/shard_map/ppermute | solution.py:24
  34.9 1.2 %collective-permute-start.8 = (bf16[2048,128]{1,0:T(8,128)(2,1)S(1)}, bf16[2048,128]{1,0:T(8,128)(2,1)S(1)}, u32[]{:S(2)}, u32[]{:S(2)}) collective-permute-start(bf16[2048,128]{1,0:T(8,128)(2,1)S(1)} %get-tuple-element.47), channel_id=1, source_target_pairs={{0,1},{1,0},{2,3},{3,2},{4,5},{5,4},{6,7},{7,6},{8,9},{9,8},{10,11... | collective-permute-start | bytes 1572872 | tf_op jit(solution)/shard_map/ppermute | solution.py:24
  36.0 0.1 collective-permute-start.7
  36.1 0.4 collective-permute-start.5
  36.5 7.5 %collective-permute-start.6 = (bf16[2048,128]{1,0:T(8,128)(2,1)S(1)}, bf16[2048,128]{1,0:T(8,128)(2,1)S(1)}, u32[]{:S(2)}, u32[]{:S(2)}) collective-permute-start(bf16[2048,128]{1,0:T(8,128)(2,1)S(1)} %get-tuple-element.50), channel_id=1, source_target_pairs={{0,255},{1,254},{2,253},{3,252},{4,3},{5,2},{6,1},{7,0},{8,7},{9,6... | collective-permute-start | bytes 1572872 | tf_op jit(solution)/shard_map/ppermute | solution.py:24
  44.0 4.5 %up.1 = (s16[5,528,128]{2,1,0:T(8,128)(2,1)S(1)}, s16[3,528,128]{2,1,0:T(8,128)(2,1)S(1)}, f32[16,512,128]{2,1,0:T(8,128)S(1)}) custom-call(s32[34]{0:T(128)S(1)} %pad_add_fusion.refs_0_.index, s32[34]{0:T(128)S(1)} %collective-permute-done.refs_1_, bf16[16,512,512]{2,1,0:T(8,128)(2,1)} %refs_2_.9, ...), custom_call_target="tpu_custom_call", output_to_operand_aliasing={{2}: (6, {})} | custom-call | flops 1000 | bytes 1000 | tf_op jit(solution)/shard_map/up/pallas_call | solution.py:294
  48.5 2.7 %collective-permute-start.11 = (s16[5,528,128]{2,1,0:T(8,128)(2,1)S(1)}, s16[5,528,128]{2,1,0:T(8,128)(2,1)S(1)}, u32[]{:S(2)}, u32[]{:S(2)}) collective-permute-start(s16[5,528,128]{2,1,0:T(8,128)(2,1)S(1)} %get-tuple-element.40), channel_id=1, source_target_pairs={{0,2},{1,3},{2,0},{3,1},{4,6},{5,7},{6,4},{7,5},{8,10},{9,11},{10,... | collective-permute-start | bytes 2027528 | tf_op jit(solution)/shard_map/ppermute | solution.py:24
  51.2 5.5 %group.1.refs_6_ = f32[16,512,128]{2,1,0:T(8,128)S(1)} custom-call(s32[34]{0:T(128)S(1)} %pad_add_fusion.refs_0_.index, s32[34]{0:T(128)S(1)} %collective-permute-done.refs_1_, bf16[16,512,512]{2,1,0:T(8,128)(2,1)} %refs_2_.9, bf16[16,512,512]{2,1,0:T(8,128)(2,1)} %collective-permute-done.1.refs_3_, ...), custom_call_target="tpu_custom_call", output_to_operand_aliasing={{}: (8, {})} | custom-call | flops 1000 | bytes 1000 | tf_op jit(solution)/shard_map/group/pallas_call | solution.py:294
  56.7 0.1 collective-permute-start.12
  56.8 4.2 %far.1 = (s16[4,528,128]{2,1,0:T(8,128)(2,1)S(1)}, s16[4,528,128]{2,1,0:T(8,128)(2,1)S(1)}, f32[16,512,128]{2,1,0:T(8,128)S(1)}) custom-call(s32[34]{0:T(128)S(1)} %pad_add_fusion.refs_0_.index, s32[34]{0:T(128)S(1)} %collective-permute-done.refs_1_, bf16[16,512,512]{2,1,0:T(8,128)(2,1)} %refs_2_.9, ...), custom_call_target="tpu_custom_call", output_to_operand_aliasing={{2}: (6, {})} | custom-call | flops 1000 | bytes 1000 | tf_op jit(solution)/shard_map/far/pallas_call | solution.py:294
  61.0 0.2 collective-permute-start.9
  61.2 4.8 %collective-permute-start.10 = (s16[4,528,128]{2,1,0:T(8,128)(2,1)S(1)}, s16[4,528,128]{2,1,0:T(8,128)(2,1)S(1)}, u32[]{:S(2)}, u32[]{:S(2)}) collective-permute-start(s16[4,528,128]{2,1,0:T(8,128)(2,1)S(1)} %get-tuple-element.38), channel_id=1, source_target_pairs={{0,2},{1,3},{2,0},{3,1},{4,6},{5,7},{6,4},{7,5},{8,10},{9,11},{10,... | collective-permute-start | bytes 1622024 | tf_op jit(solution)/shard_map/ppermute | solution.py:24
  66.0 7.1 %collective-permute-done.12.arrived = s16[3,528,128]{2,1,0:T(8,128)(2,1)S(1)} collective-permute-done((s16[3,528,128]{2,1,0:T(8,128)(2,1)S(1)}, s16[3,528,128]{2,1,0:T(8,128)(2,1)S(1)}, u32[]{:S(2)}, u32[]{:S(2)}) %collective-permute-start.12) | collective-permute-done | bytes 405536 | tf_op jit(solution)/shard_map/ppermute | solution.py:24
  73.1 0.4 add_here.1
  73.5 0.7 add_up.1
  74.2 0.1 collective-permute-start.13
  74.3 3.7 %collective-permute-start.15 = (s16[4,528,128]{2,1,0:T(8,128)(2,1)S(1)}, s16[4,528,128]{2,1,0:T(8,128)(2,1)S(1)}, u32[]{:S(2)}, u32[]{:S(2)}) collective-permute-start(s16[4,528,128]{2,1,0:T(8,128)(2,1)S(1)} %add_here.1), channel_id=1, source_target_pairs={{0,3},{1,2},{2,1},{3,0},{4,7},{5,6},{6,5},{7,4},{8,11},{9,10},{10,... | collective-permute-start | bytes 1622024 | tf_op jit(solution)/shard_map/ppermute | solution.py:24
  78.0 0.3 collective-permute-done.10.here0
  78.3 16.0 %collective-permute-done.13.below1 = s16[4,528,128]{2,1,0:T(8,128)(2,1)S(1)} collective-permute-done((s16[4,528,128]{2,1,0:T(8,128)(2,1)S(1)}, s16[4,528,128]{2,1,0:T(8,128)(2,1)S(1)}, u32[]{:S(2)}, u32[]{:S(2)}) %collective-permute-start.13) | collective-permute-done | bytes 540704 | tf_op jit(solution)/shard_map/ppermute | solution.py:24
  94.3 0.3 broadcast_in_dim.10.reflect
  94.7 1.3 %ready.1 = (f32[4,512,128]{2,1,0:T(8,128)S(1)}, f32[4,512,128]{2,1,0:T(8,128)S(1)}) custom-call(s32[34]{0:T(128)S(1)} %pad_add_fusion.refs_0_.index, f32[16,512,128]{2,1,0:T(8,128)S(1)} %get-tuple-element.36.sums, s16[4,528,128]{2,1,0:T(8,128)(2,1)S(1)} %collective-permute-done.9.sib, s16[4,528,128]{2,1,0:T(8,128)(2,1)S(1)} %collective-permute-done.10.here0, ...), custom_call_target="tpu_custom_call" | custom-call | flops 1000 | bytes 1000 | tf_op jit(solution)/shard_map/ready/pallas_call | solution.py:294
  96.0 9.9 %collective-permute-done.14.below0 = s16[4,528,128]{2,1,0:T(8,128)(2,1)S(1)} collective-permute-done((s16[4,528,128]{2,1,0:T(8,128)(2,1)S(1)}, s16[4,528,128]{2,1,0:T(8,128)(2,1)S(1)}, u32[]{:S(2)}, u32[]{:S(2)}) %collective-permute-start.14) | collective-permute-done | bytes 540704 | tf_op jit(solution)/shard_map/ppermute | solution.py:24
  105.9 2.5 %final.1 = f32[2048,256]{1,0:T(8,128)} custom-call(s32[34]{0:T(128)S(1)} %pad_add_fusion.refs_0_.index, f32[4,512,128]{2,1,0:T(8,128)S(1)} %get-tuple-element.44.mine, f32[4,512,128]{2,1,0:T(8,128)S(1)} %get-tuple-element.45.other, s16[4,528,128]{2,1,0:T(8,128)(2,1)S(1)} %collective-permute-done.14.below0, ...), custom_call_target="tpu_custom_call" | custom-call | tf_op jit(solution)/shard_map/final/pallas_call | solution.py:380
  (19 shorter events, 0.3 us)
Async XLA Ops:
  0.0 17.4 %collective-permute-start.1 = (bf16[16,512,512]{2,1,0:T(8,128)(2,1)}, bf16[16,512,512]{2,1,0:T(8,128)(2,1)}, u32[]{:S(2)}, u32[]{:S(2)}) collective-permute-start(bf16[16,512,512]{2,1,0:T(8,128)(2,1)} %refs_2_.9), channel_id=1, source_target_pairs={{0,1},{1,0},{2,3},{3,2},{4,5},{5,4},{6,7},{7,6},{8,9},{9,8},{10,11... | collective-permute-start | bytes 25165832 | tf_op jit(solution)/shard_map/ppermute | solution.py:24
  3.2 25.0 %collective-permute-start.3 = (bf16[2048,256]{1,0:T(8,128)(2,1)}, bf16[2048,256]{1,0:T(8,128)(2,1)S(1)}, u32[]{:S(2)}, u32[]{:S(2)}) collective-permute-start(bf16[2048,256]{1,0:T(8,128)(2,1)} %param.7), channel_id=1, source_target_pairs={{0,2},{1,3},{2,0},{3,1},{4,6},{5,7},{6,4},{7,5},{8,10},{9,11},{10,... | collective-permute-start | bytes 3145736 | tf_op jit(solution)/shard_map/ppermute | solution.py:24
  3.2 31.5 %collective-permute-start.2 = (bf16[2048,256]{1,0:T(8,128)(2,1)}, bf16[2048,256]{1,0:T(8,128)(2,1)S(1)}, u32[]{:S(2)}, u32[]{:S(2)}) collective-permute-start(bf16[2048,256]{1,0:T(8,128)(2,1)} %param.7), channel_id=1, source_target_pairs={{0,254},{1,255},{2,252},{3,253},{4,2},{5,3},{6,0},{7,1},{8,6},{9,7... | collective-permute-start | bytes 3145736 | tf_op jit(solution)/shard_map/ppermute | solution.py:24
  14.3 3.1 %collective-permute-start.4 = (bf16[2048,128]{1,0:T(8,128)(2,1)}, bf16[2048,128]{1,0:T(8,128)(2,1)S(1)}, u32[]{:S(2)}, u32[]{:S(2)}) collective-permute-start(bf16[2048,128]{1,0:T(8,128)(2,1)} %get-tuple-element.51), channel_id=1, source_target_pairs={{0,1},{1,0},{2,3},{3,2},{4,5},{5,4},{6,7},{7,6},{8,9},{9,8},{10,11... | collective-permute-start | bytes 1572872 | tf_op jit(solution)/shard_map/ppermute | solution.py:24
  16.2 1.1 %collective-permute-start = (s32[34]{0:T(128)S(1)}, s32[34]{0:T(128)S(1)}, u32[]{:S(2)}, u32[]{:S(2)}) collective-permute-start(s32[34]{0:T(128)S(1)} %pad_add_fusion.refs_0_.index), channel_id=1, source_target_pairs={{0,1},{1,0},{2,3},{3,2},{4,5},{5,4},{6,7},{7,6},{8,9},{9,8},{10,11... | collective-permute-start | bytes 416 | tf_op jit(solution)/shard_map/ppermute | solution.py:24
  34.9 9.2 %collective-permute-start.8 = (bf16[2048,128]{1,0:T(8,128)(2,1)S(1)}, bf16[2048,128]{1,0:T(8,128)(2,1)S(1)}, u32[]{:S(2)}, u32[]{:S(2)}) collective-permute-start(bf16[2048,128]{1,0:T(8,128)(2,1)S(1)} %get-tuple-element.47), channel_id=1, source_target_pairs={{0,1},{1,0},{2,3},{3,2},{4,5},{5,4},{6,7},{7,6},{8,9},{9,8},{10,11... | collective-permute-start | bytes 1572872 | tf_op jit(solution)/shard_map/ppermute | solution.py:24
  36.0 8.0 %collective-permute-start.7 = (bf16[2048,128]{1,0:T(8,128)(2,1)S(1)}, bf16[2048,128]{1,0:T(8,128)(2,1)S(1)}, u32[]{:S(2)}, u32[]{:S(2)}) collective-permute-start(bf16[2048,128]{1,0:T(8,128)(2,1)S(1)} %get-tuple-element.50), channel_id=1, source_target_pairs={{0,1},{1,0},{2,3},{3,2},{4,5},{5,4},{6,7},{7,6},{8,9},{9,8},{10,11... | collective-permute-start | bytes 1572872 | tf_op jit(solution)/shard_map/ppermute | solution.py:24
  36.1 20.6 %collective-permute-start.5 = (bf16[2048,128]{1,0:T(8,128)(2,1)S(1)}, bf16[2048,128]{1,0:T(8,128)(2,1)S(1)}, u32[]{:S(2)}, u32[]{:S(2)}) collective-permute-start(bf16[2048,128]{1,0:T(8,128)(2,1)S(1)} %get-tuple-element.48.refs_6_), channel_id=1, source_target_pairs={{0,2},{1,3},{2,0},{3,1},{4,6},{5,7},{6,4},{7,5},{8,10},{9,11},{10,... | collective-permute-start | bytes 1572872 | tf_op jit(solution)/shard_map/ppermute | solution.py:24
  36.5 20.2 %collective-permute-start.6 = (bf16[2048,128]{1,0:T(8,128)(2,1)S(1)}, bf16[2048,128]{1,0:T(8,128)(2,1)S(1)}, u32[]{:S(2)}, u32[]{:S(2)}) collective-permute-start(bf16[2048,128]{1,0:T(8,128)(2,1)S(1)} %get-tuple-element.50), channel_id=1, source_target_pairs={{0,255},{1,254},{2,253},{3,252},{4,3},{5,2},{6,1},{7,0},{8,7},{9,6... | collective-permute-start | bytes 1572872 | tf_op jit(solution)/shard_map/ppermute | solution.py:24
  48.5 25.0 %collective-permute-start.11 = (s16[5,528,128]{2,1,0:T(8,128)(2,1)S(1)}, s16[5,528,128]{2,1,0:T(8,128)(2,1)S(1)}, u32[]{:S(2)}, u32[]{:S(2)}) collective-permute-start(s16[5,528,128]{2,1,0:T(8,128)(2,1)S(1)} %get-tuple-element.40), channel_id=1, source_target_pairs={{0,2},{1,3},{2,0},{3,1},{4,6},{5,7},{6,4},{7,5},{8,10},{9,11},{10,... | collective-permute-start | bytes 2027528 | tf_op jit(solution)/shard_map/ppermute | solution.py:24
  56.7 16.4 %collective-permute-start.12 = (s16[3,528,128]{2,1,0:T(8,128)(2,1)S(1)}, s16[3,528,128]{2,1,0:T(8,128)(2,1)S(1)}, u32[]{:S(2)}, u32[]{:S(2)}) collective-permute-start(s16[3,528,128]{2,1,0:T(8,128)(2,1)S(1)} %get-tuple-element.41), channel_id=1, source_target_pairs={{0,6},{1,7},{2,4},{3,5},{4,10},{5,11},{6,8},{7,9},{8,14},{9,15},{1... | collective-permute-start | bytes 1216520 | tf_op jit(solution)/shard_map/ppermute | solution.py:24
  61.0 17.0 %collective-permute-start.9 = (s16[4,528,128]{2,1,0:T(8,128)(2,1)S(1)}, s16[4,528,128]{2,1,0:T(8,128)(2,1)S(1)}, u32[]{:S(2)}, u32[]{:S(2)}) collective-permute-start(s16[4,528,128]{2,1,0:T(8,128)(2,1)S(1)} %get-tuple-element.37), channel_id=1, source_target_pairs={{0,1},{1,0},{2,3},{3,2},{4,5},{5,4},{6,7},{7,6},{8,9},{9,8},{10,11... | collective-permute-start | bytes 1622024 | tf_op jit(solution)/shard_map/ppermute | solution.py:24
  61.2 17.1 %collective-permute-start.10 = (s16[4,528,128]{2,1,0:T(8,128)(2,1)S(1)}, s16[4,528,128]{2,1,0:T(8,128)(2,1)S(1)}, u32[]{:S(2)}, u32[]{:S(2)}) collective-permute-start(s16[4,528,128]{2,1,0:T(8,128)(2,1)S(1)} %get-tuple-element.38), channel_id=1, source_target_pairs={{0,2},{1,3},{2,0},{3,1},{4,6},{5,7},{6,4},{7,5},{8,10},{9,11},{10,... | collective-permute-start | bytes 1622024 | tf_op jit(solution)/shard_map/ppermute | solution.py:24
  73.1 21.2 %copy-start.1 = (f32[2048]{0:T(1024)S(1)}, f32[2048]{0:T(1024)}, u32[]{:S(2)}) copy-start(f32[2048]{0:T(1024)} %param.9) | copy-start | bytes 24580
  73.5 21.2 %copy-start = (bf16[2048,256]{1,0:T(8,128)(2,1)S(1)}, bf16[2048,256]{1,0:T(8,128)(2,1)}, u32[]{:S(2)}) copy-start(bf16[2048,256]{1,0:T(8,128)(2,1)} %source.1) | copy-start | bytes 3145732
  74.2 20.1 %collective-permute-start.13 = (s16[4,528,128]{2,1,0:T(8,128)(2,1)S(1)}, s16[4,528,128]{2,1,0:T(8,128)(2,1)S(1)}, u32[]{:S(2)}, u32[]{:S(2)}) collective-permute-start(s16[4,528,128]{2,1,0:T(8,128)(2,1)S(1)} %get-tuple-element.43), channel_id=1, source_target_pairs={{0,7},{1,6},{2,5},{3,4},{4,11},{5,10},{6,9},{7,8},{8,15},{9,14},{1... | collective-permute-start | bytes 1622024 | tf_op jit(solution)/shard_map/ppermute | solution.py:24
  74.3 21.7 %collective-permute-start.15 = (s16[4,528,128]{2,1,0:T(8,128)(2,1)S(1)}, s16[4,528,128]{2,1,0:T(8,128)(2,1)S(1)}, u32[]{:S(2)}, u32[]{:S(2)}) collective-permute-start(s16[4,528,128]{2,1,0:T(8,128)(2,1)S(1)} %add_here.1), channel_id=1, source_target_pairs={{0,3},{1,2},{2,1},{3,0},{4,7},{5,6},{6,5},{7,4},{8,11},{9,10},{10,... | collective-permute-start | bytes 1622024 | tf_op jit(solution)/shard_map/ppermute | solution.py:24
  78.0 27.9 %collective-permute-start.14 = (s16[4,528,128]{2,1,0:T(8,128)(2,1)S(1)}, s16[4,528,128]{2,1,0:T(8,128)(2,1)S(1)}, u32[]{:S(2)}, u32[]{:S(2)}) collective-permute-start(s16[4,528,128]{2,1,0:T(8,128)(2,1)S(1)} %get-tuple-element.46), channel_id=1, source_target_pairs={{0,6},{1,7},{2,4},{3,5},{4,10},{5,11},{6,8},{7,9},{8,14},{9,15},{1... | collective-permute-start | bytes 1622024 | tf_op jit(solution)/shard_map/ppermute | solution.py:24

commit v5 on v3

--- a/solution.py
+++ b/solution.py
@@ -14,13 +14,14 @@
 PARAMS = pltpu.CompilerParams(vmem_limit_bytes=12 * 1024 * 1024)
 
 
-def send(x, route):
+def send(x, route, wrap=True):
     groups, cols = lax.axis_size("row"), lax.axis_size("col")
     pairs = []
     for r in range(groups):
         for c in range(cols):
             to_r, to_h, to_k = route(r, c // 2, c % 2)
-            pairs.append((r * cols + c, to_r % groups * cols + to_h * 2 + to_k))
+            if wrap or 0 <= to_r < groups:
+                pairs.append((r * cols + c, to_r % groups * cols + to_h * 2 + to_k))
     return lax.ppermute(x, AXES, pairs)
 
 
@@ -222,7 +223,7 @@
 
     def finish(b):
         store_quantized(other0, b, sums[2 * pb + b])
-        own1[b] = sums[pb + b]
+        store_quantized(own1, b, sums[pb + b])
 
     for_blocks(pb, finish)
 
@@ -236,18 +237,32 @@
     for_blocks(out.shape[0], step)
 
 
-def final_kernel(index, sums, sib, pair0, pair1, below0, below1, source, reflect, out):
-    blk, half = sums.shape[1:]
+def ready_kernel(index, sums, sib, here0, below1, source, reflect, mine, other):
+    pb, blk, half = mine.shape
+    first = index[index.shape[0] - 1] % 2 == 0
+
+    def step(b):
+        rows = pl.ds(pl.multiple_of(b * blk, blk), blk)
+        factor = reflect[rows, :]
+        left = source[rows, :half].astype(jnp.float32)
+        right = source[rows, half:].astype(jnp.float32)
+        add = factor * (sums[b] + load_quantized(here0, b, blk))
+        mine[b] = jnp.where(first, left, right) + add
+        add = factor * (load_quantized(sib, b, blk) + load_quantized(below1, b, blk))
+        other[b] = jnp.where(first, right, left) + add
+
+    for_blocks(pb, step)
+
+
+def final_kernel(index, mine, other, below0, here1, reflect, out):
+    blk, half = mine.shape[1:]
     b = pl.program_id(0)
-    mine = sums[b] + load_quantized(pair0, b, blk) + load_quantized(below0, b, blk)
-    other = sib[b] + load_quantized(pair1, b, blk) + load_quantized(below1, b, blk)
     first = index[index.shape[0] - 1] % 2 == 0
-    rows = pl.ds(pl.multiple_of(b * blk, blk), blk)
-    factor = reflect[rows, :]
-    left = jnp.where(first, mine, other)
-    right = jnp.where(first, other, mine)
-    out[:, :half] = source[rows, :half].astype(jnp.float32) + factor * left
-    out[:, half:] = source[rows, half:].astype(jnp.float32) + factor * right
+    factor = reflect[pl.ds(pl.multiple_of(b * blk, blk), blk), :]
+    a = mine[b] + factor * load_quantized(below0, b, blk)
+    c = other[b] + factor * load_quantized(here1, b, blk)
+    out[:, :half] = jnp.where(first, a, c)
+    out[:, half:] = jnp.where(first, c, a)
 
 
 def in_vmem(x):
@@ -342,20 +357,23 @@
         (far0, far1, here, far_q1, near_q1)
     )
     part1 = send(far_q1, lambda r, h, k: (r + 1, 1 - h, k))
-    below1 = send(near_q1, lambda r, h, k: (r + 1, 1 - h, 1 - k))
-    own_f1, other_q0, here = call(
-        far_kernel, "far", tables + [far0, far1, here], [sums, sent, group], {6: 2}, scratch
+    below1 = send(near_q1, lambda r, h, k: (r + 1, 1 - h, 1 - k), wrap=False)
+    own_q1, other_q0, here = call(
+        far_kernel, "far", tables + [far0, far1, here], [sent, sent, group], {6: 2}, scratch
     )
     here0 = send(other_q0, lambda r, h, k: (r, 1 - h, k))
-    here_sib = send(own_f1, lambda r, h, k: (r, h, 1 - k))
+    here_sib = send(own_q1, lambda r, h, k: (r, h, 1 - k))
     (below0,) = call(lambda *refs: add_kernel(2 * pb, *refs), "add_up", [up, part0], [sent])
     part1, _ = lax.optimization_barrier((part1, below0))
     (here1,) = call(lambda *refs: add_kernel(3 * pb, *refs), "add_here", [here, part1], [sent])
-    below0 = send(below0, lambda r, h, k: (r + 1, 1 - h, k))
+    below0 = send(below0, lambda r, h, k: (r + 1, 1 - h, k), wrap=False)
     here1 = send(here1, lambda r, h, k: (r, 1 - h, 1 - k))
 
     factor = jnp.broadcast_to(reflect[:, None], (piece_rows, half))
-    args = [here, here_sib, here0, here1, below0, below1, source, factor]
+    ready = call(
+        ready_kernel, "ready", [index, here, here_sib, here0, below1, source, factor], [sums, sums]
+    )
+    args = [*ready, below0, here1, factor]
     return pl.pallas_call(
         final_kernel,
         grid=(pb,),

time: 102 us -> 96.5 us (0.946)
  the two profiles are of different devices: /device:TPU:1 before, /device:TPU:192 now
where the time goes in v5:
time: 96.5 us; the launch traced here: 97.4 us
  waiting for transfers between devices  39.3 us (41%)
  Pallas kernels  35.3 us (37%)
  starting transfers between devices  18.7 us (19%)
  other arithmetic  2.96 us (3%)
    ppermute x16, waiting for transfers between devices, send(): return lax.ppermute(x, AXES, pairs)  39.3 us
    pallas_call x8, Pallas kernels, call(): pl.pallas_call(kernel, in_specs=specs, out_specs=[pl.BlockSpec(memory_spa...  32.8 us
    ppermute x16, starting transfers between devices, send(): return lax.ppermute(x, AXES, pairs)  18.7 us
    pallas_call x1, Pallas kernels, per_device(): pl.pallas_call(final_kernel, grid=(pb,), in_specs=[pl.BlockSpec(memory_sp...  2.55 us
    select_n x3, other arithmetic, split_columns(): return (jnp.where(first, left, right), jnp.where(first, right, left))  2.21 us
  transfers between devices with their start and end apart: 16, of which 7 were waited for; matrix products, arithmetic and copies ran while one was open for 3% of the time, Pallas kernels for 34%

profile of v5, /device:TPU:192, one launch (start us, length us, event | category | flops | bytes accessed | tf_op | source)
XLA Modules:
  0.0 97.4 jit_solution(11418665807865831882)
XLA Ops:
  0.0 1.6 %collective-permute-start.3 = (bf16[2048,256]{1,0:T(8,128)(2,1)}, bf16[2048,256]{1,0:T(8,128)(2,1)S(1)}, u32[]{:S(2)}, u32[]{:S(2)}) collective-permute-start(bf16[2048,256]{1,0:T(8,128)(2,1)} %param.7), channel_id=1, source_target_pairs={{0,2},{1,3},{2,0},{3,1},{4,6},{5,7},{6,4},{7,5},{8,10},{9,11},{10,... | collective-permute-start | bytes 3145736 | tf_op jit(solution)/shard_map/ppermute | solution.py:25
  1.6 4.8 %collective-permute-start.2 = (bf16[2048,256]{1,0:T(8,128)(2,1)}, bf16[2048,256]{1,0:T(8,128)(2,1)S(1)}, u32[]{:S(2)}, u32[]{:S(2)}) collective-permute-start(bf16[2048,256]{1,0:T(8,128)(2,1)} %param.7), channel_id=1, source_target_pairs={{0,254},{1,255},{2,252},{3,253},{4,2},{5,3},{6,0},{7,1},{8,6},{9,7... | collective-permute-start | bytes 3145736 | tf_op jit(solution)/shard_map/ppermute | solution.py:25
  6.4 2.1 %broadcast_select_fusion.4 = (bf16[2048,128]{1,0:T(8,128)(2,1)}, bf16[2048,128]{1,0:T(8,128)(2,1)S(1)}) fusion(pred[]{:T(512)S(6)} %eq.4, bf16[2048,256]{1,0:T(8,128)(2,1)} %param.7), kind=kLoop, calls=%fused_computation.4 | loop fusion | flops 524288 | bytes 2097153 | tf_op jit(solution)/shard_map/jit(_where)/select_n | solution.py:53
  9.1 0.7 subtract_bitcast_fusion
  9.9 0.5 collective-permute-start
  10.4 2.7 %collective-permute-done.refs_1_ = s32[34]{0:T(128)S(1)} collective-permute-done((s32[34]{0:T(128)S(1)}, s32[34]{0:T(128)S(1)}, u32[]{:S(2)}, u32[]{:S(2)}) %collective-permute-start) | collective-permute-done | bytes 168 | tf_op jit(solution)/shard_map/ppermute | solution.py:25
  13.1 1.0 %collective-permute-done.4.refs_5_ = bf16[2048,128]{1,0:T(8,128)(2,1)S(1)} collective-permute-done((bf16[2048,128]{1,0:T(8,128)(2,1)}, bf16[2048,128]{1,0:T(8,128)(2,1)S(1)}, u32[]{:S(2)}, u32[]{:S(2)}) %collective-permute-start.4) | collective-permute-done | bytes 524320 | tf_op jit(solution)/shard_map/ppermute | solution.py:25
  14.1 3.9 %chip_up.1.refs_6_ = f32[16,512,128]{2,1,0:T(8,128)S(1)} custom-call(s32[34]{0:T(128)S(1)} %pad_add_fusion.refs_0_.index, s32[34]{0:T(128)S(1)} %collective-permute-done.refs_1_, bf16[16,512,512]{2,1,0:T(8,128)(2,1)} %refs_2_.9, bf16[16,512,512]{2,1,0:T(8,128)(2,1)} %collective-permute-done.1.refs_3_, bf16[2048,128]{1,0:T(8,128)(2,1)S(1)} %get-tuple-element.52.refs_4_, ...), custom_call_target="tpu_custom_call" | custom-call | flops 1000 | bytes 1000 | tf_op jit(solution)/shard_map/chip_up/pallas_call | solution.py:290
  18.0 6.3 %chip_here.1.refs_8_ = f32[16,512,128]{2,1,0:T(8,128)S(1)} custom-call(s32[34]{0:T(128)S(1)} %pad_add_fusion.refs_0_.index, s32[34]{0:T(128)S(1)} %collective-permute-done.refs_1_, bf16[16,512,512]{2,1,0:T(8,128)(2,1)} %refs_2_.9, bf16[16,512,512]{2,1,0:T(8,128)(2,1)} %collective-permute-done.1.refs_3_, bf16[2048,128]{1,0:T(8,128)(2,1)S(1)} %get-tuple-element.52.refs_4_, ...), custom_call_target="tpu_custom_call" | custom-call | flops 1000 | bytes 1000 | tf_op jit(solution)/shard_map/chip_here/pallas_call | solution.py:290
  24.3 1.5 %collective-permute-done.3 = bf16[2048,256]{1,0:T(8,128)(2,1)S(1)} collective-permute-done((bf16[2048,256]{1,0:T(8,128)(2,1)}, bf16[2048,256]{1,0:T(8,128)(2,1)S(1)}, u32[]{:S(2)}, u32[]{:S(2)}) %collective-permute-start.3) | collective-permute-done | bytes 1048608 | tf_op jit(solution)/shard_map/ppermute | solution.py:25
  25.9 3.7 %collective-permute-done.2 = bf16[2048,256]{1,0:T(8,128)(2,1)S(1)} collective-permute-done((bf16[2048,256]{1,0:T(8,128)(2,1)}, bf16[2048,256]{1,0:T(8,128)(2,1)S(1)}, u32[]{:S(2)}, u32[]{:S(2)}) %collective-permute-start.2) | collective-permute-done | bytes 1048608 | tf_op jit(solution)/shard_map/ppermute | solution.py:25
  29.6 0.1 collective-permute-start.8
  29.7 0.5 collective-permute-start.7
  30.2 0.7 collective-permute-start.5
  30.9 5.6 %collective-permute-start.6 = (bf16[2048,128]{1,0:T(8,128)(2,1)S(1)}, bf16[2048,128]{1,0:T(8,128)(2,1)S(1)}, u32[]{:S(2)}, u32[]{:S(2)}) collective-permute-start(bf16[2048,128]{1,0:T(8,128)(2,1)S(1)} %get-tuple-element.50), channel_id=1, source_target_pairs={{0,255},{1,254},{2,253},{3,252},{4,3},{5,2},{6,1},{7,0},{8,7},{9,6... | collective-permute-start | bytes 1572872 | tf_op jit(solution)/shard_map/ppermute | solution.py:25
  36.5 6.7 %up.1 = (s16[4,528,128]{2,1,0:T(8,128)(2,1)S(1)}, s16[4,528,128]{2,1,0:T(8,128)(2,1)S(1)}, s16[4,528,128]{2,1,0:T(8,128)(2,1)S(1)}, f32[16,512,128]{2,1,0:T(8,128)S(1)}) custom-call(s32[34]{0:T(128)S(1)} %pad_add_fusion.refs_0_.index, s32[34]{0:T(128)S(1)} %collective-permute-done.refs_1_, ...), custom_call_target="tpu_custom_call", output_to_operand_aliasing={{3}: (6, {})} | custom-call | flops 1000 | bytes 1000 | tf_op jit(solution)/shard_map/up/pallas_call | solution.py:290
  43.2 0.1 collective-permute-start.12
  43.3 9.4 %group.1.refs_6_ = f32[16,512,128]{2,1,0:T(8,128)S(1)} custom-call(s32[34]{0:T(128)S(1)} %pad_add_fusion.refs_0_.index, s32[34]{0:T(128)S(1)} %collective-permute-done.refs_1_, bf16[16,512,512]{2,1,0:T(8,128)(2,1)} %refs_2_.9, bf16[16,512,512]{2,1,0:T(8,128)(2,1)} %collective-permute-done.1.refs_3_, ...), custom_call_target="tpu_custom_call", output_to_operand_aliasing={{}: (8, {})} | custom-call | flops 1000 | bytes 1000 | tf_op jit(solution)/shard_map/group/pallas_call | solution.py:290
  52.7 0.1 collective-permute-start.14
  52.7 4.5 %far.1 = (s16[4,528,128]{2,1,0:T(8,128)(2,1)S(1)}, s16[4,528,128]{2,1,0:T(8,128)(2,1)S(1)}, f32[16,512,128]{2,1,0:T(8,128)S(1)}) custom-call(s32[34]{0:T(128)S(1)} %pad_add_fusion.refs_0_.index, s32[34]{0:T(128)S(1)} %collective-permute-done.refs_1_, bf16[16,512,512]{2,1,0:T(8,128)(2,1)} %refs_2_.9, ...), custom_call_target="tpu_custom_call", output_to_operand_aliasing={{2}: (6, {})} | custom-call | flops 1000 | bytes 1000 | tf_op jit(solution)/shard_map/far/pallas_call | solution.py:290
  57.2 0.6 collective-permute-start.9
  57.8 1.9 %collective-permute-start.11 = (s16[4,528,128]{2,1,0:T(8,128)(2,1)S(1)}, s16[4,528,128]{2,1,0:T(8,128)(2,1)S(1)}, u32[]{:S(2)}, u32[]{:S(2)}) collective-permute-start(s16[4,528,128]{2,1,0:T(8,128)(2,1)S(1)} %get-tuple-element.40), channel_id=1, source_target_pairs={{0,7},{1,6},{2,5},{3,4},{4,11},{5,10},{6,9},{7,8},{8,15},{9,14},{1... | collective-permute-start | bytes 1622024 | tf_op jit(solution)/shard_map/ppermute | solution.py:25
  59.8 0.4 add_up.1
  60.2 2.1 %collective-permute-start.13 = (s16[4,528,128]{2,1,0:T(8,128)(2,1)S(1)}, s16[4,528,128]{2,1,0:T(8,128)(2,1)S(1)}, u32[]{:S(2)}, u32[]{:S(2)}) collective-permute-start(s16[4,528,128]{2,1,0:T(8,128)(2,1)S(1)} %add_up.1), channel_id=1, source_target_pairs={{0,6},{1,7},{2,4},{3,5},{4,10},{5,11},{6,8},{7,9},{8,14},{9,15},{1... | collective-permute-start | bytes 1622024 | tf_op jit(solution)/shard_map/ppermute | solution.py:25
  62.3 9.8 %collective-permute-done.14.refs_1_ = s16[4,528,128]{2,1,0:T(8,128)(2,1)S(1)} collective-permute-done((s16[4,528,128]{2,1,0:T(8,128)(2,1)S(1)}, s16[4,528,128]{2,1,0:T(8,128)(2,1)S(1)}, u32[]{:S(2)}, u32[]{:S(2)}) %collective-permute-start.14) | collective-permute-done | bytes 540704 | tf_op jit(solution)/shard_map/ppermute | solution.py:25
  72.0 0.4 add_here.1
  72.4 0.1 collective-permute-start.15
  72.5 10.3 %collective-permute-done.11.below1 = s16[4,528,128]{2,1,0:T(8,128)(2,1)S(1)} collective-permute-done((s16[4,528,128]{2,1,0:T(8,128)(2,1)S(1)}, s16[4,528,128]{2,1,0:T(8,128)(2,1)S(1)}, u32[]{:S(2)}, u32[]{:S(2)}) %collective-permute-start.11) | collective-permute-done | bytes 540704 | tf_op jit(solution)/shard_map/ppermute | solution.py:25
  82.9 0.3 broadcast_in_dim.10.reflect
  83.2 1.3 %ready.1 = (f32[4,512,128]{2,1,0:T(8,128)S(1)}, f32[4,512,128]{2,1,0:T(8,128)S(1)}) custom-call(s32[34]{0:T(128)S(1)} %pad_add_fusion.refs_0_.index, f32[16,512,128]{2,1,0:T(8,128)S(1)} %get-tuple-element.37.sums.refs_0_, s16[4,528,128]{2,1,0:T(8,128)(2,1)S(1)} %collective-permute-done.9.sib, s16[4,528,128]{2,1,0:T(8,128)(2,1)S(1)} %collective-permute-done.10.here0, ...), custom_call_target="tpu_custom_call" | custom-call | flops 1000 | bytes 1000 | tf_op jit(solution)/shard_map/ready/pallas_call | solution.py:290
  84.6 10.3 %collective-permute-done.13.below0 = s16[4,528,128]{2,1,0:T(8,128)(2,1)S(1)} collective-permute-done((s16[4,528,128]{2,1,0:T(8,128)(2,1)S(1)}, s16[4,528,128]{2,1,0:T(8,128)(2,1)S(1)}, u32[]{:S(2)}, u32[]{:S(2)}) %collective-permute-start.13) | collective-permute-done | bytes 540704 | tf_op jit(solution)/shard_map/ppermute | solution.py:25
  94.8 2.5 %final.1 = f32[2048,256]{1,0:T(8,128)} custom-call(s32[34]{0:T(128)S(1)} %pad_add_fusion.refs_0_.index, f32[4,512,128]{2,1,0:T(8,128)S(1)} %get-tuple-element.41.mine, f32[4,512,128]{2,1,0:T(8,128)S(1)} %get-tuple-element.42.other, s16[4,528,128]{2,1,0:T(8,128)(2,1)S(1)} %collective-permute-done.13.below0, ...), custom_call_target="tpu_custom_call" | custom-call | tf_op jit(solution)/shard_map/final/pallas_call | solution.py:377
  (19 shorter events, 0.3 us)
Async XLA Ops:
  0.0 14.1 %collective-permute-start.1 = (bf16[16,512,512]{2,1,0:T(8,128)(2,1)}, bf16[16,512,512]{2,1,0:T(8,128)(2,1)}, u32[]{:S(2)}, u32[]{:S(2)}) collective-permute-start(bf16[16,512,512]{2,1,0:T(8,128)(2,1)} %refs_2_.9), channel_id=1, source_target_pairs={{0,1},{1,0},{2,3},{3,2},{4,5},{5,4},{6,7},{7,6},{8,9},{9,8},{10,11... | collective-permute-start | bytes 25165832 | tf_op jit(solution)/shard_map/ppermute | solution.py:25
  0.0 25.8 %collective-permute-start.3 = (bf16[2048,256]{1,0:T(8,128)(2,1)}, bf16[2048,256]{1,0:T(8,128)(2,1)S(1)}, u32[]{:S(2)}, u32[]{:S(2)}) collective-permute-start(bf16[2048,256]{1,0:T(8,128)(2,1)} %param.7), channel_id=1, source_target_pairs={{0,2},{1,3},{2,0},{3,1},{4,6},{5,7},{6,4},{7,5},{8,10},{9,11},{10,... | collective-permute-start | bytes 3145736 | tf_op jit(solution)/shard_map/ppermute | solution.py:25
  1.6 27.9 %collective-permute-start.2 = (bf16[2048,256]{1,0:T(8,128)(2,1)}, bf16[2048,256]{1,0:T(8,128)(2,1)S(1)}, u32[]{:S(2)}, u32[]{:S(2)}) collective-permute-start(bf16[2048,256]{1,0:T(8,128)(2,1)} %param.7), channel_id=1, source_target_pairs={{0,254},{1,255},{2,252},{3,253},{4,2},{5,3},{6,0},{7,1},{8,6},{9,7... | collective-permute-start | bytes 3145736 | tf_op jit(solution)/shard_map/ppermute | solution.py:25
  8.5 5.7 %collective-permute-start.4 = (bf16[2048,128]{1,0:T(8,128)(2,1)}, bf16[2048,128]{1,0:T(8,128)(2,1)S(1)}, u32[]{:S(2)}, u32[]{:S(2)}) collective-permute-start(bf16[2048,128]{1,0:T(8,128)(2,1)} %get-tuple-element.51), channel_id=1, source_target_pairs={{0,1},{1,0},{2,3},{3,2},{4,5},{5,4},{6,7},{7,6},{8,9},{9,8},{10,11... | collective-permute-start | bytes 1572872 | tf_op jit(solution)/shard_map/ppermute | solution.py:25
  9.9 3.2 %collective-permute-start = (s32[34]{0:T(128)S(1)}, s32[34]{0:T(128)S(1)}, u32[]{:S(2)}, u32[]{:S(2)}) collective-permute-start(s32[34]{0:T(128)S(1)} %pad_add_fusion.refs_0_.index), channel_id=1, source_target_pairs={{0,1},{1,0},{2,3},{3,2},{4,5},{5,4},{6,7},{7,6},{8,9},{9,8},{10,11... | collective-permute-start | bytes 416 | tf_op jit(solution)/shard_map/ppermute | solution.py:25
  29.6 6.9 %collective-permute-start.8 = (bf16[2048,128]{1,0:T(8,128)(2,1)S(1)}, bf16[2048,128]{1,0:T(8,128)(2,1)S(1)}, u32[]{:S(2)}, u32[]{:S(2)}) collective-permute-start(bf16[2048,128]{1,0:T(8,128)(2,1)S(1)} %get-tuple-element.47), channel_id=1, source_target_pairs={{0,1},{1,0},{2,3},{3,2},{4,5},{5,4},{6,7},{7,6},{8,9},{9,8},{10,11... | collective-permute-start | bytes 1572872 | tf_op jit(solution)/shard_map/ppermute | solution.py:25
  29.7 6.8 %collective-permute-start.7 = (bf16[2048,128]{1,0:T(8,128)(2,1)S(1)}, bf16[2048,128]{1,0:T(8,128)(2,1)S(1)}, u32[]{:S(2)}, u32[]{:S(2)}) collective-permute-start(bf16[2048,128]{1,0:T(8,128)(2,1)S(1)} %get-tuple-element.50), channel_id=1, source_target_pairs={{0,1},{1,0},{2,3},{3,2},{4,5},{5,4},{6,7},{7,6},{8,9},{9,8},{10,11... | collective-permute-start | bytes 1572872 | tf_op jit(solution)/shard_map/ppermute | solution.py:25
  30.2 22.4 %collective-permute-start.5 = (bf16[2048,128]{1,0:T(8,128)(2,1)S(1)}, bf16[2048,128]{1,0:T(8,128)(2,1)S(1)}, u32[]{:S(2)}, u32[]{:S(2)}) collective-permute-start(bf16[2048,128]{1,0:T(8,128)(2,1)S(1)} %get-tuple-element.48.refs_6_), channel_id=1, source_target_pairs={{0,2},{1,3},{2,0},{3,1},{4,6},{5,7},{6,4},{7,5},{8,10},{9,11},{10,... | collective-permute-start | bytes 1572872 | tf_op jit(solution)/shard_map/ppermute | solution.py:25
  30.9 21.8 %collective-permute-start.6 = (bf16[2048,128]{1,0:T(8,128)(2,1)S(1)}, bf16[2048,128]{1,0:T(8,128)(2,1)S(1)}, u32[]{:S(2)}, u32[]{:S(2)}) collective-permute-start(bf16[2048,128]{1,0:T(8,128)(2,1)S(1)} %get-tuple-element.50), channel_id=1, source_target_pairs={{0,255},{1,254},{2,253},{3,252},{4,3},{5,2},{6,1},{7,0},{8,7},{9,6... | collective-permute-start | bytes 1572872 | tf_op jit(solution)/shard_map/ppermute | solution.py:25
  43.2 16.6 %collective-permute-start.12 = (s16[4,528,128]{2,1,0:T(8,128)(2,1)S(1)}, s16[4,528,128]{2,1,0:T(8,128)(2,1)S(1)}, u32[]{:S(2)}, u32[]{:S(2)}) collective-permute-start(s16[4,528,128]{2,1,0:T(8,128)(2,1)S(1)} %get-tuple-element.44), channel_id=1, source_target_pairs={{0,2},{1,3},{2,0},{3,1},{4,6},{5,7},{6,4},{7,5},{8,10},{9,11},{10,... | collective-permute-start | bytes 1622024 | tf_op jit(solution)/shard_map/ppermute | solution.py:25
  52.7 19.4 %collective-permute-start.14 = (s16[4,528,128]{2,1,0:T(8,128)(2,1)S(1)}, s16[4,528,128]{2,1,0:T(8,128)(2,1)S(1)}, u32[]{:S(2)}, u32[]{:S(2)}) collective-permute-start(s16[4,528,128]{2,1,0:T(8,128)(2,1)S(1)} %get-tuple-element.45), channel_id=1, source_target_pairs={{0,6},{1,7},{2,4},{3,5},{4,10},{5,11},{6,8},{7,9},{8,14},{9,15},{1... | collective-permute-start | bytes 1622024 | tf_op jit(solution)/shard_map/ppermute | solution.py:25
  57.2 15.3 %collective-permute-start.9 = (s16[4,528,128]{2,1,0:T(8,128)(2,1)S(1)}, s16[4,528,128]{2,1,0:T(8,128)(2,1)S(1)}, u32[]{:S(2)}, u32[]{:S(2)}) collective-permute-start(s16[4,528,128]{2,1,0:T(8,128)(2,1)S(1)} %get-tuple-element.38), channel_id=1, source_target_pairs={{0,1},{1,0},{2,3},{3,2},{4,5},{5,4},{6,7},{7,6},{8,9},{9,8},{10,11... | collective-permute-start | bytes 1622024 | tf_op jit(solution)/shard_map/ppermute | solution.py:25
  57.8 14.7 %collective-permute-start.10 = (s16[4,528,128]{2,1,0:T(8,128)(2,1)S(1)}, s16[4,528,128]{2,1,0:T(8,128)(2,1)S(1)}, u32[]{:S(2)}, u32[]{:S(2)}) collective-permute-start(s16[4,528,128]{2,1,0:T(8,128)(2,1)S(1)} %get-tuple-element.39), channel_id=1, source_target_pairs={{0,2},{1,3},{2,0},{3,1},{4,6},{5,7},{6,4},{7,5},{8,10},{9,11},{10,... | collective-permute-start | bytes 1622024 | tf_op jit(solution)/shard_map/ppermute | solution.py:25
  57.8 25.0 %collective-permute-start.11 = (s16[4,528,128]{2,1,0:T(8,128)(2,1)S(1)}, s16[4,528,128]{2,1,0:T(8,128)(2,1)S(1)}, u32[]{:S(2)}, u32[]{:S(2)}) collective-permute-start(s16[4,528,128]{2,1,0:T(8,128)(2,1)S(1)} %get-tuple-element.40), channel_id=1, source_target_pairs={{0,7},{1,6},{2,5},{3,4},{4,11},{5,10},{6,9},{7,8},{8,15},{9,14},{1... | collective-permute-start | bytes 1622024 | tf_op jit(solution)/shard_map/ppermute | solution.py:25
  59.8 23.1 %copy-start.1 = (f32[2048]{0:T(1024)S(1)}, f32[2048]{0:T(1024)}, u32[]{:S(2)}) copy-start(f32[2048]{0:T(1024)} %param.9) | copy-start | bytes 24580
  60.2 23.0 %copy-start = (bf16[2048,256]{1,0:T(8,128)(2,1)S(1)}, bf16[2048,256]{1,0:T(8,128)(2,1)}, u32[]{:S(2)}) copy-start(bf16[2048,256]{1,0:T(8,128)(2,1)} %source.1) | copy-start | bytes 3145732
  60.2 34.6 %collective-permute-start.13 = (s16[4,528,128]{2,1,0:T(8,128)(2,1)S(1)}, s16[4,528,128]{2,1,0:T(8,128)(2,1)S(1)}, u32[]{:S(2)}, u32[]{:S(2)}) collective-permute-start(s16[4,528,128]{2,1,0:T(8,128)(2,1)S(1)} %add_up.1), channel_id=1, source_target_pairs={{0,6},{1,7},{2,4},{3,5},{4,10},{5,11},{6,8},{7,9},{8,14},{9,15},{1... | collective-permute-start | bytes 1622024 | tf_op jit(solution)/shard_map/ppermute | solution.py:25
  72.4 22.4 %collective-permute-start.15 = (s16[4,528,128]{2,1,0:T(8,128)(2,1)S(1)}, s16[4,528,128]{2,1,0:T(8,128)(2,1)S(1)}, u32[]{:S(2)}, u32[]{:S(2)}) collective-permute-start(s16[4,528,128]{2,1,0:T(8,128)(2,1)S(1)} %add_here.1), channel_id=1, source_target_pairs={{0,3},{1,2},{2,1},{3,0},{4,7},{5,6},{6,5},{7,4},{8,11},{9,10},{10,... | collective-permute-start | bytes 1622024 | tf_op jit(solution)/shard_map/ppermute | solution.py:25

commit v6 on v5

--- a/solution.py
+++ b/solution.py
@@ -57,7 +57,9 @@
     pass
 
 
-def products(mirror, direct, index, sib_index, blocks, sib_blocks, pieces, sums, plan, ring, x, sems):
+def products(
+    mirror, direct, index, sib_index, blocks, sib_blocks, pieces, sums, plan, ring, x, sems, moved=0
+):
     n_slots, blk = blocks.shape[0], blocks.shape[1]
     group = sums.shape[0]
     pb, depth = group // 4, ring.shape[0]
@@ -68,7 +70,7 @@
         def scan(is_sib, table):
             def step(slot, n):
                 hit, piece, b, at = pick(table[slot] ^ turn, table[n_slots + slot] ^ turn)
-                plan[n] = (((at * pb + b) * 8 + piece) * 2 + is_sib) * n_slots + slot
+                plan[n] = (((at * 2 * pb + b) * 8 + piece) * 2 + is_sib) * n_slots + slot
                 return n + jnp.where(hit, 1, 0)
 
             return step
@@ -89,7 +91,12 @@
 
     def pick_direct(row, col):
         hit, first = direct(col // (2 * pb))
-        return hit, first + col // pb % 2, col % pb, row
+        piece, b = first + col // pb % 2, col % pb
+        if moved:
+            b = col % (2 * pb)
+            piece = jnp.where(b < pb + moved, 0, 1)
+            b = b - piece * (pb + moved)
+        return hit, piece, b, row
 
     zero = jnp.int32(0)
     n_mirror = planned(zero, pick_mirror) if mirror else zero
@@ -118,7 +125,7 @@
 
     def staged(i, u):
         entry = plan[i] // (2 * n_slots)
-        piece, b, at = entry % 8, entry // 8 % pb, entry // (8 * pb)
+        piece, b, at = entry % 8, entry // 8 % (2 * pb), entry // (16 * pb)
         for p, ref in enumerate(pieces):
 
             @pl.when(piece == p)
@@ -218,7 +225,7 @@
     tables, pieces, earlier = refs[:4], refs[4:6], refs[6]
     own1, other0, sums = refs[7:10]
     goes_on(earlier, sums)
-    products(None, from_pair(2), *tables, pieces, sums, *refs[10:])
+    products(None, from_pair(2), *tables, pieces, sums, *refs[10:], moved=1)
     pb = own1.shape[0]
 
     def finish(b):
@@ -338,11 +345,11 @@
     pair, up, here = lax.optimization_barrier((pair, up, here))
     pair0, other = split_columns(pair, k)
     near, _ = lax.optimization_barrier((near, other))
-    far1 = send(other, lambda r, h, k: (r - 1, 1 - h, 1 - k))
+    far1 = send(other[blk:], lambda r, h, k: (r - 1, 1 - h, 1 - k))
     pair1 = send(other, to_sibling)
     near0, other = split_columns(near, k)
     near1 = send(other, to_sibling)
-    far0 = send(near0, across)
+    far0 = send(jnp.concatenate([near0, near1[:blk]]), across)
 
     up, near1 = lax.optimization_barrier((up, near1))
     far_q0, far_q1, near_q1, up = call(
@@ -353,9 +360,8 @@
     (here,) = call(
         group_kernel, "group", tables + [pair0, pair1, near0, near1, here], [group], {8: 0}, scratch
     )
-    far0, far1, here, far_q1, near_q1 = lax.optimization_barrier(
-        (far0, far1, here, far_q1, near_q1)
-    )
+    far1, here, far_q1, near_q1 = lax.optimization_barrier((far1, here, far_q1, near_q1))
+    far0, near_q1 = lax.optimization_barrier((far0, near_q1))
     part1 = send(far_q1, lambda r, h, k: (r + 1, 1 - h, k))
     below1 = send(near_q1, lambda r, h, k: (r + 1, 1 - h, 1 - k), wrap=False)
     own_q1, other_q0, here = call(
@@ -363,6 +369,7 @@
     )
     here0 = send(other_q0, lambda r, h, k: (r, 1 - h, k))
     here_sib = send(own_q1, lambda r, h, k: (r, h, 1 - k))
+    part0, _ = lax.optimization_barrier((part0, other_q0))
     (below0,) = call(lambda *refs: add_kernel(2 * pb, *refs), "add_up", [up, part0], [sent])
     part1, _ = lax.optimization_barrier((part1, below0))
     (here1,) = call(lambda *refs: add_kernel(3 * pb, *refs), "add_here", [here, part1], [sent])

time: 96.5 us -> 98.3 us (1.019)
  the two profiles are of different devices: /device:TPU:192 before, /device:TPU:1 now
where the time goes in v6:
time: 98.3 us; the launch traced here: 98 us
  waiting for transfers between devices  33.6 us (34%)
  Pallas kernels  32.8 us (33%)
  starting transfers between devices  27.3 us (28%)
  other arithmetic  3.01 us (3%)
    ppermute x16, waiting for transfers between devices, send(): return lax.ppermute(x, AXES, pairs)  33.6 us
    pallas_call x8, Pallas kernels, call(): pl.pallas_call(kernel, in_specs=specs, out_specs=[pl.BlockSpec(memory_spa...  30.3 us
    ppermute x16, starting transfers between devices, send(): return lax.ppermute(x, AXES, pairs)  27.3 us
    pallas_call x1, Pallas kernels, per_device(): pl.pallas_call(final_kernel, grid=(pb,), in_specs=[pl.BlockSpec(memory_sp...  2.55 us
    select_n x3, other arithmetic, split_columns(): return (jnp.where(first, left, right), jnp.where(first, right, left))  2.21 us
  transfers between devices with their start and end apart: 16, of which 9 were waited for; matrix products, arithmetic and copies ran while one was open for 3% of the time, Pallas kernels for 31%

profile of v6, /device:TPU:1, one launch (start us, length us, event | category | flops | bytes accessed | tf_op | source)
XLA Modules:
  0.0 98.0 jit_solution(18102516637878548957)
XLA Ops:
  0.0 3.2 %collective-permute-start.1 = (bf16[16,512,512]{2,1,0:T(8,128)(2,1)}, bf16[16,512,512]{2,1,0:T(8,128)(2,1)}, u32[]{:S(2)}, u32[]{:S(2)}) collective-permute-start(bf16[16,512,512]{2,1,0:T(8,128)(2,1)} %refs_2_.9), channel_id=1, source_target_pairs={{0,1},{1,0},{2,3},{3,2},{4,5},{5,4},{6,7},{7,6},{8,9},{9,8},{10,11... | collective-permute-start | bytes 25165832 | tf_op jit(solution)/shard_map/ppermute | solution.py:25
  3.2 8.9 %collective-permute-start.2 = (bf16[2048,256]{1,0:T(8,128)(2,1)}, bf16[2048,256]{1,0:T(8,128)(2,1)S(1)}, u32[]{:S(2)}, u32[]{:S(2)}) collective-permute-start(bf16[2048,256]{1,0:T(8,128)(2,1)} %param.7), channel_id=1, source_target_pairs={{0,254},{1,255},{2,252},{3,253},{4,2},{5,3},{6,0},{7,1},{8,6},{9,7... | collective-permute-start | bytes 3145736 | tf_op jit(solution)/shard_map/ppermute | solution.py:25
  12.2 2.1 %broadcast_select_fusion.4 = (bf16[2048,128]{1,0:T(8,128)(2,1)}, bf16[2048,128]{1,0:T(8,128)(2,1)S(1)}) fusion(pred[]{:T(512)S(6)} %eq.4, bf16[2048,256]{1,0:T(8,128)(2,1)} %param.7), kind=kLoop, calls=%fused_computation.5 | loop fusion | flops 524288 | bytes 2097153 | tf_op jit(solution)/shard_map/jit(_where)/select_n | solution.py:53
  14.3 0.6 collective-permute-start.4
  15.5 0.7 subtract_bitcast_fusion
  16.3 1.1 %collective-permute-done.refs_1_ = s32[34]{0:T(128)S(1)} collective-permute-done((s32[34]{0:T(128)S(1)}, s32[34]{0:T(128)S(1)}, u32[]{:S(2)}, u32[]{:S(2)}) %collective-permute-start) | collective-permute-done | bytes 168 | tf_op jit(solution)/shard_map/ppermute | solution.py:25
  17.4 3.2 %chip_up.1.refs_6_ = f32[16,512,128]{2,1,0:T(8,128)S(1)} custom-call(s32[34]{0:T(128)S(1)} %pad_add_fusion.refs_0_.index, s32[34]{0:T(128)S(1)} %collective-permute-done.refs_1_, bf16[16,512,512]{2,1,0:T(8,128)(2,1)} %refs_2_.9, bf16[16,512,512]{2,1,0:T(8,128)(2,1)} %collective-permute-done.1.refs_3_, bf16[2048,128]{1,0:T(8,128)(2,1)S(1)} %get-tuple-element.56.refs_4_, ...), custom_call_target="tpu_custom_call" | custom-call | flops 1000 | bytes 1000 | tf_op jit(solution)/shard_map/chip_up/pallas_call | solution.py:297
  20.6 6.0 %chip_here.1.refs_8_ = f32[16,512,128]{2,1,0:T(8,128)S(1)} custom-call(s32[34]{0:T(128)S(1)} %pad_add_fusion.refs_0_.index, s32[34]{0:T(128)S(1)} %collective-permute-done.refs_1_, bf16[16,512,512]{2,1,0:T(8,128)(2,1)} %refs_2_.9, bf16[16,512,512]{2,1,0:T(8,128)(2,1)} %collective-permute-done.1.refs_3_, bf16[2048,128]{1,0:T(8,128)(2,1)S(1)} %get-tuple-element.56.refs_4_, ...), custom_call_target="tpu_custom_call" | custom-call | flops 1000 | bytes 1000 | tf_op jit(solution)/shard_map/chip_here/pallas_call | solution.py:297
  26.6 1.6 %collective-permute-done.3 = bf16[2048,256]{1,0:T(8,128)(2,1)S(1)} collective-permute-done((bf16[2048,256]{1,0:T(8,128)(2,1)}, bf16[2048,256]{1,0:T(8,128)(2,1)S(1)}, u32[]{:S(2)}, u32[]{:S(2)}) %collective-permute-start.3) | collective-permute-done | bytes 1048608 | tf_op jit(solution)/shard_map/ppermute | solution.py:25
  28.3 6.5 %collective-permute-done.2 = bf16[2048,256]{1,0:T(8,128)(2,1)S(1)} collective-permute-done((bf16[2048,256]{1,0:T(8,128)(2,1)}, bf16[2048,256]{1,0:T(8,128)(2,1)S(1)}, u32[]{:S(2)}, u32[]{:S(2)}) %collective-permute-start.2) | collective-permute-done | bytes 1048608 | tf_op jit(solution)/shard_map/ppermute | solution.py:25
  34.9 1.2 %collective-permute-start.5 = (bf16[2048,128]{1,0:T(8,128)(2,1)S(1)}, bf16[2048,128]{1,0:T(8,128)(2,1)S(1)}, u32[]{:S(2)}, u32[]{:S(2)}) collective-permute-start(bf16[2048,128]{1,0:T(8,128)(2,1)S(1)} %get-tuple-element.54), channel_id=1, source_target_pairs={{0,1},{1,0},{2,3},{3,2},{4,5},{5,4},{6,7},{7,6},{8,9},{9,8},{10,11... | collective-permute-start | bytes 1572872 | tf_op jit(solution)/shard_map/ppermute | solution.py:25
  36.0 0.1 collective-permute-start.8
  36.2 7.9 %collective-permute-start.7 = (bf16[1536,128]{1,0:T(8,128)(2,1)S(1)}, bf16[1536,128]{1,0:T(8,128)(2,1)S(1)}, u32[]{:S(2)}, u32[]{:S(2)}) collective-permute-start(bf16[1536,128]{1,0:T(8,128)(2,1)S(1)} %slice.33), channel_id=1, source_target_pairs={{0,255},{1,254},{2,253},{3,252},{4,3},{5,2},{6,1},{7,0},{8,7},{9,6... | collective-permute-start | bytes 1179656 | tf_op jit(solution)/shard_map/ppermute | solution.py:25
  44.3 5.3 %up.1 = (s16[4,528,128]{2,1,0:T(8,128)(2,1)S(1)}, s16[4,528,128]{2,1,0:T(8,128)(2,1)S(1)}, s16[4,528,128]{2,1,0:T(8,128)(2,1)S(1)}, f32[16,512,128]{2,1,0:T(8,128)S(1)}) custom-call(s32[34]{0:T(128)S(1)} %pad_add_fusion.refs_0_.index, s32[34]{0:T(128)S(1)} %collective-permute-done.refs_1_, ...), custom_call_target="tpu_custom_call", output_to_operand_aliasing={{3}: (6, {})} | custom-call | flops 1000 | bytes 1000 | tf_op jit(solution)/shard_map/up/pallas_call | solution.py:297
  49.6 0.7 collective-permute-start.12
  50.3 9.7 %group.1.refs_6_ = f32[16,512,128]{2,1,0:T(8,128)S(1)} custom-call(s32[34]{0:T(128)S(1)} %pad_add_fusion.refs_0_.index, s32[34]{0:T(128)S(1)} %collective-permute-done.refs_1_, bf16[16,512,512]{2,1,0:T(8,128)(2,1)} %refs_2_.9, bf16[16,512,512]{2,1,0:T(8,128)(2,1)} %collective-permute-done.1.refs_3_, ...), custom_call_target="tpu_custom_call", output_to_operand_aliasing={{}: (8, {})} | custom-call | flops 1000 | bytes 1000 | tf_op jit(solution)/shard_map/group/pallas_call | solution.py:297
  60.1 0.4 collective-permute-done.6.refs_4_
  60.5 3.9 %far.1 = (s16[4,528,128]{2,1,0:T(8,128)(2,1)S(1)}, s16[4,528,128]{2,1,0:T(8,128)(2,1)S(1)}, f32[16,512,128]{2,1,0:T(8,128)S(1)}) custom-call(s32[34]{0:T(128)S(1)} %pad_add_fusion.refs_0_.index, s32[34]{0:T(128)S(1)} %collective-permute-done.refs_1_, bf16[16,512,512]{2,1,0:T(8,128)(2,1)} %refs_2_.9, ...), custom_call_target="tpu_custom_call", output_to_operand_aliasing={{2}: (6, {})} | custom-call | flops 1000 | bytes 1000 | tf_op jit(solution)/shard_map/far/pallas_call | solution.py:297
  64.5 1.4 %collective-permute-start.9 = (s16[4,528,128]{2,1,0:T(8,128)(2,1)S(1)}, s16[4,528,128]{2,1,0:T(8,128)(2,1)S(1)}, u32[]{:S(2)}, u32[]{:S(2)}) collective-permute-start(s16[4,528,128]{2,1,0:T(8,128)(2,1)S(1)} %get-tuple-element.41), channel_id=1, source_target_pairs={{0,1},{1,0},{2,3},{3,2},{4,5},{5,4},{6,7},{7,6},{8,9},{9,8},{10,11... | collective-permute-start | bytes 1622024 | tf_op jit(solution)/shard_map/ppermute | solution.py:25
  65.9 0.2 collective-permute-start.10
  66.1 1.3 %collective-permute-start.11 = (s16[4,528,128]{2,1,0:T(8,128)(2,1)S(1)}, s16[4,528,128]{2,1,0:T(8,128)(2,1)S(1)}, u32[]{:S(2)}, u32[]{:S(2)}) collective-permute-start(s16[4,528,128]{2,1,0:T(8,128)(2,1)S(1)} %get-tuple-element.43), channel_id=1, source_target_pairs={{0,7},{1,6},{2,5},{3,4},{4,11},{5,10},{6,9},{7,8},{8,15},{9,14},{1... | collective-permute-start | bytes 1622024 | tf_op jit(solution)/shard_map/ppermute | solution.py:25
  67.4 4.7 %collective-permute-done.12.refs_1_ = s16[4,528,128]{2,1,0:T(8,128)(2,1)S(1)} collective-permute-done((s16[4,528,128]{2,1,0:T(8,128)(2,1)S(1)}, s16[4,528,128]{2,1,0:T(8,128)(2,1)S(1)}, u32[]{:S(2)}, u32[]{:S(2)}) %collective-permute-start.12) | collective-permute-done | bytes 540704 | tf_op jit(solution)/shard_map/ppermute | solution.py:25
  72.1 0.4 add_up.1
  72.5 1.5 %collective-permute-start.13 = (s16[4,528,128]{2,1,0:T(8,128)(2,1)S(1)}, s16[4,528,128]{2,1,0:T(8,128)(2,1)S(1)}, u32[]{:S(2)}, u32[]{:S(2)}) collective-permute-start(s16[4,528,128]{2,1,0:T(8,128)(2,1)S(1)} %add_up.1), channel_id=1, source_target_pairs={{0,6},{1,7},{2,4},{3,5},{4,10},{5,11},{6,8},{7,9},{8,14},{9,15},{1... | collective-permute-start | bytes 1622024 | tf_op jit(solution)/shard_map/ppermute | solution.py:25
  74.0 4.7 %collective-permute-done.14.refs_1_ = s16[4,528,128]{2,1,0:T(8,128)(2,1)S(1)} collective-permute-done((s16[4,528,128]{2,1,0:T(8,128)(2,1)S(1)}, s16[4,528,128]{2,1,0:T(8,128)(2,1)S(1)}, u32[]{:S(2)}, u32[]{:S(2)}) %collective-permute-start.14) | collective-permute-done | bytes 540704 | tf_op jit(solution)/shard_map/ppermute | solution.py:25
  78.7 0.4 add_here.1
  79.2 4.5 %collective-permute-done.10.here0 = s16[4,528,128]{2,1,0:T(8,128)(2,1)S(1)} collective-permute-done((s16[4,528,128]{2,1,0:T(8,128)(2,1)S(1)}, s16[4,528,128]{2,1,0:T(8,128)(2,1)S(1)}, u32[]{:S(2)}, u32[]{:S(2)}) %collective-permute-start.10) | collective-permute-done | bytes 540704 | tf_op jit(solution)/shard_map/ppermute | solution.py:25
  83.7 0.3 broadcast_in_dim.10.reflect
  84.0 1.3 %ready.1 = (f32[4,512,128]{2,1,0:T(8,128)S(1)}, f32[4,512,128]{2,1,0:T(8,128)S(1)}) custom-call(s32[34]{0:T(128)S(1)} %pad_add_fusion.refs_0_.index, f32[16,512,128]{2,1,0:T(8,128)S(1)} %get-tuple-element.40.sums.refs_0_, s16[4,528,128]{2,1,0:T(8,128)(2,1)S(1)} %collective-permute-done.9.sib, s16[4,528,128]{2,1,0:T(8,128)(2,1)S(1)} %collective-permute-done.10.here0, ...), custom_call_target="tpu_custom_call" | custom-call | flops 1000 | bytes 1000 | tf_op jit(solution)/shard_map/ready/pallas_call | solution.py:297
  85.4 9.2 %collective-permute-done.13.below0 = s16[4,528,128]{2,1,0:T(8,128)(2,1)S(1)} collective-permute-done((s16[4,528,128]{2,1,0:T(8,128)(2,1)S(1)}, s16[4,528,128]{2,1,0:T(8,128)(2,1)S(1)}, u32[]{:S(2)}, u32[]{:S(2)}) %collective-permute-start.13) | collective-permute-done | bytes 540704 | tf_op jit(solution)/shard_map/ppermute | solution.py:25
  94.6 0.9 collective-permute-done.15.here1
  95.5 2.5 %final.1 = f32[2048,256]{1,0:T(8,128)} custom-call(s32[34]{0:T(128)S(1)} %pad_add_fusion.refs_0_.index, f32[4,512,128]{2,1,0:T(8,128)S(1)} %get-tuple-element.44.mine, f32[4,512,128]{2,1,0:T(8,128)S(1)} %get-tuple-element.45.other, s16[4,528,128]{2,1,0:T(8,128)(2,1)S(1)} %collective-permute-done.13.below0, ...), custom_call_target="tpu_custom_call" | custom-call | tf_op jit(solution)/shard_map/final/pallas_call | solution.py:384
  (22 shorter events, 0.6 us)
Async XLA Ops:
  0.0 17.4 %collective-permute-start.1 = (bf16[16,512,512]{2,1,0:T(8,128)(2,1)}, bf16[16,512,512]{2,1,0:T(8,128)(2,1)}, u32[]{:S(2)}, u32[]{:S(2)}) collective-permute-start(bf16[16,512,512]{2,1,0:T(8,128)(2,1)} %refs_2_.9), channel_id=1, source_target_pairs={{0,1},{1,0},{2,3},{3,2},{4,5},{5,4},{6,7},{7,6},{8,9},{9,8},{10,11... | collective-permute-start | bytes 25165832 | tf_op jit(solution)/shard_map/ppermute | solution.py:25
  3.2 25.0 %collective-permute-start.3 = (bf16[2048,256]{1,0:T(8,128)(2,1)}, bf16[2048,256]{1,0:T(8,128)(2,1)S(1)}, u32[]{:S(2)}, u32[]{:S(2)}) collective-permute-start(bf16[2048,256]{1,0:T(8,128)(2,1)} %param.7), channel_id=1, source_target_pairs={{0,2},{1,3},{2,0},{3,1},{4,6},{5,7},{6,4},{7,5},{8,10},{9,11},{10,... | collective-permute-start | bytes 3145736 | tf_op jit(solution)/shard_map/ppermute | solution.py:25
  3.2 31.5 %collective-permute-start.2 = (bf16[2048,256]{1,0:T(8,128)(2,1)}, bf16[2048,256]{1,0:T(8,128)(2,1)S(1)}, u32[]{:S(2)}, u32[]{:S(2)}) collective-permute-start(bf16[2048,256]{1,0:T(8,128)(2,1)} %param.7), channel_id=1, source_target_pairs={{0,254},{1,255},{2,252},{3,253},{4,2},{5,3},{6,0},{7,1},{8,6},{9,7... | collective-permute-start | bytes 3145736 | tf_op jit(solution)/shard_map/ppermute | solution.py:25
  14.3 3.1 %collective-permute-start.4 = (bf16[2048,128]{1,0:T(8,128)(2,1)}, bf16[2048,128]{1,0:T(8,128)(2,1)S(1)}, u32[]{:S(2)}, u32[]{:S(2)}) collective-permute-start(bf16[2048,128]{1,0:T(8,128)(2,1)} %get-tuple-element.55), channel_id=1, source_target_pairs={{0,1},{1,0},{2,3},{3,2},{4,5},{5,4},{6,7},{7,6},{8,9},{9,8},{10,11... | collective-permute-start | bytes 1572872 | tf_op jit(solution)/shard_map/ppermute | solution.py:25
  16.2 1.1 %collective-permute-start = (s32[34]{0:T(128)S(1)}, s32[34]{0:T(128)S(1)}, u32[]{:S(2)}, u32[]{:S(2)}) collective-permute-start(s32[34]{0:T(128)S(1)} %pad_add_fusion.refs_0_.index), channel_id=1, source_target_pairs={{0,1},{1,0},{2,3},{3,2},{4,5},{5,4},{6,7},{7,6},{8,9},{9,8},{10,11... | collective-permute-start | bytes 416 | tf_op jit(solution)/shard_map/ppermute | solution.py:25
  34.9 9.2 %collective-permute-start.5 = (bf16[2048,128]{1,0:T(8,128)(2,1)S(1)}, bf16[2048,128]{1,0:T(8,128)(2,1)S(1)}, u32[]{:S(2)}, u32[]{:S(2)}) collective-permute-start(bf16[2048,128]{1,0:T(8,128)(2,1)S(1)} %get-tuple-element.54), channel_id=1, source_target_pairs={{0,1},{1,0},{2,3},{3,2},{4,5},{5,4},{6,7},{7,6},{8,9},{9,8},{10,11... | collective-permute-start | bytes 1572872 | tf_op jit(solution)/shard_map/ppermute | solution.py:25
  36.0 8.2 %collective-permute-start.8 = (bf16[2048,128]{1,0:T(8,128)(2,1)S(1)}, bf16[2048,128]{1,0:T(8,128)(2,1)S(1)}, u32[]{:S(2)}, u32[]{:S(2)}) collective-permute-start(bf16[2048,128]{1,0:T(8,128)(2,1)S(1)} %get-tuple-element.52), channel_id=1, source_target_pairs={{0,1},{1,0},{2,3},{3,2},{4,5},{5,4},{6,7},{7,6},{8,9},{9,8},{10,11... | collective-permute-start | bytes 1572872 | tf_op jit(solution)/shard_map/ppermute | solution.py:25
  36.2 23.9 %collective-permute-start.7 = (bf16[1536,128]{1,0:T(8,128)(2,1)S(1)}, bf16[1536,128]{1,0:T(8,128)(2,1)S(1)}, u32[]{:S(2)}, u32[]{:S(2)}) collective-permute-start(bf16[1536,128]{1,0:T(8,128)(2,1)S(1)} %slice.33), channel_id=1, source_target_pairs={{0,255},{1,254},{2,253},{3,252},{4,3},{5,2},{6,1},{7,0},{8,7},{9,6... | collective-permute-start | bytes 1179656 | tf_op jit(solution)/shard_map/ppermute | solution.py:25
  44.1 16.4 %collective-permute-start.6 = (bf16[2560,128]{1,0:T(8,128)(2,1)S(1)}, bf16[2560,128]{1,0:T(8,128)(2,1)S(1)}, u32[]{:S(2)}, u32[]{:S(2)}) collective-permute-start(bf16[2560,128]{1,0:T(8,128)(2,1)S(1)} %pad_maximum_fusion), channel_id=1, source_target_pairs={{0,2},{1,3},{2,0},{3,1},{4,6},{5,7},{6,4},{7,5},{8,10},{9,11},{10,... | collective-permute-start | bytes 1966088 | tf_op jit(solution)/shard_map/ppermute | solution.py:25
  49.6 22.5 %collective-permute-start.12 = (s16[4,528,128]{2,1,0:T(8,128)(2,1)S(1)}, s16[4,528,128]{2,1,0:T(8,128)(2,1)S(1)}, u32[]{:S(2)}, u32[]{:S(2)}) collective-permute-start(s16[4,528,128]{2,1,0:T(8,128)(2,1)S(1)} %get-tuple-element.47), channel_id=1, source_target_pairs={{0,2},{1,3},{2,0},{3,1},{4,6},{5,7},{6,4},{7,5},{8,10},{9,11},{10,... | collective-permute-start | bytes 1622024 | tf_op jit(solution)/shard_map/ppermute | solution.py:25
  60.0 18.7 %collective-permute-start.14 = (s16[4,528,128]{2,1,0:T(8,128)(2,1)S(1)}, s16[4,528,128]{2,1,0:T(8,128)(2,1)S(1)}, u32[]{:S(2)}, u32[]{:S(2)}) collective-permute-start(s16[4,528,128]{2,1,0:T(8,128)(2,1)S(1)} %get-tuple-element.49), channel_id=1, source_target_pairs={{0,6},{1,7},{2,4},{3,5},{4,10},{5,11},{6,8},{7,9},{8,14},{9,15},{1... | collective-permute-start | bytes 1622024 | tf_op jit(solution)/shard_map/ppermute | solution.py:25
  64.5 14.7 %collective-permute-start.9 = (s16[4,528,128]{2,1,0:T(8,128)(2,1)S(1)}, s16[4,528,128]{2,1,0:T(8,128)(2,1)S(1)}, u32[]{:S(2)}, u32[]{:S(2)}) collective-permute-start(s16[4,528,128]{2,1,0:T(8,128)(2,1)S(1)} %get-tuple-element.41), channel_id=1, source_target_pairs={{0,1},{1,0},{2,3},{3,2},{4,5},{5,4},{6,7},{7,6},{8,9},{9,8},{10,11... | collective-permute-start | bytes 1622024 | tf_op jit(solution)/shard_map/ppermute | solution.py:25
  65.9 17.8 %collective-permute-start.10 = (s16[4,528,128]{2,1,0:T(8,128)(2,1)S(1)}, s16[4,528,128]{2,1,0:T(8,128)(2,1)S(1)}, u32[]{:S(2)}, u32[]{:S(2)}) collective-permute-start(s16[4,528,128]{2,1,0:T(8,128)(2,1)S(1)} %get-tuple-element.42), channel_id=1, source_target_pairs={{0,2},{1,3},{2,0},{3,1},{4,6},{5,7},{6,4},{7,5},{8,10},{9,11},{10,... | collective-permute-start | bytes 1622024 | tf_op jit(solution)/shard_map/ppermute | solution.py:25
  66.1 17.6 %collective-permute-start.11 = (s16[4,528,128]{2,1,0:T(8,128)(2,1)S(1)}, s16[4,528,128]{2,1,0:T(8,128)(2,1)S(1)}, u32[]{:S(2)}, u32[]{:S(2)}) collective-permute-start(s16[4,528,128]{2,1,0:T(8,128)(2,1)S(1)} %get-tuple-element.43), channel_id=1, source_target_pairs={{0,7},{1,6},{2,5},{3,4},{4,11},{5,10},{6,9},{7,8},{8,15},{9,14},{1... | collective-permute-start | bytes 1622024 | tf_op jit(solution)/shard_map/ppermute | solution.py:25
  72.1 11.6 %copy-start.1 = (f32[2048]{0:T(1024)S(1)}, f32[2048]{0:T(1024)}, u32[]{:S(2)}) copy-start(f32[2048]{0:T(1024)} %param.9) | copy-start | bytes 24580
  72.5 11.5 %copy-start = (bf16[2048,256]{1,0:T(8,128)(2,1)S(1)}, bf16[2048,256]{1,0:T(8,128)(2,1)}, u32[]{:S(2)}) copy-start(bf16[2048,256]{1,0:T(8,128)(2,1)} %source.1) | copy-start | bytes 3145732
  72.5 22.1 %collective-permute-start.13 = (s16[4,528,128]{2,1,0:T(8,128)(2,1)S(1)}, s16[4,528,128]{2,1,0:T(8,128)(2,1)S(1)}, u32[]{:S(2)}, u32[]{:S(2)}) collective-permute-start(s16[4,528,128]{2,1,0:T(8,128)(2,1)S(1)} %add_up.1), channel_id=1, source_target_pairs={{0,6},{1,7},{2,4},{3,5},{4,10},{5,11},{6,8},{7,9},{8,14},{9,15},{1... | collective-permute-start | bytes 1622024 | tf_op jit(solution)/shard_map/ppermute | solution.py:25
  79.1 16.3 %collective-permute-start.15 = (s16[4,528,128]{2,1,0:T(8,128)(2,1)S(1)}, s16[4,528,128]{2,1,0:T(8,128)(2,1)S(1)}, u32[]{:S(2)}, u32[]{:S(2)}) collective-permute-start(s16[4,528,128]{2,1,0:T(8,128)(2,1)S(1)} %add_here.1), channel_id=1, source_target_pairs={{0,3},{1,2},{2,1},{3,0},{4,7},{5,6},{6,5},{7,4},{8,11},{9,10},{10,... | collective-permute-start | bytes 1622024 | tf_op jit(solution)/shard_map/ppermute | solution.py:25

commit v7 on v5

--- a/solution.py
+++ b/solution.py
@@ -338,7 +338,7 @@
     pair, up, here = lax.optimization_barrier((pair, up, here))
     pair0, other = split_columns(pair, k)
     near, _ = lax.optimization_barrier((near, other))
-    far1 = send(other, lambda r, h, k: (r - 1, 1 - h, 1 - k))
+    far1 = send(other, lambda r, h, k: (r - 1, 1 - h, 1 - k), wrap=False)
     pair1 = send(other, to_sibling)
     near0, other = split_columns(near, k)
     near1 = send(other, to_sibling)

time: 96.5 us -> 97.6 us (1.011)
  the two profiles are of different devices: /device:TPU:192 before, /device:TPU:128 now
where the time goes in v7:
time: 97.6 us; the launch traced here: 97.2 us
  waiting for transfers between devices  40.9 us (42%)
  starting transfers between devices  29.7 us (30%)
  Pallas kernels  22.4 us (23%)
  other arithmetic  2.96 us (3%)
    ppermute x16, waiting for transfers between devices, send(): return lax.ppermute(x, AXES, pairs)  40.9 us
    ppermute x16, starting transfers between devices, send(): return lax.ppermute(x, AXES, pairs)  29.7 us
    pallas_call x8, Pallas kernels, call(): pl.pallas_call(kernel, in_specs=specs, out_specs=[pl.BlockSpec(memory_spa...  19.9 us
    pallas_call x1, Pallas kernels, per_device(): pl.pallas_call(final_kernel, grid=(pb,), in_specs=[pl.BlockSpec(memory_sp...  2.55 us
    select_n x3, other arithmetic, split_columns(): return (jnp.where(first, left, right), jnp.where(first, right, left))  2.21 us
  transfers between devices with their start and end apart: 16, of which 7 were waited for; matrix products, arithmetic and copies ran while one was open for 3% of the time, Pallas kernels for 20%

profile of v7, /device:TPU:128, one launch (start us, length us, event | category | flops | bytes accessed | tf_op | source)
XLA Modules:
  0.0 97.2 jit_solution(18130172562565418529)
XLA Ops:
  0.0 1.6 %collective-permute-start.3 = (bf16[2048,256]{1,0:T(8,128)(2,1)}, bf16[2048,256]{1,0:T(8,128)(2,1)S(1)}, u32[]{:S(2)}, u32[]{:S(2)}) collective-permute-start(bf16[2048,256]{1,0:T(8,128)(2,1)} %param.7), channel_id=1, source_target_pairs={{0,2},{1,3},{2,0},{3,1},{4,6},{5,7},{6,4},{7,5},{8,10},{9,11},{10,... | collective-permute-start | bytes 3145736 | tf_op jit(solution)/shard_map/ppermute | solution.py:25
  1.6 3.9 %collective-permute-start.2 = (bf16[2048,256]{1,0:T(8,128)(2,1)}, bf16[2048,256]{1,0:T(8,128)(2,1)S(1)}, u32[]{:S(2)}, u32[]{:S(2)}) collective-permute-start(bf16[2048,256]{1,0:T(8,128)(2,1)} %param.7), channel_id=1, source_target_pairs={{0,254},{1,255},{2,252},{3,253},{4,2},{5,3},{6,0},{7,1},{8,6},{9,7... | collective-permute-start | bytes 3145736 | tf_op jit(solution)/shard_map/ppermute | solution.py:25
  5.5 2.1 %broadcast_select_fusion.4 = (bf16[2048,128]{1,0:T(8,128)(2,1)}, bf16[2048,128]{1,0:T(8,128)(2,1)S(1)}) fusion(pred[]{:T(512)S(6)} %eq.4, bf16[2048,256]{1,0:T(8,128)(2,1)} %param.7), kind=kLoop, calls=%fused_computation.4 | loop fusion | flops 524288 | bytes 2097153 | tf_op jit(solution)/shard_map/jit(_where)/select_n | solution.py:53
  8.2 0.7 subtract_bitcast_fusion
  9.0 0.5 collective-permute-start
  9.5 3.6 %collective-permute-done.refs_1_ = s32[34]{0:T(128)S(1)} collective-permute-done((s32[34]{0:T(128)S(1)}, s32[34]{0:T(128)S(1)}, u32[]{:S(2)}, u32[]{:S(2)}) %collective-permute-start) | collective-permute-done | bytes 168 | tf_op jit(solution)/shard_map/ppermute | solution.py:25
  13.1 1.0 %collective-permute-done.4.refs_5_ = bf16[2048,128]{1,0:T(8,128)(2,1)S(1)} collective-permute-done((bf16[2048,128]{1,0:T(8,128)(2,1)}, bf16[2048,128]{1,0:T(8,128)(2,1)S(1)}, u32[]{:S(2)}, u32[]{:S(2)}) %collective-permute-start.4) | collective-permute-done | bytes 524320 | tf_op jit(solution)/shard_map/ppermute | solution.py:25
  14.1 2.9 %chip_up.1.refs_6_ = f32[16,512,128]{2,1,0:T(8,128)S(1)} custom-call(s32[34]{0:T(128)S(1)} %pad_add_fusion.refs_0_.index, s32[34]{0:T(128)S(1)} %collective-permute-done.refs_1_, bf16[16,512,512]{2,1,0:T(8,128)(2,1)} %refs_2_.9, bf16[16,512,512]{2,1,0:T(8,128)(2,1)} %collective-permute-done.1.refs_3_, bf16[2048,128]{1,0:T(8,128)(2,1)S(1)} %get-tuple-element.52.refs_4_, ...), custom_call_target="tpu_custom_call" | custom-call | flops 1000 | bytes 1000 | tf_op jit(solution)/shard_map/chip_up/pallas_call | solution.py:290
  17.0 3.7 %chip_here.1.refs_8_ = f32[16,512,128]{2,1,0:T(8,128)S(1)} custom-call(s32[34]{0:T(128)S(1)} %pad_add_fusion.refs_0_.index, s32[34]{0:T(128)S(1)} %collective-permute-done.refs_1_, bf16[16,512,512]{2,1,0:T(8,128)(2,1)} %refs_2_.9, bf16[16,512,512]{2,1,0:T(8,128)(2,1)} %collective-permute-done.1.refs_3_, bf16[2048,128]{1,0:T(8,128)(2,1)S(1)} %get-tuple-element.52.refs_4_, ...), custom_call_target="tpu_custom_call" | custom-call | flops 1000 | bytes 1000 | tf_op jit(solution)/shard_map/chip_here/pallas_call | solution.py:290
  20.7 5.1 %collective-permute-done.3 = bf16[2048,256]{1,0:T(8,128)(2,1)S(1)} collective-permute-done((bf16[2048,256]{1,0:T(8,128)(2,1)}, bf16[2048,256]{1,0:T(8,128)(2,1)S(1)}, u32[]{:S(2)}, u32[]{:S(2)}) %collective-permute-start.3) | collective-permute-done | bytes 1048608 | tf_op jit(solution)/shard_map/ppermute | solution.py:25
  25.9 2.8 %collective-permute-done.2 = bf16[2048,256]{1,0:T(8,128)(2,1)S(1)} collective-permute-done((bf16[2048,256]{1,0:T(8,128)(2,1)}, bf16[2048,256]{1,0:T(8,128)(2,1)S(1)}, u32[]{:S(2)}, u32[]{:S(2)}) %collective-permute-start.2) | collective-permute-done | bytes 1048608 | tf_op jit(solution)/shard_map/ppermute | solution.py:25
  28.7 0.1 collective-permute-start.8
  28.8 0.5 collective-permute-start.7
  29.3 0.7 collective-permute-start.5
  30.0 8.7 %collective-permute-start.6 = (bf16[2048,128]{1,0:T(8,128)(2,1)S(1)}, bf16[2048,128]{1,0:T(8,128)(2,1)S(1)}, u32[]{:S(2)}, u32[]{:S(2)}) collective-permute-start(bf16[2048,128]{1,0:T(8,128)(2,1)S(1)} %get-tuple-element.50), channel_id=1, source_target_pairs={{4,3},{5,2},{6,1},{7,0},{8,7},{9,6},{10,5},{11,4},{12,11},{13,10},... | collective-permute-start | bytes 1572872 | tf_op jit(solution)/shard_map/ppermute | solution.py:25
  38.7 3.8 %up.1 = (s16[4,528,128]{2,1,0:T(8,128)(2,1)S(1)}, s16[4,528,128]{2,1,0:T(8,128)(2,1)S(1)}, s16[4,528,128]{2,1,0:T(8,128)(2,1)S(1)}, f32[16,512,128]{2,1,0:T(8,128)S(1)}) custom-call(s32[34]{0:T(128)S(1)} %pad_add_fusion.refs_0_.index, s32[34]{0:T(128)S(1)} %collective-permute-done.refs_1_, ...), custom_call_target="tpu_custom_call", output_to_operand_aliasing={{3}: (6, {})} | custom-call | flops 1000 | bytes 1000 | tf_op jit(solution)/shard_map/up/pallas_call | solution.py:290
  42.6 2.7 %collective-permute-start.12 = (s16[4,528,128]{2,1,0:T(8,128)(2,1)S(1)}, s16[4,528,128]{2,1,0:T(8,128)(2,1)S(1)}, u32[]{:S(2)}, u32[]{:S(2)}) collective-permute-start(s16[4,528,128]{2,1,0:T(8,128)(2,1)S(1)} %get-tuple-element.44), channel_id=1, source_target_pairs={{0,2},{1,3},{2,0},{3,1},{4,6},{5,7},{6,4},{7,5},{8,10},{9,11},{10,... | collective-permute-start | bytes 1622024 | tf_op jit(solution)/shard_map/ppermute | solution.py:25
  45.3 6.0 %group.1.refs_6_ = f32[16,512,128]{2,1,0:T(8,128)S(1)} custom-call(s32[34]{0:T(128)S(1)} %pad_add_fusion.refs_0_.index, s32[34]{0:T(128)S(1)} %collective-permute-done.refs_1_, bf16[16,512,512]{2,1,0:T(8,128)(2,1)} %refs_2_.9, bf16[16,512,512]{2,1,0:T(8,128)(2,1)} %collective-permute-done.1.refs_3_, ...), custom_call_target="tpu_custom_call", output_to_operand_aliasing={{}: (8, {})} | custom-call | flops 1000 | bytes 1000 | tf_op jit(solution)/shard_map/group/pallas_call | solution.py:290
  51.4 1.4 %far.1 = (s16[4,528,128]{2,1,0:T(8,128)(2,1)S(1)}, s16[4,528,128]{2,1,0:T(8,128)(2,1)S(1)}, f32[16,512,128]{2,1,0:T(8,128)S(1)}) custom-call(s32[34]{0:T(128)S(1)} %pad_add_fusion.refs_0_.index, s32[34]{0:T(128)S(1)} %collective-permute-done.refs_1_, bf16[16,512,512]{2,1,0:T(8,128)(2,1)} %refs_2_.9, ...), custom_call_target="tpu_custom_call", output_to_operand_aliasing={{2}: (6, {})} | custom-call | flops 1000 | bytes 1000 | tf_op jit(solution)/shard_map/far/pallas_call | solution.py:290
  52.9 0.5 collective-permute-start.9
  53.4 3.6 %collective-permute-start.10 = (s16[4,528,128]{2,1,0:T(8,128)(2,1)S(1)}, s16[4,528,128]{2,1,0:T(8,128)(2,1)S(1)}, u32[]{:S(2)}, u32[]{:S(2)}) collective-permute-start(s16[4,528,128]{2,1,0:T(8,128)(2,1)S(1)} %get-tuple-element.39), channel_id=1, source_target_pairs={{0,2},{1,3},{2,0},{3,1},{4,6},{5,7},{6,4},{7,5},{8,10},{9,11},{10,... | collective-permute-start | bytes 1622024 | tf_op jit(solution)/shard_map/ppermute | solution.py:25
  57.0 1.9 %collective-permute-start.11 = (s16[4,528,128]{2,1,0:T(8,128)(2,1)S(1)}, s16[4,528,128]{2,1,0:T(8,128)(2,1)S(1)}, u32[]{:S(2)}, u32[]{:S(2)}) collective-permute-start(s16[4,528,128]{2,1,0:T(8,128)(2,1)S(1)} %get-tuple-element.40), channel_id=1, source_target_pairs={{0,7},{1,6},{2,5},{3,4},{4,11},{5,10},{6,9},{7,8},{8,15},{9,14},{1... | collective-permute-start | bytes 1622024 | tf_op jit(solution)/shard_map/ppermute | solution.py:25
  58.9 0.4 add_up.1
  59.3 4.7 %collective-permute-start.13 = (s16[4,528,128]{2,1,0:T(8,128)(2,1)S(1)}, s16[4,528,128]{2,1,0:T(8,128)(2,1)S(1)}, u32[]{:S(2)}, u32[]{:S(2)}) collective-permute-start(s16[4,528,128]{2,1,0:T(8,128)(2,1)S(1)} %add_up.1), channel_id=1, source_target_pairs={{0,6},{1,7},{2,4},{3,5},{4,10},{5,11},{6,8},{7,9},{8,14},{9,15},{1... | collective-permute-start | bytes 1622024 | tf_op jit(solution)/shard_map/ppermute | solution.py:25
  64.0 7.9 %collective-permute-done.14.refs_1_ = s16[4,528,128]{2,1,0:T(8,128)(2,1)S(1)} collective-permute-done((s16[4,528,128]{2,1,0:T(8,128)(2,1)S(1)}, s16[4,528,128]{2,1,0:T(8,128)(2,1)S(1)}, u32[]{:S(2)}, u32[]{:S(2)}) %collective-permute-start.14) | collective-permute-done | bytes 540704 | tf_op jit(solution)/shard_map/ppermute | solution.py:25
  71.9 0.4 add_here.1
  72.3 0.1 collective-permute-start.15
  72.5 10.1 %collective-permute-done.11.below1 = s16[4,528,128]{2,1,0:T(8,128)(2,1)S(1)} collective-permute-done((s16[4,528,128]{2,1,0:T(8,128)(2,1)S(1)}, s16[4,528,128]{2,1,0:T(8,128)(2,1)S(1)}, u32[]{:S(2)}, u32[]{:S(2)}) %collective-permute-start.11) | collective-permute-done | bytes 540704 | tf_op jit(solution)/shard_map/ppermute | solution.py:25
  82.6 0.3 broadcast_in_dim.10.reflect
  82.9 1.3 %ready.1 = (f32[4,512,128]{2,1,0:T(8,128)S(1)}, f32[4,512,128]{2,1,0:T(8,128)S(1)}) custom-call(s32[34]{0:T(128)S(1)} %pad_add_fusion.refs_0_.index, f32[16,512,128]{2,1,0:T(8,128)S(1)} %get-tuple-element.37.sums.refs_0_, s16[4,528,128]{2,1,0:T(8,128)(2,1)S(1)} %collective-permute-done.9.sib, s16[4,528,128]{2,1,0:T(8,128)(2,1)S(1)} %collective-permute-done.10.here0, ...), custom_call_target="tpu_custom_call" | custom-call | flops 1000 | bytes 1000 | tf_op jit(solution)/shard_map/ready/pallas_call | solution.py:290
  84.3 10.4 %collective-permute-done.13.below0 = s16[4,528,128]{2,1,0:T(8,128)(2,1)S(1)} collective-permute-done((s16[4,528,128]{2,1,0:T(8,128)(2,1)S(1)}, s16[4,528,128]{2,1,0:T(8,128)(2,1)S(1)}, u32[]{:S(2)}, u32[]{:S(2)}) %collective-permute-start.13) | collective-permute-done | bytes 540704 | tf_op jit(solution)/shard_map/ppermute | solution.py:25
  94.6 2.5 %final.1 = f32[2048,256]{1,0:T(8,128)} custom-call(s32[34]{0:T(128)S(1)} %pad_add_fusion.refs_0_.index, f32[4,512,128]{2,1,0:T(8,128)S(1)} %get-tuple-element.41.mine, f32[4,512,128]{2,1,0:T(8,128)S(1)} %get-tuple-element.42.other, s16[4,528,128]{2,1,0:T(8,128)(2,1)S(1)} %collective-permute-done.13.below0, ...), custom_call_target="tpu_custom_call" | custom-call | tf_op jit(solution)/shard_map/final/pallas_call | solution.py:377
  (19 shorter events, 0.3 us)
Async XLA Ops:
  0.0 14.1 %collective-permute-start.1 = (bf16[16,512,512]{2,1,0:T(8,128)(2,1)}, bf16[16,512,512]{2,1,0:T(8,128)(2,1)}, u32[]{:S(2)}, u32[]{:S(2)}) collective-permute-start(bf16[16,512,512]{2,1,0:T(8,128)(2,1)} %refs_2_.9), channel_id=1, source_target_pairs={{0,1},{1,0},{2,3},{3,2},{4,5},{5,4},{6,7},{7,6},{8,9},{9,8},{10,11... | collective-permute-start | bytes 25165832 | tf_op jit(solution)/shard_map/ppermute | solution.py:25
  0.0 25.8 %collective-permute-start.3 = (bf16[2048,256]{1,0:T(8,128)(2,1)}, bf16[2048,256]{1,0:T(8,128)(2,1)S(1)}, u32[]{:S(2)}, u32[]{:S(2)}) collective-permute-start(bf16[2048,256]{1,0:T(8,128)(2,1)} %param.7), channel_id=1, source_target_pairs={{0,2},{1,3},{2,0},{3,1},{4,6},{5,7},{6,4},{7,5},{8,10},{9,11},{10,... | collective-permute-start | bytes 3145736 | tf_op jit(solution)/shard_map/ppermute | solution.py:25
  1.6 27.0 %collective-permute-start.2 = (bf16[2048,256]{1,0:T(8,128)(2,1)}, bf16[2048,256]{1,0:T(8,128)(2,1)S(1)}, u32[]{:S(2)}, u32[]{:S(2)}) collective-permute-start(bf16[2048,256]{1,0:T(8,128)(2,1)} %param.7), channel_id=1, source_target_pairs={{0,254},{1,255},{2,252},{3,253},{4,2},{5,3},{6,0},{7,1},{8,6},{9,7... | collective-permute-start | bytes 3145736 | tf_op jit(solution)/shard_map/ppermute | solution.py:25
  7.6 6.6 %collective-permute-start.4 = (bf16[2048,128]{1,0:T(8,128)(2,1)}, bf16[2048,128]{1,0:T(8,128)(2,1)S(1)}, u32[]{:S(2)}, u32[]{:S(2)}) collective-permute-start(bf16[2048,128]{1,0:T(8,128)(2,1)} %get-tuple-element.51), channel_id=1, source_target_pairs={{0,1},{1,0},{2,3},{3,2},{4,5},{5,4},{6,7},{7,6},{8,9},{9,8},{10,11... | collective-permute-start | bytes 1572872 | tf_op jit(solution)/shard_map/ppermute | solution.py:25
  9.0 4.1 %collective-permute-start = (s32[34]{0:T(128)S(1)}, s32[34]{0:T(128)S(1)}, u32[]{:S(2)}, u32[]{:S(2)}) collective-permute-start(s32[34]{0:T(128)S(1)} %pad_add_fusion.refs_0_.index), channel_id=1, source_target_pairs={{0,1},{1,0},{2,3},{3,2},{4,5},{5,4},{6,7},{7,6},{8,9},{9,8},{10,11... | collective-permute-start | bytes 416 | tf_op jit(solution)/shard_map/ppermute | solution.py:25
  28.7 10.0 %collective-permute-start.8 = (bf16[2048,128]{1,0:T(8,128)(2,1)S(1)}, bf16[2048,128]{1,0:T(8,128)(2,1)S(1)}, u32[]{:S(2)}, u32[]{:S(2)}) collective-permute-start(bf16[2048,128]{1,0:T(8,128)(2,1)S(1)} %get-tuple-element.47), channel_id=1, source_target_pairs={{0,1},{1,0},{2,3},{3,2},{4,5},{5,4},{6,7},{7,6},{8,9},{9,8},{10,11... | collective-permute-start | bytes 1572872 | tf_op jit(solution)/shard_map/ppermute | solution.py:25
  28.8 9.9 %collective-permute-start.7 = (bf16[2048,128]{1,0:T(8,128)(2,1)S(1)}, bf16[2048,128]{1,0:T(8,128)(2,1)S(1)}, u32[]{:S(2)}, u32[]{:S(2)}) collective-permute-start(bf16[2048,128]{1,0:T(8,128)(2,1)S(1)} %get-tuple-element.50), channel_id=1, source_target_pairs={{0,1},{1,0},{2,3},{3,2},{4,5},{5,4},{6,7},{7,6},{8,9},{9,8},{10,11... | collective-permute-start | bytes 1572872 | tf_op jit(solution)/shard_map/ppermute | solution.py:25
  29.3 22.0 %collective-permute-start.5 = (bf16[2048,128]{1,0:T(8,128)(2,1)S(1)}, bf16[2048,128]{1,0:T(8,128)(2,1)S(1)}, u32[]{:S(2)}, u32[]{:S(2)}) collective-permute-start(bf16[2048,128]{1,0:T(8,128)(2,1)S(1)} %get-tuple-element.48.refs_6_), channel_id=1, source_target_pairs={{0,2},{1,3},{2,0},{3,1},{4,6},{5,7},{6,4},{7,5},{8,10},{9,11},{10,... | collective-permute-start | bytes 1572872 | tf_op jit(solution)/shard_map/ppermute | solution.py:25
  30.0 21.4 %collective-permute-start.6 = (bf16[2048,128]{1,0:T(8,128)(2,1)S(1)}, bf16[2048,128]{1,0:T(8,128)(2,1)S(1)}, u32[]{:S(2)}, u32[]{:S(2)}) collective-permute-start(bf16[2048,128]{1,0:T(8,128)(2,1)S(1)} %get-tuple-element.50), channel_id=1, source_target_pairs={{4,3},{5,2},{6,1},{7,0},{8,7},{9,6},{10,5},{11,4},{12,11},{13,10},... | collective-permute-start | bytes 1572872 | tf_op jit(solution)/shard_map/ppermute | solution.py:25
  42.6 16.3 %collective-permute-start.12 = (s16[4,528,128]{2,1,0:T(8,128)(2,1)S(1)}, s16[4,528,128]{2,1,0:T(8,128)(2,1)S(1)}, u32[]{:S(2)}, u32[]{:S(2)}) collective-permute-start(s16[4,528,128]{2,1,0:T(8,128)(2,1)S(1)} %get-tuple-element.44), channel_id=1, source_target_pairs={{0,2},{1,3},{2,0},{3,1},{4,6},{5,7},{6,4},{7,5},{8,10},{9,11},{10,... | collective-permute-start | bytes 1622024 | tf_op jit(solution)/shard_map/ppermute | solution.py:25
  51.3 20.6 %collective-permute-start.14 = (s16[4,528,128]{2,1,0:T(8,128)(2,1)S(1)}, s16[4,528,128]{2,1,0:T(8,128)(2,1)S(1)}, u32[]{:S(2)}, u32[]{:S(2)}) collective-permute-start(s16[4,528,128]{2,1,0:T(8,128)(2,1)S(1)} %get-tuple-element.45), channel_id=1, source_target_pairs={{0,6},{1,7},{2,4},{3,5},{4,10},{5,11},{6,8},{7,9},{8,14},{9,15},{1... | collective-permute-start | bytes 1622024 | tf_op jit(solution)/shard_map/ppermute | solution.py:25
  52.9 19.6 %collective-permute-start.9 = (s16[4,528,128]{2,1,0:T(8,128)(2,1)S(1)}, s16[4,528,128]{2,1,0:T(8,128)(2,1)S(1)}, u32[]{:S(2)}, u32[]{:S(2)}) collective-permute-start(s16[4,528,128]{2,1,0:T(8,128)(2,1)S(1)} %get-tuple-element.38), channel_id=1, source_target_pairs={{0,1},{1,0},{2,3},{3,2},{4,5},{5,4},{6,7},{7,6},{8,9},{9,8},{10,11... | collective-permute-start | bytes 1622024 | tf_op jit(solution)/shard_map/ppermute | solution.py:25
  53.4 19.1 %collective-permute-start.10 = (s16[4,528,128]{2,1,0:T(8,128)(2,1)S(1)}, s16[4,528,128]{2,1,0:T(8,128)(2,1)S(1)}, u32[]{:S(2)}, u32[]{:S(2)}) collective-permute-start(s16[4,528,128]{2,1,0:T(8,128)(2,1)S(1)} %get-tuple-element.39), channel_id=1, source_target_pairs={{0,2},{1,3},{2,0},{3,1},{4,6},{5,7},{6,4},{7,5},{8,10},{9,11},{10,... | collective-permute-start | bytes 1622024 | tf_op jit(solution)/shard_map/ppermute | solution.py:25
  57.0 25.6 %collective-permute-start.11 = (s16[4,528,128]{2,1,0:T(8,128)(2,1)S(1)}, s16[4,528,128]{2,1,0:T(8,128)(2,1)S(1)}, u32[]{:S(2)}, u32[]{:S(2)}) collective-permute-start(s16[4,528,128]{2,1,0:T(8,128)(2,1)S(1)} %get-tuple-element.40), channel_id=1, source_target_pairs={{0,7},{1,6},{2,5},{3,4},{4,11},{5,10},{6,9},{7,8},{8,15},{9,14},{1... | collective-permute-start | bytes 1622024 | tf_op jit(solution)/shard_map/ppermute | solution.py:25
  58.9 23.7 %copy-start.1 = (f32[2048]{0:T(1024)S(1)}, f32[2048]{0:T(1024)}, u32[]{:S(2)}) copy-start(f32[2048]{0:T(1024)} %param.9) | copy-start | bytes 24580
  59.3 23.6 %copy-start = (bf16[2048,256]{1,0:T(8,128)(2,1)S(1)}, bf16[2048,256]{1,0:T(8,128)(2,1)}, u32[]{:S(2)}) copy-start(bf16[2048,256]{1,0:T(8,128)(2,1)} %source.1) | copy-start | bytes 3145732
  59.3 35.3 %collective-permute-start.13 = (s16[4,528,128]{2,1,0:T(8,128)(2,1)S(1)}, s16[4,528,128]{2,1,0:T(8,128)(2,1)S(1)}, u32[]{:S(2)}, u32[]{:S(2)}) collective-permute-start(s16[4,528,128]{2,1,0:T(8,128)(2,1)S(1)} %add_up.1), channel_id=1, source_target_pairs={{0,6},{1,7},{2,4},{3,5},{4,10},{5,11},{6,8},{7,9},{8,14},{9,15},{1... | collective-permute-start | bytes 1622024 | tf_op jit(solution)/shard_map/ppermute | solution.py:25
  72.3 22.3 %collective-permute-start.15 = (s16[4,528,128]{2,1,0:T(8,128)(2,1)S(1)}, s16[4,528,128]{2,1,0:T(8,128)(2,1)S(1)}, u32[]{:S(2)}, u32[]{:S(2)}) collective-permute-start(s16[4,528,128]{2,1,0:T(8,128)(2,1)S(1)} %add_here.1), channel_id=1, source_target_pairs={{0,3},{1,2},{2,1},{3,0},{4,7},{5,6},{6,5},{7,4},{8,11},{9,10},{10,... | collective-permute-start | bytes 1622024 | tf_op jit(solution)/shard_map/ppermute | solution.py:25
